TPU v7x, 256 devices: a whole 4x4x8 slice. The times are simulated.
256 devices in a mesh: dp: 16 (over z, core), head: 16 (over x, y).
Axes of the slice: x: 4, y: 4, z: 8, core: 2. Of those that a mesh axis runs over, the one named last changes fastest.
Arguments:
- layer_input: bfloat16 [32768, 8192], P(('dp', 'head')), may hold values from -6 to 6
- queries: bfloat16 [32768, 4096], P(('dp', 'head')), may hold values from -8 to 8
- key_rows: bfloat16 [32768, 512], P(('dp', 'head')), may hold values from -8 to 8
- value_rows: bfloat16 [32768, 512], P(('dp', 'head')), may hold values from -6 to 6
- d_out: bfloat16 [32768, 4096], P(('dp', 'head')), may hold values from -6 to 6
- doc_lengths: int32 [16, 8], P('dp'), may hold values from 1 to 1024, 2048 in all within a row
Outputs:
- grad_q: bfloat16 [32768, 4096], P(('dp', 'head'))
- grad_wk: float32 [8192, 512], P(('dp', 'head'))
- grad_wv: float32 [8192, 512], P(('dp', 'head'))
Inputs may be any that keep to these rules, and one draw needn't show every extreme that they name: `doc_lengths`: each row sums to 2048; its longest document has exactly 1024 positions.
All inputs are finite; a program needn't handle non-finite values.
Results may differ from a plain program's by a relative error of at most 0.025.
Values may be sent and summed in bfloat16 or wider, within the bound.
No kernel may reach another device: no remote copies, remote signals or barrier semaphores. Data moves between devices by JAX's collectives and lax.ppermute only.
A program may use at most 128 MiB of HBM per device.

v0:
```python
import jax
import jax.numpy as jnp
from jax import lax
from jax.sharding import PartitionSpec as P

HQ = 32
HK = 4
HD = 128


def on_device(layer_input, queries, key_rows, value_rows, d_out, doc_lengths):
    tok_dev = layer_input.shape[0]
    width_in = layer_input.shape[1]
    heads_n = lax.axis_size("head")
    windows_n = lax.axis_size("dp")
    window_len = tok_dev * heads_n
    group_q = HQ // heads_n
    repeat = heads_n // HK
    scale = HD ** (-0.5)
    q_win, do_win = (
        lax.all_to_all(queries, "head", split_axis=1, concat_axis=0, tiled=True),
        lax.all_to_all(d_out, "head", split_axis=1, concat_axis=0, tiled=True),
    )
    k_all, v_all = (
        lax.all_gather(key_rows, "head", axis=0, tiled=True),
        lax.all_gather(value_rows, "head", axis=0, tiled=True),
    )
    first_col = lax.axis_index("head") // repeat * HD
    k_win = lax.dynamic_slice_in_dim(k_all, first_col, HD, 1)
    v_win = lax.dynamic_slice_in_dim(v_all, first_col, HD, 1)
    positions = jnp.arange(window_len, dtype=jnp.int32)
    doc_ends = jnp.cumsum(doc_lengths[0])
    doc_id = jnp.sum((positions[:, None] >= doc_ends[None, :]).astype(jnp.int32), axis=1)
    q_heads = q_win.reshape(window_len, group_q, HD)
    do_heads = do_win.reshape(window_len, group_q, HD)
    block_rows = max(min(512, window_len), window_len // 8)
    grad_k = jnp.zeros((window_len, HD), jnp.float32)
    grad_v = jnp.zeros((window_len, HD), jnp.float32)
    dq_blocks = []
    for block_idx in range(window_len // block_rows):
        row_lo = block_idx * block_rows
        row_hi = row_lo + block_rows
        q_block = q_heads[row_lo:row_hi]
        do_block = do_heads[row_lo:row_hi]
        k_keys = k_win[:row_hi]
        v_keys = v_win[:row_hi]
        allowed = (doc_id[row_lo:row_hi, None] == doc_id[None, :row_hi]) & (
            positions[row_lo:row_hi, None] >= positions[None, :row_hi]
        )
        scores = (
            jnp.einsum("qgd,kd->gqk", q_block, k_keys, preferred_element_type=jnp.float32) * scale
        )
        scores = jnp.where(allowed[None], scores, -jnp.inf)
        row_max = jnp.max(scores, axis=-1, keepdims=True)
        shifted = jnp.exp(scores - row_max)
        probs = shifted / jnp.sum(shifted, axis=-1, keepdims=True)
        probs_b = probs.astype(jnp.bfloat16)
        dprob = jnp.einsum("qgd,kd->gqk", do_block, v_keys, preferred_element_type=jnp.float32)
        row_dot = jnp.sum(probs * dprob, axis=-1, keepdims=True)
        dscore = (probs * (dprob - row_dot)).astype(jnp.bfloat16)
        dq_part = (
            jnp.einsum("gqk,kd->qgd", dscore, k_keys, preferred_element_type=jnp.float32) * scale
        )
        dq_blocks.append(dq_part.astype(jnp.bfloat16))
        grad_k = grad_k.at[:row_hi].add(
            jnp.einsum("gqk,qgd->kd", dscore, q_block, preferred_element_type=jnp.float32) * scale
        )
        grad_v = grad_v.at[:row_hi].add(
            jnp.einsum("gqk,qgd->kd", probs_b, do_block, preferred_element_type=jnp.float32)
        )
    dq_window = jnp.concatenate(dq_blocks, axis=0).reshape(window_len, group_q * HD)
    grad_q = lax.all_to_all(dq_window, "head", split_axis=0, concat_axis=1, tiled=True)
    k_terms, v_terms = (
        lax.all_to_all(
            grad_k.astype(jnp.bfloat16), "head", split_axis=0, concat_axis=1, tiled=True
        ).astype(grad_k.dtype),
        lax.all_to_all(
            grad_v.astype(jnp.bfloat16), "head", split_axis=0, concat_axis=1, tiled=True
        ).astype(grad_v.dtype),
    )
    dk_tok = (
        jnp.sum(k_terms.reshape(tok_dev, HK, repeat, HD), axis=2)
        .reshape(tok_dev, HK * HD)
        .astype(jnp.bfloat16)
    )
    dv_tok = (
        jnp.sum(v_terms.reshape(tok_dev, HK, repeat, HD), axis=2)
        .reshape(tok_dev, HK * HD)
        .astype(jnp.bfloat16)
    )
    width_kv = HK * HD
    rows_out = width_in // (windows_n * heads_n)
    contract = (((0,), (0,)), ((), ()))
    arranged = (
        layer_input.reshape(tok_dev, windows_n, heads_n, rows_out)
        .transpose(0, 2, 1, 3)
        .reshape(tok_dev, width_in)
    )
    x_cols = lax.all_to_all(arranged, "head", split_axis=1, concat_axis=0, tiled=True)
    dk_all, dv_all = (
        lax.all_gather(dk_tok, "head", axis=0, tiled=True),
        lax.all_gather(dv_tok, "head", axis=0, tiled=True),
    )
    cols_n = width_in // heads_n

    def add_block(totals, pieces):
        x_part, k_part, v_part = pieces
        term_k = lax.dot_general(x_part, k_part, contract, preferred_element_type=jnp.float32)
        term_v = lax.dot_general(x_part, v_part, contract, preferred_element_type=jnp.float32)
        term_k = lax.optimization_barrier(term_k.astype(jnp.bfloat16)).astype(jnp.float32)
        term_v = lax.optimization_barrier(term_v.astype(jnp.bfloat16)).astype(jnp.float32)
        return ((totals[0] + term_k, totals[1] + term_v), None)

    empty = jnp.zeros((cols_n, width_kv), jnp.float32)
    (window_k, window_v), unused = lax.scan(
        add_block,
        (empty, empty),
        (
            x_cols.reshape(heads_n, tok_dev, cols_n),
            dk_all.reshape(heads_n, tok_dev, width_kv),
            dv_all.reshape(heads_n, tok_dev, width_kv),
        ),
    )
    final_k, final_v = (
        lax.psum_scatter(
            window_k.reshape(windows_n, rows_out, width_kv).astype(jnp.bfloat16),
            "dp",
            scatter_dimension=0,
            tiled=True,
        ).astype(jnp.float32),
        lax.psum_scatter(
            window_v.reshape(windows_n, rows_out, width_kv).astype(jnp.bfloat16),
            "dp",
            scatter_dimension=0,
            tiled=True,
        ).astype(jnp.float32),
    )
    return (grad_q, final_k.reshape(rows_out, width_kv), final_v.reshape(rows_out, width_kv))


def solution(mesh):
    return jax.shard_map(
        on_device,
        mesh=mesh,
        in_specs=(
            P(("dp", "head"), None),
            P(("dp", "head"), None),
            P(("dp", "head"), None),
            P(("dp", "head"), None),
            P(("dp", "head"), None),
            P("dp", None),
        ),
        out_specs=(P(("dp", "head"), None), P(("dp", "head"), None), P(("dp", "head"), None)),
        check_vma=False,
    )
```

profile of v0, /device:TPU:1, one launch (start us, length us, event | category | flops | bytes accessed | tf_op | source)
XLA Modules:
  0.0 525.6 jit_solution(312996556513863017)
XLA Ops:
  11.0 7.6 %all-to-all-start = ((bf16[128,16,256]{2,0,1:T(8,128)(2,1)}), bf16[128,16,256]{2,0,1:T(8,128)(2,1)S(1)}, u32[]{:S(2)}, u32[]{:S(2)}) async-start(bf16[128,16,256]{2,0,1:T(8,128)(2,1)} %bitcast.281), calls=%async_computation | async-start | bytes 2097152 | tf_op jit(solution)/shard_map/all_to_all | solution.py:21
  22.7 11.1 %all-to-all-done = bf16[128,16,256]{2,0,1:T(8,128)(2,1)S(1)} async-done(((bf16[128,16,256]{2,0,1:T(8,128)(2,1)}), bf16[128,16,256]{2,0,1:T(8,128)(2,1)S(1)}, u32[]{:S(2)}, u32[]{:S(2)}) %all-to-all-start) | async-done | bytes 1048608 | tf_op jit(solution)/shard_map/all_to_all | solution.py:21
  33.8 5.0 all-to-all-start.1
  42.6 10.5 %all-to-all-done.1 = bf16[128,16,256]{2,0,1:T(8,128)(2,1)S(1)} async-done(((bf16[128,16,256]{2,0,1:T(8,128)(2,1)}), bf16[128,16,256]{2,0,1:T(8,128)(2,1)S(1)}, u32[]{:S(2)}, u32[]{:S(2)}) %all-to-all-start.1) | async-done | bytes 1048608 | tf_op jit(solution)/shard_map/all_to_all | solution.py:22
  56.3 11.5 %all-gather.5.cloned.1.call-done = bf16[2048,512]{1,0:T(8,128)(2,1)} async-done(((bf16[128,512]{1,0:T(8,128)(2,1)}), bf16[2048,512]{1,0:T(8,128)(2,1)}) %all-gather.5.cloned.1.call-update) | async-done | bytes 2097168 | tf_op jit(solution)/shard_map/all_gather | solution.py:25
  69.8 49.9 %all-gather.7.cloned.1.call-done = bf16[2048,512]{1,0:T(8,128)(2,1)} async-done(((bf16[128,512]{1,0:T(8,128)(2,1)}), bf16[2048,512]{1,0:T(8,128)(2,1)}) %all-gather.7.cloned.1.call-update) | async-done | bytes 2097168 | tf_op jit(solution)/shard_map/all_gather | solution.py:26
  126.5 4.6 fusion.208
  131.1 3.0 fusion.79
  134.1 6.2 %fusion.205 = (f32[2,512]{1,0:T(2,128)S(1)}, f32[2,512,1536]{1,2,0:T(8,128)}) fusion(pred[512,1536]{0,1:T(8,128)(4,1)S(1)} %copy-done.11, bf16[2048,512]{1,0:T(8,128)(2,1)} %all-gather.5.cloned.1.call-done, s32[]{:T(128)S(6)} %select_n.26, bf16[512,2,128]{2,1,0:T(2,128)(2,1)S(1)} %slice.264), kind=kOutput, calls=%fused_computation.201 | convolution fusion | flops 408946176 | bytes 7737348 | tf_op jit(solution)/shard_map/sub | solution.py:55
  140.3 7.4 %fusion.196 = (f32[2,512]{1,0:T(2,128)S(1)}, f32[2,512,2048]{1,2,0:T(8,128)}) fusion(pred[512,2048]{0,1:T(8,128)(4,1)S(1)} %copy-done.8, bf16[2048,512]{1,0:T(8,128)(2,1)} %all-gather.5.cloned.1.call-done, s32[]{:T(128)S(6)} %select_n.26, bf16[512,2,128]{2,1,0:T(2,128)(2,1)S(1)} %slice.271), kind=kOutput, calls=%fused_computation.200 | convolution fusion | flops 545261568 | bytes 10227716 | tf_op jit(solution)/shard_map/sub | solution.py:55
  147.7 4.6 fusion.51
  152.4 5.5 %fusion.58 = bf16[2048,128]{1,0:T(8,128)(2,1)} fusion(f32[2048,128]{1,0:T(8,128)S(1)} %fusion.51, bf16[512,2,128]{2,1,0:T(2,128)(2,1)S(1)} %copy-done.13, f32[2,512,2048]{1,2,0:T(8,128)} %get-tuple-element.231, f32[2,512]{1,0:T(2,128)S(1)} %get-tuple-element.230), kind=kOutput, calls=%fused_computation.70 | convolution fusion | flops 541589504 | bytes 10227712 | tf_op jit(solution)/shard_map/gqk,qgd->kd/dot_general | solution.py:69
  157.9 4.7 all-to-all-start.5
  162.7 4.1 fusion.18
  169.3 3.2 fusion.22
  177.5 3.3 fusion.75
  180.8 3.1 fusion.44
  184.0 5.0 fusion.14
  193.4 15.6 %all_to_all.93 = bf16[16,128,128]{2,1,0:T(8,128)(2,1)S(1)} all-to-all(bf16[16,128,128]{2,1,0:T(8,128)(2,1)S(1)} %bitcast.304), channel_id=1, replica_groups=mesh['dp'=16,'head'=16] {'head'}, dimensions={0} | all-to-all | bytes 1048576 | tf_op jit(solution)/shard_map/all_to_all | solution.py:74
  209.8 4.1 copy.134
  213.9 3.5 copy.135
  217.3 4.4 all-to-all-start.3
  223.5 2.9 fusion.87
  226.4 28.3 %all-gather.11.cloned.1.call-done = bf16[2048,512]{0,1:T(8,128)(2,1)} async-done(((bf16[128,512]{0,1:T(8,128)(2,1)}), bf16[2048,512]{0,1:T(8,128)(2,1)}) %all-gather.11.cloned.1.call-update) | async-done | bytes 2097168 | tf_op jit(solution)/shard_map/all_gather | solution.py:102
  254.6 3.9 copy.163
  258.6 51.1 %all-gather.9.cloned.1.call-done = bf16[2048,512]{0,1:T(8,128)(2,1)} async-done(((bf16[128,512]{0,1:T(8,128)(2,1)}), bf16[2048,512]{0,1:T(8,128)(2,1)}) %all-gather.9.cloned.1.call-update) | async-done | bytes 2097168 | tf_op jit(solution)/shard_map/all_gather | solution.py:101
  309.7 3.9 copy.162
  313.6 89.7 %while.23 = (s32[]{:T(128)}, f32[512,512]{1,0:T(8,128)}, f32[512,512]{1,0:T(8,128)}, bf16[16,128,512]{1,2,0:T(8,128)(2,1)}, bf16[16,128,512]{2,1,0:T(8,128)(2,1)...) while((s32[]{:T(128)}, f32[512,512]{1,0:T(8,128)}, f32[512,512]{1,0:T(8,128)}, ...), condition=%wide.region_17.18_spmd.clone, body=%wide.region_16.17_spmd.clone.sunk | while | flops 136314880 | bytes 6817895 | solution.py:115
  320.2 3.2 select_add_fusion.3
  325.9 3.2 select_add_fusion.3
  331.6 3.2 select_add_fusion.3
  337.3 3.2 select_add_fusion.3
  343.0 3.2 select_add_fusion.3
  348.7 3.2 select_add_fusion.3
  354.4 3.2 select_add_fusion.3
  360.1 3.2 select_add_fusion.3
  365.8 3.2 select_add_fusion.3
  371.5 3.2 select_add_fusion.3
  377.2 3.2 select_add_fusion.3
  382.9 3.2 select_add_fusion.3
  388.6 3.2 select_add_fusion.3
  394.3 3.2 select_add_fusion.3
  400.0 3.2 select_add_fusion.3
  407.0 3.2 fusion.86
  411.8 4.7 all-to-all-start.2
  417.4 14.1 %all-to-all-done.2 = bf16[16,128,256]{1,2,0:T(8,128)(2,1)S(1)} async-done(((bf16[16,128,256]{1,2,0:T(8,128)(2,1)}), bf16[16,128,256]{1,2,0:T(8,128)(2,1)S(1)}, u32[]{:S(2)}, u32[]{:S(2)}) %all-to-all-start.2) | async-done | bytes 1048608 | tf_op jit(solution)/shard_map/all_to_all | solution.py:72
  432.8 27.1 %reduce-scatter.5.cloned.1.call-done = bf16[1,32,512]{2,1,0:T(8,128)(2,1)} async-done(((bf16[16,32,512]{2,1,0:T(8,128)(2,1)}), bf16[1,32,512]{2,1,0:T(8,128)(2,1)}) %reduce-scatter.5.cloned.1.call-update) | async-done | bytes 32784 | tf_op jit(solution)/shard_map/reduce_scatter | solution.py:131
  461.3 56.1 %reduce-scatter.3.cloned.1.call-done = bf16[1,32,512]{2,1,0:T(8,128)(2,1)} async-done(((bf16[16,32,512]{2,1,0:T(8,128)(2,1)}), bf16[1,32,512]{2,1,0:T(8,128)(2,1)}) %reduce-scatter.3.cloned.1.call-update) | async-done | bytes 32784 | tf_op jit(solution)/shard_map/reduce_scatter | solution.py:125
  (150 shorter events, 89.9 us)
Async XLA Ops:
  7.2 11.5 %copy-start.19 = (s32[1,8]{1,0:T(1,128)S(1)}, s32[1,8]{1,0:T(1,128)}, u32[]{:S(2)}) copy-start(s32[1,8]{1,0:T(1,128)} %param.33) | copy-start | bytes 100
  7.2 11.8 %copy-start.7 = (bf16[128,4096]{1,0:T(8,128)(2,1)S(1)}, bf16[128,4096]{1,0:T(8,128)(2,1)}, u32[]{:S(2)}) copy-start(bf16[128,4096]{1,0:T(8,128)(2,1)} %param.32) | copy-start | bytes 3145732
  7.2 60.6 %all-gather.5.cloned.1.call-start = ((), (), s32[]{:S(2)}) async-start(), calls=%async_computation.8 | async-start | bytes 2228224 | tf_op jit(solution)/shard_map/all_gather | solution.py:25
  7.9 111.7 %all-gather.7.cloned.1.call-start = ((), (), s32[]{:S(2)}) async-start(), calls=%async_computation.9 | async-start | bytes 2228224 | tf_op jit(solution)/shard_map/all_gather | solution.py:26
  11.0 22.8 %all-to-all-start = ((bf16[128,16,256]{2,0,1:T(8,128)(2,1)}), bf16[128,16,256]{2,0,1:T(8,128)(2,1)S(1)}, u32[]{:S(2)}, u32[]{:S(2)}) async-start(bf16[128,16,256]{2,0,1:T(8,128)(2,1)} %bitcast.281), calls=%async_computation | async-start | bytes 2097152 | tf_op jit(solution)/shard_map/all_to_all | solution.py:21
  33.8 19.3 %all-to-all-start.1 = ((bf16[128,16,256]{2,0,1:T(8,128)(2,1)}), bf16[128,16,256]{2,0,1:T(8,128)(2,1)S(1)}, u32[]{:S(2)}, u32[]{:S(2)}) async-start(bf16[128,16,256]{2,0,1:T(8,128)(2,1)} %bitcast.280), calls=%async_computation.1 | async-start | bytes 2097152 | tf_op jit(solution)/shard_map/all_to_all | solution.py:22
  42.5 105.3 %copy-start.5 = (bf16[512,2,128]{2,1,0:T(2,128)(2,1)}, bf16[512,2,128]{2,1,0:T(2,128)(2,1)S(1)}, u32[]{:S(2)}) copy-start(bf16[512,2,128]{2,1,0:T(2,128)(2,1)S(1)} %slice.264) | copy-start | bytes 786436
  42.6 83.8 %copy-start.9 = (bf16[512,2,128]{2,1,0:T(2,128)(2,1)}, bf16[512,2,128]{2,1,0:T(2,128)(2,1)S(1)}, u32[]{:S(2)}) copy-start(bf16[512,2,128]{2,1,0:T(2,128)(2,1)S(1)} %slice.254) | copy-start | bytes 786436
  56.3 63.3 %copy-start.18 = (bf16[512,2,128]{2,1,0:T(2,128)(2,1)S(1)}, bf16[512,2,128]{2,1,0:T(2,128)(2,1)}, u32[]{:S(2)}) copy-start(bf16[512,2,128]{2,1,0:T(2,128)(2,1)} %slice.247) | copy-start | bytes 786436
  121.5 1.0 copy-start.3
  123.0 3.5 copy-start.12
  126.5 4.6 copy-start.15
  131.0 3.0 copy-start.11
  134.1 6.2 %copy-start.8 = (pred[512,2048]{0,1:T(8,128)(4,1)S(1)}, pred[512,2048]{0,1:T(8,128)(4,1)}, u32[]{:S(2)}) copy-start(pred[512,2048]{0,1:T(8,128)(4,1)} %fusion.29) | copy-start | bytes 3145732
  147.7 4.7 copy-start.13
  152.4 10.3 %copy-start.17 = (bf16[512,2,128]{2,1,0:T(2,128)(2,1)S(1)}, bf16[512,2,128]{2,1,0:T(2,128)(2,1)}, u32[]{:S(2)}) copy-start(bf16[512,2,128]{2,1,0:T(2,128)(2,1)} %slice.267) | copy-start | bytes 786436
  157.9 17.4 %all-to-all-start.5 = ((bf16[16,128,128]{2,1,0:T(8,128)(2,1)}), bf16[16,128,128]{2,1,0:T(8,128)(2,1)}, u32[]{:S(2)}, u32[]{:S(2)}) async-start(bf16[16,128,128]{2,1,0:T(8,128)(2,1)} %bitcast.47), calls=%async_computation.5 | async-start | bytes 1048576 | tf_op jit(solution)/shard_map/all_to_all | solution.py:77
  162.6 92.0 %all-gather.11.cloned.1.call-start = ((), (), s32[]{:S(2)}) async-start(), calls=%async_computation.11 | async-start | bytes 2228224 | tf_op jit(solution)/shard_map/all_gather | solution.py:102
  162.7 4.1 slice-start.2
  162.7 4.8 slice-start.3
  167.5 1.8 copy-start.16
  169.3 3.5 copy-start.4
  177.2 132.4 %all-gather.9.cloned.1.call-start = ((), (), s32[]{:S(2)}) async-start(), calls=%async_computation.10 | async-start | bytes 2228224 | tf_op jit(solution)/shard_map/all_gather | solution.py:101
  177.5 3.3 copy-start.6
  180.8 3.1 copy-start.14
  180.8 8.1 %slice-start = ((s8[8388608]{0:T(1024)(128)(4,1)}), s8[4194304]{0:T(1024)(128)(4,1)S(1)}, s32[]{:S(2)}) async-start(s8[8388608]{0:T(1024)(128)(4,1)} %bitcast.291), calls=%async_computation.14 | async-start | bytes 8388608
  184.0 5.0 slice-start.1
  189.0 2.4 copy-start.2
  191.4 1.9 copy-start
  217.3 96.2 %all-to-all-start.3 = ((bf16[128,16,512]{0,2,1:T(8,128)(2,1)}), bf16[128,16,512]{0,2,1:T(8,128)(2,1)}, u32[]{:S(2)}, u32[]{:S(2)}) async-start(bf16[128,16,512]{0,2,1:T(8,128)(2,1)} %bitcast.293), calls=%async_computation.3 | async-start | bytes 4194304 | tf_op jit(solution)/shard_map/all_to_all | solution.py:99
  221.8 238.1 %reduce-scatter.5.cloned.1.call-start = ((), (), s32[]{:S(2)}) async-start(), calls=%async_computation.13 | async-start | bytes 557056 | tf_op jit(solution)/shard_map/reduce_scatter | solution.py:131
  407.0 3.2 copy-start.10
  410.3 6.2 %copy-start.1 = (f32[512,512]{1,0:T(8,128)S(1)}, f32[512,512]{1,0:T(8,128)}, u32[]{:S(2)}) copy-start(f32[512,512]{1,0:T(8,128)} %get-tuple-element.148) | copy-start | bytes 3145732
  411.8 19.7 %all-to-all-start.2 = ((bf16[16,128,256]{1,2,0:T(8,128)(2,1)}), bf16[16,128,256]{1,2,0:T(8,128)(2,1)S(1)}, u32[]{:S(2)}, u32[]{:S(2)}) async-start(bf16[16,128,256]{1,2,0:T(8,128)(2,1)} %copy.133), calls=%async_computation.2 | async-start | bytes 2097152 | tf_op jit(solution)/shard_map/all_to_all | solution.py:72
  416.5 100.9 %reduce-scatter.3.cloned.1.call-start = ((), (), s32[]{:S(2)}) async-start(), calls=%async_computation.12 | async-start | bytes 557056 | tf_op jit(solution)/shard_map/reduce_scatter | solution.py:125
Sparse Core Ops, SparseCore 0:
  10.5 57.2 all-gather.4
  70.2 49.3 all-gather.6
  177.3 77.2 all-gather.10
  256.9 52.7 all-gather.8
  405.5 54.3 reduce-scatter.4
  462.4 54.9 reduce-scatter.2
where the time goes:
time: 530 us; the launch traced here: 526 us
  waiting for transfers between devices  261 us (49%)
  matrix products  106 us (20%)
  other arithmetic  70.2 us (13%)
  local copies, waits for them, and re-layouts  30.5 us (6%)
  starting transfers between devices  26.9 us (5%)
  blocking collectives  15.6 us (3%)
  between operations  14.6 us (3%)
    reduce_scatter x1, waiting for transfers between devices, on_device(): lax.psum_scatter(window_k.reshape(windows_n, rows_out, width_kv).astype(j...  56.1 us
    all_gather x1, waiting for transfers between devices, on_device(): lax.all_gather(dk_tok, 'head', axis=0, tiled=True)  51.1 us
    all_gather x1, waiting for transfers between devices, on_device(): lax.all_gather(value_rows, 'head', axis=0, tiled=True)  49.9 us
    add x16, other arithmetic, add_block(): return ((totals[0] + term_k, totals[1] + term_v), None)  49.6 us
    all_gather x1, waiting for transfers between devices, on_device(): lax.all_gather(dv_tok, 'head', axis=0, tiled=True)  28.3 us
    reduce_scatter x1, waiting for transfers between devices, on_device(): lax.psum_scatter(window_v.reshape(windows_n, rows_out, width_kv).astype(j...  27.1 us
    sub x4, matrix products, on_device(): shifted = jnp.exp(scores - row_max)  20.2 us
    dot_general x16, matrix products, add_block(): lax.dot_general(x_part, k_part, contract, preferred_element_type=jnp.floa...  19.9 us
  transfers between devices with their start and end apart: 11, of which 9 were waited for; matrix products, arithmetic and copies ran while one was open for 14% of the time, Pallas kernels for 0%

commit v1 on v0

v1 whole, which is shorter than its diff:
```python
import functools
import math

import jax
import jax.numpy as jnp
from jax import lax
from jax.experimental import pallas as pl
from jax.experimental.pallas import tpu as pltpu
from jax.sharding import PartitionSpec as P

HQ = 32
HK = 4
HD = 128
BLK = 128
KB = 256
NX = 4
NY = 4
NZ = 8
NC = 2
MAX_KB = 5
SCALE = HD ** (-0.5)
LOG2E = math.log2(math.e)
BF = jnp.bfloat16
F32 = jnp.float32
AXES = ("dp", "head")
VM = pl.BlockSpec(memory_space=pltpu.VMEM)
SM = pl.BlockSpec(memory_space=pltpu.SMEM)


def send(value, dx=0, dy=0, dc=0):
    pairs = []
    for z in range(NZ):
        for c in range(NC):
            for x in range(NX):
                for y in range(NY):
                    src = ((z * NC + c) * NX + x) * NY + y
                    dst = ((z * NC + (c + dc) % NC) * NX + (x + dx) % NX) * NY + (y + dy) % NY
                    pairs.append((src, dst))
    return lax.ppermute(value, AXES, pairs)


def call(kernel, outs, ins, scratch=(), flops=0, moved=0, limit=56, smem=1):
    return pl.pallas_call(
        kernel,
        out_shape=outs,
        in_specs=[SM] * smem + [VM] * (len(ins) - smem),
        out_specs=[VM] * len(outs),
        scratch_shapes=list(scratch),
        compiler_params=pltpu.CompilerParams(vmem_limit_bytes=limit * 1024 * 1024),
        cost_estimate=pl.CostEstimate(flops=flops, bytes_accessed=moved, transcendentals=0),
    )(*ins)


def sds(shape, dtype=BF):
    return jax.ShapeDtypeStruct(shape, dtype)


def pack_kv_kernel(at, k, v, *outs):
    for s in range(NX):
        first = pl.multiple_of(lax.rem(at[0] + s, NX) * HD, HD)
        outs[s][:, 0:HD] = k[:, pl.ds(first, HD)]
        outs[s][:, HD : 2 * HD] = v[:, pl.ds(first, HD)]


def pack_heads_kernel(at, q, do, *outs):
    group = HQ // HK
    for s in range(NX):
        first = lax.rem(at[0] + s, NX) * (group * HD)
        for h in range(group):
            col = pl.multiple_of(first + h * HD, HD)
            outs[s][0, h * BLK : (h + 1) * BLK, :] = q[:, pl.ds(col, HD)]
            outs[s][1, h * BLK : (h + 1) * BLK, :] = do[:, pl.ds(col, HD)]


def pack_x_kernel(at, li, *outs):
    for s in range(NX):
        for d in range(NC):
            core = lax.rem(at[2] + d, NC)
            for z in range(NZ):
                col = z * (NC * 512) + core * 512 + lax.rem(at[0] + s, NX) * BLK
                outs[2 * s + d][:, z * BLK : (z + 1) * BLK] = li[:, pl.ds(pl.multiple_of(col, BLK), BLK)]


def turn_x_kernel(at, *refs):
    out = refs[-1]
    for d in range(NC):
        for s in range(NX):
            spot = pl.multiple_of(d * 512 + lax.rem(at[0] - s + NX, NX) * BLK, BLK)
            for z in range(NZ):
                rows = pl.ds(z * BLK, BLK)
                out[rows, pl.ds(spot, BLK)] = refs[2 * s + d][:, z * BLK : (z + 1) * BLK].T


def attention_kernel(at, lens, *refs):
    qd_in, kv_in = refs[0:4], refs[4:8]
    dq_out, r_out = refs[8:12], refs[12:16]
    qd, k_all, v_all, kt_all, s_all, dp_all, pb, dsb, dqt, dk, dv, dq_all = refs[16:]
    x, y = at[0], at[1]
    group = HQ // HK
    rows_n = group * BLK
    chunks = [slice(i * KB, (i + 1) * KB) for i in range(rows_n // KB)]
    nt = (((1,), (1,)), ((), ()))

    for s in range(NY):
        for t in range(NX):
            blk = NY * lax.rem(x - t + NX, NX) + lax.rem(y - s + NY, NY)
            rows = pl.ds(pl.multiple_of(blk * BLK, BLK), BLK)
            k_piece = kv_in[s][t * BLK : (t + 1) * BLK, 0:HD]
            k_all[rows, :] = k_piece
            v_all[rows, :] = kv_in[s][t * BLK : (t + 1) * BLK, HD : 2 * HD]
            kt_all[lax.div(blk, 2), :, pl.ds(pl.multiple_of(lax.rem(blk, 2) * BLK, BLK), BLK)] = k_piece.T
    for s in range(NX):
        qd[s] = qd_in[s][...]
    dk[...] = jnp.zeros_like(dk)
    dv[...] = jnp.zeros_like(dv)

    def fold(value, op):
        return op(value.reshape(KB // 8, 8, KB), axis=0)

    def query_block(j, carry):
        base = (NY * lax.rem(x - j + NX, NX) + y) * BLK
        q_pos = base + (lax.broadcasted_iota(jnp.int32, (1, KB), 1) & (BLK - 1))
        start = jnp.zeros((1, KB), jnp.int32)
        first, run = jnp.int32(0), jnp.int32(0)
        for n in range(8):
            run = run + lens[n]
            start = jnp.maximum(start, jnp.where(q_pos >= run, run, 0))
            first = jnp.maximum(first, jnp.where(base >= run, run, 0))
        lo, hi = lax.div(first, KB), lax.div(base, KB) + 1

        def scores(kb, tops):
            keys = k_all[pl.ds(pl.multiple_of(kb * KB, KB), KB), :]
            k_pos = kb * KB + lax.broadcasted_iota(jnp.int32, (KB, KB), 0)
            keep = (k_pos >= start) & (k_pos <= q_pos)
            out = []
            for i, part in enumerate(chunks):
                s = lax.dot_general(keys, qd[j, 0, part, :], nt, preferred_element_type=F32)
                s = jnp.where(keep, s, -jnp.inf)
                s_all[kb - lo, :, part] = s
                out.append(jnp.maximum(tops[i], fold(s, jnp.max)))
            return tuple(out)

        tops = lax.fori_loop(lo, hi, scores, tuple(jnp.full((8, KB), -jnp.inf, F32) for _ in chunks))
        factor = SCALE * LOG2E
        tops = [jnp.max(t, axis=0, keepdims=True) * factor for t in tops]

        def weights(kb, sums):
            vals = v_all[pl.ds(pl.multiple_of(kb * KB, KB), KB), :]
            total, dots = [], []
            for i, part in enumerate(chunks):
                dp = lax.dot_general(vals, qd[j, 1, part, :], nt, preferred_element_type=F32)
                p = jnp.exp2(s_all[kb - lo, :, part] * factor - tops[i])
                s_all[kb - lo, :, part] = p
                dp_all[kb - lo, :, part] = dp
                total.append(sums[0][i] + fold(p, jnp.sum))
                dots.append(sums[1][i] + fold(p * dp, jnp.sum))
            return tuple(total), tuple(dots)

        zero = tuple(jnp.zeros((8, KB), F32) for _ in chunks)
        total, dots = lax.fori_loop(lo, hi, weights, (zero, zero))
        inv = [1.0 / jnp.sum(t, axis=0, keepdims=True) for t in total]
        row_dot = [jnp.sum(d, axis=0, keepdims=True) * i for d, i in zip(dots, inv)]
        dqt[...] = jnp.zeros_like(dqt)

        def grads(kb, carry):
            rows = pl.ds(pl.multiple_of(kb * KB, KB), KB)
            for i, part in enumerate(chunks):
                p = s_all[kb - lo, :, part] * inv[i]
                pb[:, part] = p.astype(BF)
                dsb[:, part] = (p * (dp_all[kb - lo, :, part] - row_dot[i])).astype(BF)
            dv[rows, :] += jnp.dot(pb[...], qd[j, 1], preferred_element_type=F32)
            dk[rows, :] += jnp.dot(dsb[...], qd[j, 0], preferred_element_type=F32)
            dqt[...] += jnp.dot(kt_all[kb], dsb[...], preferred_element_type=F32)
            return carry

        lax.fori_loop(lo, hi, grads, 0)
        for h in range(group):
            head = slice(h * BLK, (h + 1) * BLK)
            dq_all[j, head, :] = (dqt[:, head].T * SCALE).astype(BF)
        return carry

    lax.fori_loop(0, NX, query_block, 0)
    for s in range(NX):
        dq_out[s][...] = dq_all[s]
    for s in range(NY):
        for t in range(NX):
            blk = NY * t + lax.rem(y + s, NY)
            rows = pl.ds(pl.multiple_of(blk * BLK, BLK), BLK)
            r_out[s][t * BLK : (t + 1) * BLK, 0:HD] = (dk[rows, :] * SCALE).astype(BF)
            r_out[s][t * BLK : (t + 1) * BLK, HD : 2 * HD] = dv[rows, :].astype(BF)


def join_q_kernel(at, *refs):
    out = refs[-1]
    group = HQ // HK
    for s in range(NX):
        first = lax.rem(at[0] + s, NX) * (group * HD)
        for h in range(group):
            out[:, pl.ds(pl.multiple_of(first + h * HD, HD), HD)] = refs[s][h * BLK : (h + 1) * BLK, :]


def project_kernel(pairs_n, at, xt, *refs):
    own, other = refs[0:pairs_n], refs[pairs_n : 2 * pairs_n]
    outs, acc = refs[2 * pairs_n : 2 * pairs_n + NY], refs[-1]
    for t in range(pairs_n):
        acc[...] = jnp.dot(xt[:, 0:512], own[t][...], preferred_element_type=F32) + jnp.dot(
            xt[:, 512:1024], other[t][...], preferred_element_type=F32
        )
        for s in range(NY):
            for z in range(NZ):
                row = pl.multiple_of(z * BLK + lax.rem(at[1] + s, NY) * 32, 32)
                outs[s][z, :, t * 256 : (t + 1) * 256] = acc[pl.ds(row, 32), :].astype(BF)


def finish_kernel(at, *refs):
    parts, wk, wv = refs[:-2], refs[-2], refs[-1]
    for t in range(NX):
        part = parts[t // 2]
        col = pl.multiple_of(lax.rem(at[0] - t + NX, NX) * HD, HD)
        first = (t % 2) * 256
        wk[:, pl.ds(col, HD)] = jnp.sum(part[:, :, first : first + HD].astype(F32), axis=0)
        wv[:, pl.ds(col, HD)] = jnp.sum(part[:, :, first + HD : first + 2 * HD].astype(F32), axis=0)


def total(values):
    acc = values[0].astype(F32)
    for value in values[1:]:
        acc = acc + value.astype(F32)
    return acc.astype(BF)


def on_device(layer_input, queries, key_rows, value_rows, d_out, doc_lengths):
    head, dp = lax.axis_index("head"), lax.axis_index("dp")
    at = jnp.stack([head // NY, head % NY, dp % NC, dp // NC]).astype(jnp.int32)
    with jax.named_scope("pack_kv"):
        kv = call(pack_kv_kernel, [sds((BLK, 256))] * 4, (at, key_rows, value_rows), moved=1 << 19)
    with jax.named_scope("pack_q_do"):
        qd = call(pack_heads_kernel, [sds((2, 1024, HD))] * 4, (at, queries, d_out), moved=1 << 22)
    with jax.named_scope("pack_x"):
        xp = call(pack_x_kernel, [sds((BLK, 1024))] * 8, (at, layer_input), moved=1 << 22)
    with jax.named_scope("kv_over_x"):
        kv = [kv[0]] + [send(kv[s], dx=s) for s in range(1, NX)]
        kv = jnp.concatenate(kv, axis=0)
    with jax.named_scope("q_do_over_x"):
        qd = [qd[0]] + [send(qd[s], dx=s) for s in range(1, NX)]
    with jax.named_scope("kv_over_y"):
        kv = [kv] + [send(kv, dy=s) for s in range(1, NY)]
    with jax.named_scope("x_over_x"):
        xp = [xp[i] if i == 0 else send(xp[i], dx=i // 2, dc=i % 2) for i in range(8)]
        (xt,) = call(turn_x_kernel, [sds((1024, 1024))], (at, *xp), moved=1 << 22)
    with jax.named_scope("attention"):
        outs = call(
            attention_kernel,
            [sds((1024, HD))] * 4 + [sds((512, 256))] * 4,
            (at, doc_lengths[0], *qd, *kv),
            scratch=[
                pltpu.VMEM((4, 2, 1024, HD), BF),
                pltpu.VMEM((2048, HD), BF),
                pltpu.VMEM((2048, HD), BF),
                pltpu.VMEM((8, HD, KB), BF),
                pltpu.VMEM((MAX_KB, KB, 1024), F32),
                pltpu.VMEM((MAX_KB, KB, 1024), F32),
                pltpu.VMEM((KB, 1024), BF),
                pltpu.VMEM((KB, 1024), BF),
                pltpu.VMEM((HD, 1024), F32),
                pltpu.VMEM((2048, HD), F32),
                pltpu.VMEM((2048, HD), F32),
                pltpu.VMEM((4, 1024, HD), BF),
            ],
            flops=15 * 10**9,
            moved=6 << 20,
            smem=2,
        )
    dq, terms = outs[:4], outs[4:]
    with jax.named_scope("terms_over_y"):
        dkv = total([terms[0]] + [send(terms[s], dy=s) for s in range(1, NY)])
    with jax.named_scope("dkv_over_x"):
        own = [dkv] + [send(dkv, dx=s) for s in range(1, NX)]
        other = [send(piece, dc=1) for piece in own]
    with jax.named_scope("project"):
        halves = []
        for half in range(2):
            pick = slice(2 * half, 2 * half + 2)
            partial = call(
                functools.partial(project_kernel, 2),
                [sds((NZ, 32, 512))] * 4,
                (at, xt, *own[pick], *other[pick]),
                scratch=[pltpu.VMEM((1024, 256), F32)],
                flops=10**9,
                moved=1 << 22,
            )
            with jax.named_scope("partial_over_y"):
                summed = total([partial[0]] + [send(partial[s], dy=s) for s in range(1, NY)])
            with jax.named_scope("partial_over_z"):
                groups = [[z * NC + c for z in range(NZ)] for c in range(NC)]
                halves.append(lax.all_to_all(summed, "dp", 0, 0, axis_index_groups=groups, tiled=True))
    with jax.named_scope("grad_q"):
        dq = [dq[0]] + [send(dq[s], dx=-s) for s in range(1, NX)]
        (grad_q,) = call(join_q_kernel, [sds((BLK, HQ * HD))], (at, *dq), moved=1 << 21)
    with jax.named_scope("finish"):
        wk, wv = call(finish_kernel, [sds((32, 512), F32)] * 2, (at, *halves), moved=1 << 20)
    return grad_q, wk, wv


def solution(mesh):
    spec = P(("dp", "head"), None)
    return jax.shard_map(
        on_device,
        mesh=mesh,
        in_specs=(spec, spec, spec, spec, spec, P("dp", None)),
        out_specs=(spec, spec, spec),
        check_vma=False,
    )
```

time: 530 us -> 183 us (0.35)
  waiting for transfers between devices: 261 us -> 73.4 us
  matrix products: 106 us -> 0 us
  other arithmetic: 70.2 us -> 3.34 us
  Pallas kernels: 0 us -> 42.4 us
  starting transfers between devices: 26.9 us -> 56.7 us
  local copies, waits for them, and re-layouts: 30.5 us -> 5.73 us
  blocking collectives: 15.6 us -> 0 us
  between operations: 14.6 us -> 0.98 us
    all_gather x4 -> x0, waiting for transfers between devices: 141 us -> none  [the longest x1 51.1 us: on_device(): lax.all_gather(dk_tok, 'head', axis=0, tiled=True)]
    dot_general x48 -> x0, matrix products: 86.3 us -> none  [the longest x16 19.9 us: add_block(): lax.dot_general(x_part, k_part, contract, preferred_element_type=jnp.floa...]
    reduce_scatter x2 -> x0, waiting for transfers between devices: 83.2 us -> none  [the longest x1 56.1 us: on_device(): lax.psum_scatter(window_k.reshape(windows_n, rows_out, width_kv).astype(j...]
    ppermute x0 -> x35, waiting for transfers between devices: none -> 66.4 us  [send(): return lax.ppermute(value, AXES, pairs)]
    add x16 -> x0, other arithmetic: 49.6 us -> none  [add_block(): return ((totals[0] + term_k, totals[1] + term_v), None)]
    ppermute x0 -> x35, starting transfers between devices: none -> 44.5 us  [send(): return lax.ppermute(value, AXES, pairs)]
    pallas_call x0 -> x9, Pallas kernels: none -> 42.4 us  [call(): pl.pallas_call(kernel, out_shape=outs, in_specs=[SM] * smem + [VM] * (len...]
    all_to_all x5 -> x2, waiting for transfers between devices: 35.7 us -> 7.02 us  [on_device(): lax.all_to_all(summed, 'dp', 0, 0, axis_index_groups=groups, tiled=True)]
  transfers between devices with their start and end apart: 11 -> 37, of which waited for: 9 -> 20; matrix products, arithmetic and copies ran while one was open for 14% -> 2% of each run, Pallas kernels for 0% -> 12%
where the time goes in v1:
time: 183 us
  waiting for transfers between devices  73.4 us (40%)
  starting transfers between devices  56.7 us (31%)
  Pallas kernels  42.4 us (23%)
  local copies, waits for them, and re-layouts  5.73 us (3%)
  other arithmetic  3.34 us (2%)
    ppermute x35, waiting for transfers between devices, send(): return lax.ppermute(value, AXES, pairs)  66.4 us
    ppermute x35, starting transfers between devices, send(): return lax.ppermute(value, AXES, pairs)  44.5 us
    pallas_call x9, Pallas kernels, call(): pl.pallas_call(kernel, out_shape=outs, in_specs=[SM] * smem + [VM] * (len...  42.4 us
    all_to_all x2, starting transfers between devices, on_device(): lax.all_to_all(summed, 'dp', 0, 0, axis_index_groups=groups, tiled=True)  12.2 us
    all_to_all x2, waiting for transfers between devices, on_device(): lax.all_to_all(summed, 'dp', 0, 0, axis_index_groups=groups, tiled=True)  7.02 us
    unnamed x69, local copies, waits for them, and re-layouts  5.72 us
  transfers between devices with their start and end apart: 37, of which 20 were waited for; matrix products, arithmetic and copies ran while one was open for 2% of the time, Pallas kernels for 12%

profile of v1, /device:TPU:1, one launch (start us, length us, event | category | flops | bytes accessed | tf_op | source)
XLA Modules:
  0.0 182.6 jit_solution(7145501046671064520)
XLA Ops:
  1.2 1.7 pack_kv.1
  2.9 2.0 %collective-permute-start.3 = (bf16[128,256]{1,0:T(8,128)(2,1)}, bf16[128,256]{1,0:T(8,128)(2,1)S(1)}, u32[]{:S(2)}, u32[]{:S(2)}) collective-permute-start(bf16[128,256]{1,0:T(8,128)(2,1)} %get-tuple-element.42), channel_id=1, source_target_pairs={{0,4},{1,5},{2,6},{3,7},{4,8},{5,9},{6,10},{7,11},{8,12},{9,13},{1... | collective-permute-start | bytes 196616 | tf_op jit(solution)/shard_map/kv_over_x/ppermute | solution.py:39
  5.0 2.5 %collective-permute-start.4 = (bf16[128,256]{1,0:T(8,128)(2,1)}, bf16[128,256]{1,0:T(8,128)(2,1)S(1)}, u32[]{:S(2)}, u32[]{:S(2)}) collective-permute-start(bf16[128,256]{1,0:T(8,128)(2,1)} %get-tuple-element.43), channel_id=1, source_target_pairs={{0,8},{1,9},{2,10},{3,11},{4,12},{5,13},{6,14},{7,15},{8,0},{9,1},... | collective-permute-start | bytes 196616 | tf_op jit(solution)/shard_map/kv_over_x/ppermute | solution.py:39
  7.4 1.2 collective-permute-start.5
  8.6 3.4 %pack_q_do.1 = (bf16[2,1024,128]{2,1,0:T(8,128)(2,1)}, bf16[2,1024,128]{2,1,0:T(8,128)(2,1)}, bf16[2,1024,128]{2,1,0:T(8,128)(2,1)}, bf16[2,1024,128]{2,1,0:T(8,128)(2,1)}) custom-call(s32[4]{0:T(128)} %pad_add_fusion.at, bf16[128,4096]{1,0:T(8,128)(2,1)} %q.1, bf16[128,4096]{1,0:T(8,128)(2,1)} %do.1), custom_call_target="tpu_custom_call" | custom-call | bytes 4194304 | tf_op jit(solution)/shard_map/pack_q_do/pallas_call | solution.py:43
  12.1 1.4 collective-permute-start.6
  13.8 2.2 %collective-permute-start.1 = (bf16[2,1024,128]{2,1,0:T(8,128)(2,1)}, bf16[2,1024,128]{2,1,0:T(8,128)(2,1)S(1)}, u32[]{:S(2)}, u32[]{:S(2)}) collective-permute-start(bf16[2,1024,128]{2,1,0:T(8,128)(2,1)} %get-tuple-element.39), channel_id=1, source_target_pairs={{0,8},{1,9},{2,10},{3,11},{4,12},{5,13},{6,14},{7,15},{8,0},{9,1},... | collective-permute-start | bytes 1572872 | tf_op jit(solution)/shard_map/q_do_over_x/ppermute | solution.py:39
  16.2 2.6 %collective-permute-start.7 = (bf16[512,256]{1,0:T(8,128)(2,1)S(1)}, bf16[512,256]{1,0:T(8,128)(2,1)S(1)}, u32[]{:S(2)}, u32[]{:S(2)}) collective-permute-start(bf16[512,256]{1,0:T(8,128)(2,1)S(1)} %constant_dynamic-update-slice_fusion.refs_4_), channel_id=1, source_target_pairs={{0,2},{1,3},{2,0},{3,1},{4,6},{5,7},{6,4},{7,5},{8,10},{9,11},{10,... | collective-permute-start | bytes 786440 | tf_op jit(solution)/shard_map/kv_over_y/ppermute | solution.py:39
  18.8 1.0 collective-permute-done.6.refs_5_
  19.8 1.4 collective-permute-start.8
  21.2 5.3 %collective-permute-done.7.refs_6_ = bf16[512,256]{1,0:T(8,128)(2,1)S(1)} collective-permute-done((bf16[512,256]{1,0:T(8,128)(2,1)S(1)}, bf16[512,256]{1,0:T(8,128)(2,1)S(1)}, u32[]{:S(2)}, u32[]{:S(2)}) %collective-permute-start.7) | collective-permute-done | bytes 262176 | tf_op jit(solution)/shard_map/kv_over_y/ppermute | solution.py:39
  27.3 9.7 %collective-permute-done.1.refs_2_ = bf16[2,1024,128]{2,1,0:T(8,128)(2,1)S(1)} collective-permute-done((bf16[2,1024,128]{2,1,0:T(8,128)(2,1)}, bf16[2,1024,128]{2,1,0:T(8,128)(2,1)S(1)}, u32[]{:S(2)}, u32[]{:S(2)}) %collective-permute-start.1) | collective-permute-done | bytes 524320 | tf_op jit(solution)/shard_map/q_do_over_x/ppermute | solution.py:39
  37.0 2.0 %collective-permute-done.2.refs_3_ = bf16[2,1024,128]{2,1,0:T(8,128)(2,1)S(1)} collective-permute-done((bf16[2,1024,128]{2,1,0:T(8,128)(2,1)}, bf16[2,1024,128]{2,1,0:T(8,128)(2,1)S(1)}, u32[]{:S(2)}, u32[]{:S(2)}) %collective-permute-start.2) | collective-permute-done | bytes 524320 | tf_op jit(solution)/shard_map/q_do_over_x/ppermute | solution.py:39
  39.8 17.3 %attention.1 = (bf16[1024,128]{1,0:T(8,128)(2,1)}, bf16[1024,128]{1,0:T(8,128)(2,1)}, bf16[1024,128]{1,0:T(8,128)(2,1)}, bf16[1024,128]{1,0:T(8,128)(2,1)}, bf16...) custom-call(s32[4]{0:T(128)} %pad_add_fusion.at, ...), custom_call_target="tpu_custom_call" | custom-call | flops 15000000512 | bytes 6291456 | tf_op jit(solution)/shard_map/attention/pallas_call | solution.py:43
  57.3 1.6 collective-permute-start.20
  59.6 3.5 %pack_x.1 = (bf16[128,1024]{1,0:T(8,128)(2,1)}, bf16[128,1024]{1,0:T(8,128)(2,1)}, bf16[128,1024]{1,0:T(8,128)(2,1)}, bf16[128,1024]{1,0:T(8,128)(2,1)}, bf16[12...) custom-call(s32[4]{0:T(128)} %pad_add_fusion.at, ...), custom_call_target="tpu_custom_call" | custom-call | bytes 4194304 | tf_op jit(solution)/shard_map/pack_x/pallas_call | solution.py:43
  63.1 2.9 %collective-permute-start.12 = (bf16[128,1024]{1,0:T(8,128)(2,1)}, bf16[128,1024]{1,0:T(8,128)(2,1)S(1)}, u32[]{:S(2)}, u32[]{:S(2)}) collective-permute-start(bf16[128,1024]{1,0:T(8,128)(2,1)} %get-tuple-element.50), channel_id=1, source_target_pairs={{0,16},{1,17},{2,18},{3,19},{4,20},{5,21},{6,22},{7,23},{8,24},{9,... | collective-permute-start | bytes 786440 | tf_op jit(solution)/shard_map/x_over_x/ppermute | solution.py:39
  66.0 2.5 %collective-permute-start.14 = (bf16[128,1024]{1,0:T(8,128)(2,1)}, bf16[128,1024]{1,0:T(8,128)(2,1)S(1)}, u32[]{:S(2)}, u32[]{:S(2)}) collective-permute-start(bf16[128,1024]{1,0:T(8,128)(2,1)} %get-tuple-element.52), channel_id=1, source_target_pairs={{0,20},{1,21},{2,22},{3,23},{4,24},{5,25},{6,26},{7,27},{8,28},{9,... | collective-permute-start | bytes 786440 | tf_op jit(solution)/shard_map/x_over_x/ppermute | solution.py:39
  68.5 3.3 %collective-permute-start.15 = (bf16[128,1024]{1,0:T(8,128)(2,1)}, bf16[128,1024]{1,0:T(8,128)(2,1)S(1)}, u32[]{:S(2)}, u32[]{:S(2)}) collective-permute-start(bf16[128,1024]{1,0:T(8,128)(2,1)} %get-tuple-element.53), channel_id=1, source_target_pairs={{0,8},{1,9},{2,10},{3,11},{4,12},{5,13},{6,14},{7,15},{8,0},{9,1},... | collective-permute-start | bytes 786440 | tf_op jit(solution)/shard_map/x_over_x/ppermute | solution.py:39
  72.5 2.1 %collective-permute-start.16 = (bf16[128,1024]{1,0:T(8,128)(2,1)}, bf16[128,1024]{1,0:T(8,128)(2,1)S(1)}, u32[]{:S(2)}, u32[]{:S(2)}) collective-permute-start(bf16[128,1024]{1,0:T(8,128)(2,1)} %get-tuple-element.54), channel_id=1, source_target_pairs={{0,24},{1,25},{2,26},{3,27},{4,28},{5,29},{6,30},{7,31},{8,16},{9,... | collective-permute-start | bytes 786440 | tf_op jit(solution)/shard_map/x_over_x/ppermute | solution.py:39
  74.7 2.8 %collective-permute-start.17 = (bf16[128,1024]{1,0:T(8,128)(2,1)}, bf16[128,1024]{1,0:T(8,128)(2,1)S(1)}, u32[]{:S(2)}, u32[]{:S(2)}) collective-permute-start(bf16[128,1024]{1,0:T(8,128)(2,1)} %get-tuple-element.55), channel_id=1, source_target_pairs={{0,12},{1,13},{2,14},{3,15},{4,0},{5,1},{6,2},{7,3},{8,4},{9,5},{1... | collective-permute-start | bytes 786440 | tf_op jit(solution)/shard_map/x_over_x/ppermute | solution.py:39
  77.5 3.5 %collective-permute-done.14.refs_3_ = bf16[128,1024]{1,0:T(8,128)(2,1)S(1)} collective-permute-done((bf16[128,1024]{1,0:T(8,128)(2,1)}, bf16[128,1024]{1,0:T(8,128)(2,1)S(1)}, u32[]{:S(2)}, u32[]{:S(2)}) %collective-permute-start.14) | collective-permute-done | bytes 262176 | tf_op jit(solution)/shard_map/x_over_x/ppermute | solution.py:39
  81.1 6.1 %collective-permute-done.15.refs_4_ = bf16[128,1024]{1,0:T(8,128)(2,1)S(1)} collective-permute-done((bf16[128,1024]{1,0:T(8,128)(2,1)}, bf16[128,1024]{1,0:T(8,128)(2,1)S(1)}, u32[]{:S(2)}, u32[]{:S(2)}) %collective-permute-start.15) | collective-permute-done | bytes 262176 | tf_op jit(solution)/shard_map/x_over_x/ppermute | solution.py:39
  87.2 6.1 %collective-permute-done.16.refs_5_ = bf16[128,1024]{1,0:T(8,128)(2,1)S(1)} collective-permute-done((bf16[128,1024]{1,0:T(8,128)(2,1)}, bf16[128,1024]{1,0:T(8,128)(2,1)S(1)}, u32[]{:S(2)}, u32[]{:S(2)}) %collective-permute-start.16) | collective-permute-done | bytes 262176 | tf_op jit(solution)/shard_map/x_over_x/ppermute | solution.py:39
  93.5 4.3 %collective-permute-done.22.refs_1_ = bf16[512,256]{1,0:T(8,128)(2,1)S(1)} collective-permute-done((bf16[512,256]{1,0:T(8,128)(2,1)S(1)}, bf16[512,256]{1,0:T(8,128)(2,1)S(1)}, u32[]{:S(2)}, u32[]{:S(2)}) %collective-permute-start.22) | collective-permute-done | bytes 262176 | tf_op jit(solution)/shard_map/dkv_over_x/ppermute | solution.py:39
  98.6 5.4 %collective-permute-done.28.refs_0_ = bf16[512,256]{1,0:T(8,128)(2,1)S(1)} collective-permute-done((bf16[512,256]{1,0:T(8,128)(2,1)S(1)}, bf16[512,256]{1,0:T(8,128)(2,1)S(1)}, u32[]{:S(2)}, u32[]{:S(2)}) %collective-permute-start.28) | collective-permute-done | bytes 262176 | tf_op jit(solution)/shard_map/dkv_over_x/ppermute | solution.py:39
  105.0 1.9 %collective-permute-done.18.refs_7_ = bf16[128,1024]{1,0:T(8,128)(2,1)S(1)} collective-permute-done((bf16[128,1024]{1,0:T(8,128)(2,1)}, bf16[128,1024]{1,0:T(8,128)(2,1)S(1)}, u32[]{:S(2)}, u32[]{:S(2)}) %collective-permute-start.18) | collective-permute-done | bytes 262176 | tf_op jit(solution)/shard_map/x_over_x/ppermute | solution.py:39
  107.6 3.5 %x_over_x.1.xt = bf16[1024,1024]{1,0:T(8,128)(2,1)} custom-call(s32[4]{0:T(128)} %pad_add_fusion.at, bf16[128,1024]{1,0:T(8,128)(2,1)} %get-tuple-element.49.refs_0_, bf16[128,1024]{1,0:T(8,128)(2,1)} %copy-done.2, bf16[128,1024]{1,0:T(8,128)(2,1)} %copy-done.3, bf16[128,1024]{1,0:T(8,128)(2,1)} %copy-done.4, bf16[128,1024]{1,0:T(8,128)(2,1)} %copy-done.6, ...), custom_call_target="tpu_custom_call" | custom-call | bytes 4194304 | tf_op jit(solution)/shard_map/x_over_x/pallas_call | solution.py:43
  112.5 4.4 %project.2 = (bf16[8,32,512]{2,1,0:T(8,128)(2,1)}, bf16[8,32,512]{2,1,0:T(8,128)(2,1)}, bf16[8,32,512]{2,1,0:T(8,128)(2,1)}, bf16[8,32,512]{2,1,0:T(8,128)(2,1)}) custom-call(s32[4]{0:T(128)} %pad_add_fusion.at, bf16[1024,1024]{1,0:T(8,128)(2,1)} %x_over_x.1.xt, bf16[512,256]{1,0:T(8,128)(2,1)} %copy-done.5, bf16[512,256]{1,0:T(8,128)(2,1)} %copy-done.25, ...), custom_call_target="tpu_custom_call" | custom-call | flops 1000000000 | bytes 4194304 | tf_op jit(solution)/shard_map/project/pallas_call | solution.py:43
  116.9 4.5 %collective-permute-start.27 = (bf16[8,32,512]{2,1,0:T(8,128)(2,1)}, bf16[8,32,512]{2,1,0:T(8,128)(2,1)S(1)}, u32[]{:S(2)}, u32[]{:S(2)}) collective-permute-start(bf16[8,32,512]{2,1,0:T(8,128)(2,1)} %get-tuple-element.64), channel_id=1, source_target_pairs={{0,3},{1,0},{2,1},{3,2},{4,7},{5,4},{6,5},{7,6},{8,11},{9,8},{10,9... | collective-permute-start | bytes 786440 | tf_op jit(solution)/shard_map/project/partial_over_y/ppermute | solution.py:39
  123.4 4.4 %project.3 = (bf16[8,32,512]{2,1,0:T(8,128)(2,1)}, bf16[8,32,512]{2,1,0:T(8,128)(2,1)}, bf16[8,32,512]{2,1,0:T(8,128)(2,1)}, bf16[8,32,512]{2,1,0:T(8,128)(2,1)}) custom-call(s32[4]{0:T(128)} %pad_add_fusion.at, bf16[1024,1024]{1,0:T(8,128)(2,1)} %x_over_x.1.xt, bf16[512,256]{1,0:T(8,128)(2,1)} %copy-done.23, bf16[512,256]{1,0:T(8,128)(2,1)} %copy-done.24, ...), custom_call_target="tpu_custom_call" | custom-call | flops 1000000000 | bytes 4194304 | tf_op jit(solution)/shard_map/project/pallas_call | solution.py:43
  127.8 2.4 %collective-permute-start.34 = (bf16[8,32,512]{2,1,0:T(8,128)(2,1)}, bf16[8,32,512]{2,1,0:T(8,128)(2,1)S(1)}, u32[]{:S(2)}, u32[]{:S(2)}) collective-permute-start(bf16[8,32,512]{2,1,0:T(8,128)(2,1)} %get-tuple-element.68), channel_id=1, source_target_pairs={{0,3},{1,0},{2,1},{3,2},{4,7},{5,4},{6,5},{7,6},{8,11},{9,8},{10,9... | collective-permute-start | bytes 786440 | tf_op jit(solution)/shard_map/project/partial_over_y/ppermute | solution.py:39
  130.2 1.4 collective-permute-start.33
  131.7 1.7 collective-permute-done.27
  133.4 3.8 %collective-permute-done.25 = bf16[8,32,512]{2,1,0:T(8,128)(2,1)S(1)} collective-permute-done((bf16[8,32,512]{2,1,0:T(8,128)(2,1)}, bf16[8,32,512]{2,1,0:T(8,128)(2,1)S(1)}, u32[]{:S(2)}, u32[]{:S(2)}) %collective-permute-start.25) | collective-permute-done | bytes 262176 | tf_op jit(solution)/shard_map/project/partial_over_y/ppermute | solution.py:39
  137.2 0.8 add_convert_fusion.1
  138.0 8.8 %all-to-all-start = ((bf16[8,32,512]{2,1,0:T(8,128)(2,1)}), bf16[8,32,512]{2,1,0:T(8,128)(2,1)S(1)}, u32[]{:S(2)}, u32[]{:S(2)}) async-start(bf16[8,32,512]{2,1,0:T(8,128)(2,1)} %add_convert_fusion.1), calls=%async_computation | async-start | bytes 524288 | tf_op jit(solution)/shard_map/project/partial_over_z/all_to_all | solution.py:296
  146.8 1.4 collective-permute-done.32
  148.2 1.8 add_convert_fusion
  150.0 7.0 %all-to-all-done.refs_0_ = bf16[8,32,512]{2,1,0:T(8,128)(2,1)S(1)} async-done(((bf16[8,32,512]{2,1,0:T(8,128)(2,1)}), bf16[8,32,512]{2,1,0:T(8,128)(2,1)S(1)}, u32[]{:S(2)}, u32[]{:S(2)}) %all-to-all-start) | async-done | bytes 262176 | tf_op jit(solution)/shard_map/project/partial_over_z/all_to_all | solution.py:296
  157.0 3.4 %all-to-all-start.1 = ((bf16[8,32,512]{2,1,0:T(8,128)(2,1)}), bf16[8,32,512]{2,1,0:T(8,128)(2,1)S(1)}, u32[]{:S(2)}, u32[]{:S(2)}) async-start(bf16[8,32,512]{2,1,0:T(8,128)(2,1)} %add_convert_fusion), calls=%async_computation.1 | async-start | bytes 524288 | tf_op jit(solution)/shard_map/project/partial_over_z/all_to_all | solution.py:296
  160.5 2.5 %collective-permute-start.9 = (bf16[1024,128]{1,0:T(8,128)(2,1)S(1)}, bf16[1024,128]{1,0:T(8,128)(2,1)S(1)}, u32[]{:S(2)}, u32[]{:S(2)}) collective-permute-start(bf16[1024,128]{1,0:T(8,128)(2,1)S(1)} %copy-done.22), channel_id=1, source_target_pairs={{0,12},{1,13},{2,14},{3,15},{4,0},{5,1},{6,2},{7,3},{8,4},{9,5},{1... | collective-permute-start | bytes 786440 | tf_op jit(solution)/shard_map/grad_q/ppermute | solution.py:39
  163.0 1.4 collective-permute-start.10
  164.4 2.6 %collective-permute-done.9.refs_1_ = bf16[1024,128]{1,0:T(8,128)(2,1)S(1)} collective-permute-done((bf16[1024,128]{1,0:T(8,128)(2,1)S(1)}, bf16[1024,128]{1,0:T(8,128)(2,1)S(1)}, u32[]{:S(2)}, u32[]{:S(2)}) %collective-permute-start.9) | collective-permute-done | bytes 262176 | tf_op jit(solution)/shard_map/grad_q/ppermute | solution.py:39
  167.0 3.1 %collective-permute-done.10.refs_2_ = bf16[1024,128]{1,0:T(8,128)(2,1)S(1)} collective-permute-done((bf16[1024,128]{1,0:T(8,128)(2,1)S(1)}, bf16[1024,128]{1,0:T(8,128)(2,1)S(1)}, u32[]{:S(2)}, u32[]{:S(2)}) %collective-permute-start.10) | collective-permute-done | bytes 262176 | tf_op jit(solution)/shard_map/grad_q/ppermute | solution.py:39
  170.1 6.9 %collective-permute-done.11.refs_3_ = bf16[1024,128]{1,0:T(8,128)(2,1)S(1)} collective-permute-done((bf16[1024,128]{1,0:T(8,128)(2,1)S(1)}, bf16[1024,128]{1,0:T(8,128)(2,1)S(1)}, u32[]{:S(2)}, u32[]{:S(2)}) %collective-permute-start.11) | collective-permute-done | bytes 262176 | tf_op jit(solution)/shard_map/grad_q/ppermute | solution.py:39
  177.6 2.4 %grad_q.1 = bf16[128,4096]{1,0:T(8,128)(2,1)} custom-call(s32[4]{0:T(128)} %pad_add_fusion.at, bf16[1024,128]{1,0:T(8,128)(2,1)} %get-tuple-element.45.refs_0_, bf16[1024,128]{1,0:T(8,128)(2,1)} %copy-done.12, bf16[1024,128]{1,0:T(8,128)(2,1)} %copy-done.13, bf16[1024,128]{1,0:T(8,128)(2,1)} %copy-done.14), custom_call_target="tpu_custom_call" | custom-call | bytes 2097152 | tf_op jit(solution)/shard_map/grad_q/pallas_call | solution.py:43
  180.8 1.8 finish.1
  (109 shorter events, 11.7 us)
Async XLA Ops:
  2.9 9.1 %collective-permute-start.3 = (bf16[128,256]{1,0:T(8,128)(2,1)}, bf16[128,256]{1,0:T(8,128)(2,1)S(1)}, u32[]{:S(2)}, u32[]{:S(2)}) collective-permute-start(bf16[128,256]{1,0:T(8,128)(2,1)} %get-tuple-element.42), channel_id=1, source_target_pairs={{0,4},{1,5},{2,6},{3,7},{4,8},{5,9},{6,10},{7,11},{8,12},{9,13},{1... | collective-permute-start | bytes 196616 | tf_op jit(solution)/shard_map/kv_over_x/ppermute | solution.py:39
  5.0 7.1 %collective-permute-start.4 = (bf16[128,256]{1,0:T(8,128)(2,1)}, bf16[128,256]{1,0:T(8,128)(2,1)S(1)}, u32[]{:S(2)}, u32[]{:S(2)}) collective-permute-start(bf16[128,256]{1,0:T(8,128)(2,1)} %get-tuple-element.43), channel_id=1, source_target_pairs={{0,8},{1,9},{2,10},{3,11},{4,12},{5,13},{6,14},{7,15},{8,0},{9,1},... | collective-permute-start | bytes 196616 | tf_op jit(solution)/shard_map/kv_over_x/ppermute | solution.py:39
  7.4 4.6 %collective-permute-start.5 = (bf16[128,256]{1,0:T(8,128)(2,1)}, bf16[128,256]{1,0:T(8,128)(2,1)S(1)}, u32[]{:S(2)}, u32[]{:S(2)}) collective-permute-start(bf16[128,256]{1,0:T(8,128)(2,1)} %get-tuple-element.44), channel_id=1, source_target_pairs={{0,12},{1,13},{2,14},{3,15},{4,0},{5,1},{6,2},{7,3},{8,4},{9,5},{1... | collective-permute-start | bytes 196616 | tf_op jit(solution)/shard_map/kv_over_x/ppermute | solution.py:39
  12.1 27.0 %copy-start.16 = (bf16[512,256]{1,0:T(8,128)(2,1)}, bf16[512,256]{1,0:T(8,128)(2,1)S(1)}, u32[]{:S(2)}) copy-start(bf16[512,256]{1,0:T(8,128)(2,1)S(1)} %constant_dynamic-update-slice_fusion.refs_4_) | copy-start | bytes 786436
  12.1 7.7 %collective-permute-start.6 = (bf16[512,256]{1,0:T(8,128)(2,1)S(1)}, bf16[512,256]{1,0:T(8,128)(2,1)S(1)}, u32[]{:S(2)}, u32[]{:S(2)}) collective-permute-start(bf16[512,256]{1,0:T(8,128)(2,1)S(1)} %constant_dynamic-update-slice_fusion.refs_4_), channel_id=1, source_target_pairs={{0,1},{1,2},{2,3},{3,0},{4,5},{5,6},{6,7},{7,4},{8,9},{9,10},{10,1... | collective-permute-start | bytes 786440 | tf_op jit(solution)/shard_map/kv_over_y/ppermute | solution.py:39
  13.5 13.8 %collective-permute-start = (bf16[2,1024,128]{2,1,0:T(8,128)(2,1)}, bf16[2,1024,128]{2,1,0:T(8,128)(2,1)S(1)}, u32[]{:S(2)}, u32[]{:S(2)}) collective-permute-start(bf16[2,1024,128]{2,1,0:T(8,128)(2,1)} %get-tuple-element.38), channel_id=1, source_target_pairs={{0,4},{1,5},{2,6},{3,7},{4,8},{5,9},{6,10},{7,11},{8,12},{9,13},{1... | collective-permute-start | bytes 1572872 | tf_op jit(solution)/shard_map/q_do_over_x/ppermute | solution.py:39
  13.8 23.2 %collective-permute-start.1 = (bf16[2,1024,128]{2,1,0:T(8,128)(2,1)}, bf16[2,1024,128]{2,1,0:T(8,128)(2,1)S(1)}, u32[]{:S(2)}, u32[]{:S(2)}) collective-permute-start(bf16[2,1024,128]{2,1,0:T(8,128)(2,1)} %get-tuple-element.39), channel_id=1, source_target_pairs={{0,8},{1,9},{2,10},{3,11},{4,12},{5,13},{6,14},{7,15},{8,0},{9,1},... | collective-permute-start | bytes 1572872 | tf_op jit(solution)/shard_map/q_do_over_x/ppermute | solution.py:39
  16.0 23.1 %collective-permute-start.2 = (bf16[2,1024,128]{2,1,0:T(8,128)(2,1)}, bf16[2,1024,128]{2,1,0:T(8,128)(2,1)S(1)}, u32[]{:S(2)}, u32[]{:S(2)}) collective-permute-start(bf16[2,1024,128]{2,1,0:T(8,128)(2,1)} %get-tuple-element.40), channel_id=1, source_target_pairs={{0,12},{1,13},{2,14},{3,15},{4,0},{5,1},{6,2},{7,3},{8,4},{9,5},{1... | collective-permute-start | bytes 1572872 | tf_op jit(solution)/shard_map/q_do_over_x/ppermute | solution.py:39
  16.2 10.3 %collective-permute-start.7 = (bf16[512,256]{1,0:T(8,128)(2,1)S(1)}, bf16[512,256]{1,0:T(8,128)(2,1)S(1)}, u32[]{:S(2)}, u32[]{:S(2)}) collective-permute-start(bf16[512,256]{1,0:T(8,128)(2,1)S(1)} %constant_dynamic-update-slice_fusion.refs_4_), channel_id=1, source_target_pairs={{0,2},{1,3},{2,0},{3,1},{4,6},{5,7},{6,4},{7,5},{8,10},{9,11},{10,... | collective-permute-start | bytes 786440 | tf_op jit(solution)/shard_map/kv_over_y/ppermute | solution.py:39
  19.8 7.0 %collective-permute-start.8 = (bf16[512,256]{1,0:T(8,128)(2,1)S(1)}, bf16[512,256]{1,0:T(8,128)(2,1)S(1)}, u32[]{:S(2)}, u32[]{:S(2)}) collective-permute-start(bf16[512,256]{1,0:T(8,128)(2,1)S(1)} %constant_dynamic-update-slice_fusion.refs_4_), channel_id=1, source_target_pairs={{0,3},{1,0},{2,1},{3,2},{4,7},{5,4},{6,5},{7,6},{8,11},{9,8},{10,9... | collective-permute-start | bytes 786440 | tf_op jit(solution)/shard_map/kv_over_y/ppermute | solution.py:39
  57.2 8.8 %collective-permute-start.21 = (bf16[512,256]{1,0:T(8,128)(2,1)}, bf16[512,256]{1,0:T(8,128)(2,1)S(1)}, u32[]{:S(2)}, u32[]{:S(2)}) collective-permute-start(bf16[512,256]{1,0:T(8,128)(2,1)} %get-tuple-element.60), channel_id=1, source_target_pairs={{0,3},{1,0},{2,1},{3,2},{4,7},{5,4},{6,5},{7,6},{8,11},{9,8},{10,9... | collective-permute-start | bytes 786440 | tf_op jit(solution)/shard_map/terms_over_y/ppermute | solution.py:39
  57.3 11.3 %collective-permute-start.20 = (bf16[512,256]{1,0:T(8,128)(2,1)}, bf16[512,256]{1,0:T(8,128)(2,1)S(1)}, u32[]{:S(2)}, u32[]{:S(2)}) collective-permute-start(bf16[512,256]{1,0:T(8,128)(2,1)} %get-tuple-element.59), channel_id=1, source_target_pairs={{0,2},{1,3},{2,0},{3,1},{4,6},{5,7},{6,4},{7,5},{8,10},{9,11},{10,... | collective-permute-start | bytes 786440 | tf_op jit(solution)/shard_map/terms_over_y/ppermute | solution.py:39
  58.9 13.6 %collective-permute-start.19 = (bf16[512,256]{1,0:T(8,128)(2,1)}, bf16[512,256]{1,0:T(8,128)(2,1)S(1)}, u32[]{:S(2)}, u32[]{:S(2)}) collective-permute-start(bf16[512,256]{1,0:T(8,128)(2,1)} %get-tuple-element.58), channel_id=1, source_target_pairs={{0,1},{1,2},{2,3},{3,0},{4,5},{5,6},{6,7},{7,4},{8,9},{9,10},{10,1... | collective-permute-start | bytes 786440 | tf_op jit(solution)/shard_map/terms_over_y/ppermute | solution.py:39
  63.1 11.5 %collective-permute-start.12 = (bf16[128,1024]{1,0:T(8,128)(2,1)}, bf16[128,1024]{1,0:T(8,128)(2,1)S(1)}, u32[]{:S(2)}, u32[]{:S(2)}) collective-permute-start(bf16[128,1024]{1,0:T(8,128)(2,1)} %get-tuple-element.50), channel_id=1, source_target_pairs={{0,16},{1,17},{2,18},{3,19},{4,20},{5,21},{6,22},{7,23},{8,24},{9,... | collective-permute-start | bytes 786440 | tf_op jit(solution)/shard_map/x_over_x/ppermute | solution.py:39
  66.0 11.5 %collective-permute-start.13 = (bf16[128,1024]{1,0:T(8,128)(2,1)}, bf16[128,1024]{1,0:T(8,128)(2,1)S(1)}, u32[]{:S(2)}, u32[]{:S(2)}) collective-permute-start(bf16[128,1024]{1,0:T(8,128)(2,1)} %get-tuple-element.51), channel_id=1, source_target_pairs={{0,4},{1,5},{2,6},{3,7},{4,8},{5,9},{6,10},{7,11},{8,12},{9,13},{1... | collective-permute-start | bytes 786440 | tf_op jit(solution)/shard_map/x_over_x/ppermute | solution.py:39
  66.0 15.1 %collective-permute-start.14 = (bf16[128,1024]{1,0:T(8,128)(2,1)}, bf16[128,1024]{1,0:T(8,128)(2,1)S(1)}, u32[]{:S(2)}, u32[]{:S(2)}) collective-permute-start(bf16[128,1024]{1,0:T(8,128)(2,1)} %get-tuple-element.52), channel_id=1, source_target_pairs={{0,20},{1,21},{2,22},{3,23},{4,24},{5,25},{6,26},{7,27},{8,28},{9,... | collective-permute-start | bytes 786440 | tf_op jit(solution)/shard_map/x_over_x/ppermute | solution.py:39
  68.5 18.7 %collective-permute-start.15 = (bf16[128,1024]{1,0:T(8,128)(2,1)}, bf16[128,1024]{1,0:T(8,128)(2,1)S(1)}, u32[]{:S(2)}, u32[]{:S(2)}) collective-permute-start(bf16[128,1024]{1,0:T(8,128)(2,1)} %get-tuple-element.53), channel_id=1, source_target_pairs={{0,8},{1,9},{2,10},{3,11},{4,12},{5,13},{6,14},{7,15},{8,0},{9,1},... | collective-permute-start | bytes 786440 | tf_op jit(solution)/shard_map/x_over_x/ppermute | solution.py:39
  72.5 20.9 %collective-permute-start.16 = (bf16[128,1024]{1,0:T(8,128)(2,1)}, bf16[128,1024]{1,0:T(8,128)(2,1)S(1)}, u32[]{:S(2)}, u32[]{:S(2)}) collective-permute-start(bf16[128,1024]{1,0:T(8,128)(2,1)} %get-tuple-element.54), channel_id=1, source_target_pairs={{0,24},{1,25},{2,26},{3,27},{4,28},{5,29},{6,30},{7,31},{8,16},{9,... | collective-permute-start | bytes 786440 | tf_op jit(solution)/shard_map/x_over_x/ppermute | solution.py:39
  74.7 36.5 %copy-start.5 = (bf16[512,256]{1,0:T(8,128)(2,1)}, bf16[512,256]{1,0:T(8,128)(2,1)S(1)}, u32[]{:S(2)}) copy-start(bf16[512,256]{1,0:T(8,128)(2,1)S(1)} %add_convert_fusion.2.refs_0_) | copy-start | bytes 786436
  74.7 32.2 %copy-start.2 = (bf16[128,1024]{1,0:T(8,128)(2,1)}, bf16[128,1024]{1,0:T(8,128)(2,1)S(1)}, u32[]{:S(2)}) copy-start(bf16[128,1024]{1,0:T(8,128)(2,1)S(1)} %collective-permute-done.12.refs_1_) | copy-start | bytes 786436
  74.7 18.7 %collective-permute-start.17 = (bf16[128,1024]{1,0:T(8,128)(2,1)}, bf16[128,1024]{1,0:T(8,128)(2,1)S(1)}, u32[]{:S(2)}, u32[]{:S(2)}) collective-permute-start(bf16[128,1024]{1,0:T(8,128)(2,1)} %get-tuple-element.55), channel_id=1, source_target_pairs={{0,12},{1,13},{2,14},{3,15},{4,0},{5,1},{6,2},{7,3},{8,4},{9,5},{1... | collective-permute-start | bytes 786440 | tf_op jit(solution)/shard_map/x_over_x/ppermute | solution.py:39
  77.5 29.4 %copy-start.3 = (bf16[128,1024]{1,0:T(8,128)(2,1)}, bf16[128,1024]{1,0:T(8,128)(2,1)S(1)}, u32[]{:S(2)}) copy-start(bf16[128,1024]{1,0:T(8,128)(2,1)S(1)} %collective-permute-done.13.refs_2_) | copy-start | bytes 786436
  77.5 20.3 %collective-permute-start.22 = (bf16[512,256]{1,0:T(8,128)(2,1)S(1)}, bf16[512,256]{1,0:T(8,128)(2,1)S(1)}, u32[]{:S(2)}, u32[]{:S(2)}) collective-permute-start(bf16[512,256]{1,0:T(8,128)(2,1)S(1)} %add_convert_fusion.2.refs_0_), channel_id=1, source_target_pairs={{0,4},{1,5},{2,6},{3,7},{4,8},{5,9},{6,10},{7,11},{8,12},{9,13},{1... | collective-permute-start | bytes 786440 | tf_op jit(solution)/shard_map/dkv_over_x/ppermute | solution.py:39
  81.1 25.8 %copy-start.4 = (bf16[128,1024]{1,0:T(8,128)(2,1)}, bf16[128,1024]{1,0:T(8,128)(2,1)S(1)}, u32[]{:S(2)}) copy-start(bf16[128,1024]{1,0:T(8,128)(2,1)S(1)} %collective-permute-done.14.refs_3_) | copy-start | bytes 786436
  81.1 23.0 %collective-permute-start.28 = (bf16[512,256]{1,0:T(8,128)(2,1)S(1)}, bf16[512,256]{1,0:T(8,128)(2,1)S(1)}, u32[]{:S(2)}, u32[]{:S(2)}) collective-permute-start(bf16[512,256]{1,0:T(8,128)(2,1)S(1)} %add_convert_fusion.2.refs_0_), channel_id=1, source_target_pairs={{0,8},{1,9},{2,10},{3,11},{4,12},{5,13},{6,14},{7,15},{8,0},{9,1},... | collective-permute-start | bytes 786440 | tf_op jit(solution)/shard_map/dkv_over_x/ppermute | solution.py:39
  87.2 19.7 %copy-start.6 = (bf16[128,1024]{1,0:T(8,128)(2,1)}, bf16[128,1024]{1,0:T(8,128)(2,1)S(1)}, u32[]{:S(2)}) copy-start(bf16[128,1024]{1,0:T(8,128)(2,1)S(1)} %collective-permute-done.15.refs_4_) | copy-start | bytes 786436
  87.2 17.7 %collective-permute-start.29 = (bf16[512,256]{1,0:T(8,128)(2,1)S(1)}, bf16[512,256]{1,0:T(8,128)(2,1)S(1)}, u32[]{:S(2)}, u32[]{:S(2)}) collective-permute-start(bf16[512,256]{1,0:T(8,128)(2,1)S(1)} %add_convert_fusion.2.refs_0_), channel_id=1, source_target_pairs={{0,12},{1,13},{2,14},{3,15},{4,0},{5,1},{6,2},{7,3},{8,4},{9,5},{1... | collective-permute-start | bytes 786440 | tf_op jit(solution)/shard_map/dkv_over_x/ppermute | solution.py:39
  93.4 13.5 %collective-permute-start.18 = (bf16[128,1024]{1,0:T(8,128)(2,1)}, bf16[128,1024]{1,0:T(8,128)(2,1)S(1)}, u32[]{:S(2)}, u32[]{:S(2)}) collective-permute-start(bf16[128,1024]{1,0:T(8,128)(2,1)} %get-tuple-element.56), channel_id=1, source_target_pairs={{0,28},{1,29},{2,30},{3,31},{4,16},{5,17},{6,18},{7,19},{8,20},{9,... | collective-permute-start | bytes 786440 | tf_op jit(solution)/shard_map/x_over_x/ppermute | solution.py:39
  93.4 17.7 %collective-permute-start.23 = (bf16[512,256]{1,0:T(8,128)(2,1)S(1)}, bf16[512,256]{1,0:T(8,128)(2,1)S(1)}, u32[]{:S(2)}, u32[]{:S(2)}) collective-permute-start(bf16[512,256]{1,0:T(8,128)(2,1)S(1)} %add_convert_fusion.2.refs_0_), channel_id=1, source_target_pairs={{0,16},{1,17},{2,18},{3,19},{4,20},{5,21},{6,22},{7,23},{8,24},{9,... | collective-permute-start | bytes 786440 | tf_op jit(solution)/shard_map/dkv_over_x/ppermute | solution.py:39
  97.8 13.3 %collective-permute-start.24 = (bf16[512,256]{1,0:T(8,128)(2,1)S(1)}, bf16[512,256]{1,0:T(8,128)(2,1)S(1)}, u32[]{:S(2)}, u32[]{:S(2)}) collective-permute-start(bf16[512,256]{1,0:T(8,128)(2,1)S(1)} %collective-permute-done.22.refs_1_), channel_id=1, source_target_pairs={{0,16},{1,17},{2,18},{3,19},{4,20},{5,21},{6,22},{7,23},{8,24},{9,... | collective-permute-start | bytes 786440 | tf_op jit(solution)/shard_map/dkv_over_x/ppermute | solution.py:39
  104.1 17.9 %collective-permute-start.30 = (bf16[512,256]{1,0:T(8,128)(2,1)S(1)}, bf16[512,256]{1,0:T(8,128)(2,1)S(1)}, u32[]{:S(2)}, u32[]{:S(2)}) collective-permute-start(bf16[512,256]{1,0:T(8,128)(2,1)S(1)} %collective-permute-done.28.refs_0_), channel_id=1, source_target_pairs={{0,16},{1,17},{2,18},{3,19},{4,20},{5,21},{6,22},{7,23},{8,24},{9,... | collective-permute-start | bytes 786440 | tf_op jit(solution)/shard_map/dkv_over_x/ppermute | solution.py:39
  104.9 17.1 %collective-permute-start.31 = (bf16[512,256]{1,0:T(8,128)(2,1)S(1)}, bf16[512,256]{1,0:T(8,128)(2,1)S(1)}, u32[]{:S(2)}, u32[]{:S(2)}) collective-permute-start(bf16[512,256]{1,0:T(8,128)(2,1)S(1)} %collective-permute-done.29.refs_1_), channel_id=1, source_target_pairs={{0,16},{1,17},{2,18},{3,19},{4,20},{5,21},{6,22},{7,23},{8,24},{9,... | collective-permute-start | bytes 786440 | tf_op jit(solution)/shard_map/dkv_over_x/ppermute | solution.py:39
  116.9 20.3 %copy-start.10 = (bf16[8,32,512]{2,1,0:T(8,128)(2,1)S(1)}, bf16[8,32,512]{2,1,0:T(8,128)(2,1)}, u32[]{:S(2)}) copy-start(bf16[8,32,512]{2,1,0:T(8,128)(2,1)} %get-tuple-element.61) | copy-start | bytes 786436
  116.9 16.5 %collective-permute-start.27 = (bf16[8,32,512]{2,1,0:T(8,128)(2,1)}, bf16[8,32,512]{2,1,0:T(8,128)(2,1)S(1)}, u32[]{:S(2)}, u32[]{:S(2)}) collective-permute-start(bf16[8,32,512]{2,1,0:T(8,128)(2,1)} %get-tuple-element.64), channel_id=1, source_target_pairs={{0,3},{1,0},{2,1},{3,2},{4,7},{5,4},{6,5},{7,6},{8,11},{9,8},{10,9... | collective-permute-start | bytes 786440 | tf_op jit(solution)/shard_map/project/partial_over_y/ppermute | solution.py:39
  121.3 12.0 %collective-permute-start.26 = (bf16[8,32,512]{2,1,0:T(8,128)(2,1)}, bf16[8,32,512]{2,1,0:T(8,128)(2,1)S(1)}, u32[]{:S(2)}, u32[]{:S(2)}) collective-permute-start(bf16[8,32,512]{2,1,0:T(8,128)(2,1)} %get-tuple-element.63), channel_id=1, source_target_pairs={{0,2},{1,3},{2,0},{3,1},{4,6},{5,7},{6,4},{7,5},{8,10},{9,11},{10,... | collective-permute-start | bytes 786440 | tf_op jit(solution)/shard_map/project/partial_over_y/ppermute | solution.py:39
  121.6 15.5 %collective-permute-start.25 = (bf16[8,32,512]{2,1,0:T(8,128)(2,1)}, bf16[8,32,512]{2,1,0:T(8,128)(2,1)S(1)}, u32[]{:S(2)}, u32[]{:S(2)}) collective-permute-start(bf16[8,32,512]{2,1,0:T(8,128)(2,1)} %get-tuple-element.62), channel_id=1, source_target_pairs={{0,1},{1,2},{2,3},{3,0},{4,5},{5,6},{6,7},{7,4},{8,9},{9,10},{10,1... | collective-permute-start | bytes 786440 | tf_op jit(solution)/shard_map/project/partial_over_y/ppermute | solution.py:39
  127.8 32.6 %copy-start.22 = (bf16[1024,128]{1,0:T(8,128)(2,1)S(1)}, bf16[1024,128]{1,0:T(8,128)(2,1)}, u32[]{:S(2)}) copy-start(bf16[1024,128]{1,0:T(8,128)(2,1)} %get-tuple-element.46) | copy-start | bytes 786436
  127.8 35.2 %copy-start.21 = (bf16[1024,128]{1,0:T(8,128)(2,1)S(1)}, bf16[1024,128]{1,0:T(8,128)(2,1)}, u32[]{:S(2)}) copy-start(bf16[1024,128]{1,0:T(8,128)(2,1)} %get-tuple-element.47) | copy-start | bytes 786436
  127.8 36.5 %copy-start.20 = (bf16[1024,128]{1,0:T(8,128)(2,1)S(1)}, bf16[1024,128]{1,0:T(8,128)(2,1)}, u32[]{:S(2)}) copy-start(bf16[1024,128]{1,0:T(8,128)(2,1)} %get-tuple-element.48) | copy-start | bytes 786436
  127.8 19.0 %collective-permute-start.34 = (bf16[8,32,512]{2,1,0:T(8,128)(2,1)}, bf16[8,32,512]{2,1,0:T(8,128)(2,1)S(1)}, u32[]{:S(2)}, u32[]{:S(2)}) collective-permute-start(bf16[8,32,512]{2,1,0:T(8,128)(2,1)} %get-tuple-element.68), channel_id=1, source_target_pairs={{0,3},{1,0},{2,1},{3,2},{4,7},{5,4},{6,5},{7,6},{8,11},{9,8},{10,9... | collective-permute-start | bytes 786440 | tf_op jit(solution)/shard_map/project/partial_over_y/ppermute | solution.py:39
  130.2 16.6 %collective-permute-start.33 = (bf16[8,32,512]{2,1,0:T(8,128)(2,1)}, bf16[8,32,512]{2,1,0:T(8,128)(2,1)S(1)}, u32[]{:S(2)}, u32[]{:S(2)}) collective-permute-start(bf16[8,32,512]{2,1,0:T(8,128)(2,1)} %get-tuple-element.67), channel_id=1, source_target_pairs={{0,2},{1,3},{2,0},{3,1},{4,6},{5,7},{6,4},{7,5},{8,10},{9,11},{10,... | collective-permute-start | bytes 786440 | tf_op jit(solution)/shard_map/project/partial_over_y/ppermute | solution.py:39
  133.3 14.9 %collective-permute-start.32 = (bf16[8,32,512]{2,1,0:T(8,128)(2,1)}, bf16[8,32,512]{2,1,0:T(8,128)(2,1)S(1)}, u32[]{:S(2)}, u32[]{:S(2)}) collective-permute-start(bf16[8,32,512]{2,1,0:T(8,128)(2,1)} %get-tuple-element.66), channel_id=1, source_target_pairs={{0,1},{1,2},{2,3},{3,0},{4,5},{5,6},{6,7},{7,4},{8,9},{9,10},{10,1... | collective-permute-start | bytes 786440 | tf_op jit(solution)/shard_map/project/partial_over_y/ppermute | solution.py:39
  138.0 19.0 %all-to-all-start = ((bf16[8,32,512]{2,1,0:T(8,128)(2,1)}), bf16[8,32,512]{2,1,0:T(8,128)(2,1)S(1)}, u32[]{:S(2)}, u32[]{:S(2)}) async-start(bf16[8,32,512]{2,1,0:T(8,128)(2,1)} %add_convert_fusion.1), calls=%async_computation | async-start | bytes 524288 | tf_op jit(solution)/shard_map/project/partial_over_z/all_to_all | solution.py:296
  157.0 23.1 %copy-start = (bf16[8,32,512]{2,1,0:T(8,128)(2,1)}, bf16[8,32,512]{2,1,0:T(8,128)(2,1)S(1)}, u32[]{:S(2)}) copy-start(bf16[8,32,512]{2,1,0:T(8,128)(2,1)S(1)} %all-to-all-done.refs_0_) | copy-start | bytes 786436
  157.0 23.1 %all-to-all-start.1 = ((bf16[8,32,512]{2,1,0:T(8,128)(2,1)}), bf16[8,32,512]{2,1,0:T(8,128)(2,1)S(1)}, u32[]{:S(2)}, u32[]{:S(2)}) async-start(bf16[8,32,512]{2,1,0:T(8,128)(2,1)} %add_convert_fusion), calls=%async_computation.1 | async-start | bytes 524288 | tf_op jit(solution)/shard_map/project/partial_over_z/all_to_all | solution.py:296
  160.5 6.5 %collective-permute-start.9 = (bf16[1024,128]{1,0:T(8,128)(2,1)S(1)}, bf16[1024,128]{1,0:T(8,128)(2,1)S(1)}, u32[]{:S(2)}, u32[]{:S(2)}) collective-permute-start(bf16[1024,128]{1,0:T(8,128)(2,1)S(1)} %copy-done.22), channel_id=1, source_target_pairs={{0,12},{1,13},{2,14},{3,15},{4,0},{5,1},{6,2},{7,3},{8,4},{9,5},{1... | collective-permute-start | bytes 786440 | tf_op jit(solution)/shard_map/grad_q/ppermute | solution.py:39
  163.0 7.0 %collective-permute-start.10 = (bf16[1024,128]{1,0:T(8,128)(2,1)S(1)}, bf16[1024,128]{1,0:T(8,128)(2,1)S(1)}, u32[]{:S(2)}, u32[]{:S(2)}) collective-permute-start(bf16[1024,128]{1,0:T(8,128)(2,1)S(1)} %copy-done.21), channel_id=1, source_target_pairs={{0,8},{1,9},{2,10},{3,11},{4,12},{5,13},{6,14},{7,15},{8,0},{9,1},... | collective-permute-start | bytes 786440 | tf_op jit(solution)/shard_map/grad_q/ppermute | solution.py:39
  164.4 12.6 %collective-permute-start.11 = (bf16[1024,128]{1,0:T(8,128)(2,1)S(1)}, bf16[1024,128]{1,0:T(8,128)(2,1)S(1)}, u32[]{:S(2)}, u32[]{:S(2)}) collective-permute-start(bf16[1024,128]{1,0:T(8,128)(2,1)S(1)} %copy-done.20), channel_id=1, source_target_pairs={{0,4},{1,5},{2,6},{3,7},{4,8},{5,9},{6,10},{7,11},{8,12},{9,13},{1... | collective-permute-start | bytes 786440 | tf_op jit(solution)/shard_map/grad_q/ppermute | solution.py:39
  (22 other events, 182.4 us)

commit v2 on v1

--- a/solution.py
+++ b/solution.py
@@ -39,16 +39,20 @@
     return lax.ppermute(value, AXES, pairs)
 
 
-def call(kernel, outs, ins, scratch=(), flops=0, moved=0, limit=56, smem=1):
+def call(kernel, outs, ins, scratch=(), flops=0, moved=0, limit=16, smem=1, late=()):
+    body = kernel
+    if late:
+        n, skip = len(ins), len(late)
+        body = lambda *refs: kernel(*refs[:n], *refs[n + skip :])
     return pl.pallas_call(
-        kernel,
+        body,
         out_shape=outs,
-        in_specs=[SM] * smem + [VM] * (len(ins) - smem),
+        in_specs=[SM] * smem + [VM] * (len(ins) - smem) + [VM] * len(late),
         out_specs=[VM] * len(outs),
         scratch_shapes=list(scratch),
         compiler_params=pltpu.CompilerParams(vmem_limit_bytes=limit * 1024 * 1024),
         cost_estimate=pl.CostEstimate(flops=flops, bytes_accessed=moved, transcendentals=0),
-    )(*ins)
+    )(*ins, *late)
 
 
 def sds(shape, dtype=BF):
@@ -60,6 +64,11 @@
         first = pl.multiple_of(lax.rem(at[0] + s, NX) * HD, HD)
         outs[s][:, 0:HD] = k[:, pl.ds(first, HD)]
         outs[s][:, HD : 2 * HD] = v[:, pl.ds(first, HD)]
+
+
+def join_kv_kernel(at, *refs):
+    for s in range(NX):
+        refs[-1][s * BLK : (s + 1) * BLK, :] = refs[s][...]
 
 
 def pack_heads_kernel(at, q, do, *outs):
@@ -78,47 +87,53 @@
             core = lax.rem(at[2] + d, NC)
             for z in range(NZ):
                 col = z * (NC * 512) + core * 512 + lax.rem(at[0] + s, NX) * BLK
-                outs[2 * s + d][:, z * BLK : (z + 1) * BLK] = li[:, pl.ds(pl.multiple_of(col, BLK), BLK)]
+                outs[s][d, :, z * BLK : (z + 1) * BLK] = li[:, pl.ds(pl.multiple_of(col, BLK), BLK)]
 
 
 def turn_x_kernel(at, *refs):
-    out = refs[-1]
+    outs = refs[NX:]
     for d in range(NC):
         for s in range(NX):
-            spot = pl.multiple_of(d * 512 + lax.rem(at[0] - s + NX, NX) * BLK, BLK)
+            spot = pl.multiple_of(lax.rem(at[0] - s + NX, NX) * BLK, BLK)
             for z in range(NZ):
                 rows = pl.ds(z * BLK, BLK)
-                out[rows, pl.ds(spot, BLK)] = refs[2 * s + d][:, z * BLK : (z + 1) * BLK].T
-
-
-def attention_kernel(at, lens, *refs):
-    qd_in, kv_in = refs[0:4], refs[4:8]
-    dq_out, r_out = refs[8:12], refs[12:16]
-    qd, k_all, v_all, kt_all, s_all, dp_all, pb, dsb, dqt, dk, dv, dq_all = refs[16:]
+                outs[d][rows, pl.ds(spot, BLK)] = refs[s][d, :, z * BLK : (z + 1) * BLK].T
+
+
+def attention_kernel(first_piece, at, lens, *refs):
     x, y = at[0], at[1]
     group = HQ // HK
     rows_n = group * BLK
     chunks = [slice(i * KB, (i + 1) * KB) for i in range(rows_n // KB)]
     nt = (((1,), (1,)), ((), ()))
-
-    for s in range(NY):
-        for t in range(NX):
-            blk = NY * lax.rem(x - t + NX, NX) + lax.rem(y - s + NY, NY)
-            rows = pl.ds(pl.multiple_of(blk * BLK, BLK), BLK)
-            k_piece = kv_in[s][t * BLK : (t + 1) * BLK, 0:HD]
-            k_all[rows, :] = k_piece
-            v_all[rows, :] = kv_in[s][t * BLK : (t + 1) * BLK, HD : 2 * HD]
-            kt_all[lax.div(blk, 2), :, pl.ds(pl.multiple_of(lax.rem(blk, 2) * BLK, BLK), BLK)] = k_piece.T
-    for s in range(NX):
+    qd_in, refs = refs[0:2], refs[2:]
+    if first_piece == 0:
+        kv_in, dq_out = refs[0:4], refs[4:6]
+        dk, dv, k_all, v_all, kt_all, qd, s_all, dp_all, pb, dsb, dqt, dq_all = refs[6:]
+        for s in range(NY):
+            for t in range(NX):
+                blk = NY * lax.rem(x - t + NX, NX) + lax.rem(y - s + NY, NY)
+                rows = pl.ds(pl.multiple_of(blk * BLK, BLK), BLK)
+                k_piece = kv_in[s][t * BLK : (t + 1) * BLK, 0:HD]
+                k_all[rows, :] = k_piece
+                v_all[rows, :] = kv_in[s][t * BLK : (t + 1) * BLK, HD : 2 * HD]
+                kt_all[lax.div(blk, 2), :, pl.ds(pl.multiple_of(lax.rem(blk, 2) * BLK, BLK), BLK)] = k_piece.T
+        dk[...] = jnp.zeros_like(dk)
+        dv[...] = jnp.zeros_like(dv)
+    else:
+        dk_in, dv_in, k_all, v_all, kt_all = refs[0:5]
+        dq_out, r_out = refs[5:7], refs[7:11]
+        qd, s_all, dp_all, pb, dsb, dqt, dq_all, dk, dv = refs[11:]
+        dk[...] = dk_in[...]
+        dv[...] = dv_in[...]
+    for s in range(2):
         qd[s] = qd_in[s][...]
-    dk[...] = jnp.zeros_like(dk)
-    dv[...] = jnp.zeros_like(dv)
 
     def fold(value, op):
         return op(value.reshape(KB // 8, 8, KB), axis=0)
 
     def query_block(j, carry):
-        base = (NY * lax.rem(x - j + NX, NX) + y) * BLK
+        base = (NY * lax.rem(x - j - first_piece + NX, NX) + y) * BLK
         q_pos = base + (lax.broadcasted_iota(jnp.int32, (1, KB), 1) & (BLK - 1))
         start = jnp.zeros((1, KB), jnp.int32)
         first, run = jnp.int32(0), jnp.int32(0)
@@ -179,9 +194,11 @@
             dq_all[j, head, :] = (dqt[:, head].T * SCALE).astype(BF)
         return carry
 
-    lax.fori_loop(0, NX, query_block, 0)
-    for s in range(NX):
+    lax.fori_loop(0, 2, query_block, 0)
+    for s in range(2):
         dq_out[s][...] = dq_all[s]
+    if first_piece == 0:
+        return
     for s in range(NY):
         for t in range(NX):
             blk = NY * t + lax.rem(y + s, NY)
@@ -199,12 +216,12 @@
             out[:, pl.ds(pl.multiple_of(first + h * HD, HD), HD)] = refs[s][h * BLK : (h + 1) * BLK, :]
 
 
-def project_kernel(pairs_n, at, xt, *refs):
+def project_kernel(pairs_n, at, xt, xt_other, *refs):
     own, other = refs[0:pairs_n], refs[pairs_n : 2 * pairs_n]
     outs, acc = refs[2 * pairs_n : 2 * pairs_n + NY], refs[-1]
     for t in range(pairs_n):
-        acc[...] = jnp.dot(xt[:, 0:512], own[t][...], preferred_element_type=F32) + jnp.dot(
-            xt[:, 512:1024], other[t][...], preferred_element_type=F32
+        acc[...] = jnp.dot(xt[...], own[t][...], preferred_element_type=F32) + jnp.dot(
+            xt_other[...], other[t][...], preferred_element_type=F32
         )
         for s in range(NY):
             for z in range(NZ):
@@ -212,14 +229,39 @@
                 outs[s][z, :, t * 256 : (t + 1) * 256] = acc[pl.ds(row, 32), :].astype(BF)
 
 
-def finish_kernel(at, *refs):
-    parts, wk, wv = refs[:-2], refs[-2], refs[-1]
+def add_kernel(*refs):
+    out, first = refs[-1], 0
+    for terms in [refs[i : i + NY] for i in range(0, len(refs) - 1, NY)]:
+        wide = terms[0].shape[2]
+        for z in range(NZ):
+            acc = terms[0][z].astype(F32)
+            for term in terms[1:]:
+                acc = acc + term[z].astype(F32)
+            out[z, :, first : first + wide] = acc.astype(BF)
+        first += wide
+
+
+def finish_kernel(at, part, wk, wv):
     for t in range(NX):
-        part = parts[t // 2]
         col = pl.multiple_of(lax.rem(at[0] - t + NX, NX) * HD, HD)
-        first = (t % 2) * 256
+        first = t * 256
         wk[:, pl.ds(col, HD)] = jnp.sum(part[:, :, first : first + HD].astype(F32), axis=0)
         wv[:, pl.ds(col, HD)] = jnp.sum(part[:, :, first + HD : first + 2 * HD].astype(F32), axis=0)
+
+
+def pass_kernel(n, *refs):
+    for i in range(n):
+        refs[i - n][...] = refs[i][...]
+
+
+def after(values, first):
+    n = len(values)
+    outs = [sds(v.shape, v.dtype) for v in values]
+    return call(functools.partial(pass_kernel, n), outs, (*values, *first), moved=1024, smem=0)
+
+
+def split(n, values):
+    return list(values[:n]), list(values[n:])
 
 
 def total(values):
@@ -235,70 +277,93 @@
     with jax.named_scope("pack_kv"):
         kv = call(pack_kv_kernel, [sds((BLK, 256))] * 4, (at, key_rows, value_rows), moved=1 << 19)
     with jax.named_scope("pack_q_do"):
-        qd = call(pack_heads_kernel, [sds((2, 1024, HD))] * 4, (at, queries, d_out), moved=1 << 22)
-    with jax.named_scope("pack_x"):
-        xp = call(pack_x_kernel, [sds((BLK, 1024))] * 8, (at, layer_input), moved=1 << 22)
+        qd = call(pack_heads_kernel, [sds((2, 1024, HD))] * 4, (at, queries, d_out), moved=1 << 22, late=[kv[1]])
     with jax.named_scope("kv_over_x"):
         kv = [kv[0]] + [send(kv[s], dx=s) for s in range(1, NX)]
-        kv = jnp.concatenate(kv, axis=0)
+        qd = [qd[0], *after(qd[1:], kv[1:])]
+        (kv,) = call(join_kv_kernel, [sds((512, 256))], (at, *kv), moved=1 << 19, late=[qd[1]])
+    with jax.named_scope("pack_x"):
+        xp = call(pack_x_kernel, [sds((NC, BLK, 1024))] * 4, (at, layer_input), moved=1 << 22, late=[kv])
     with jax.named_scope("q_do_over_x"):
         qd = [qd[0]] + [send(qd[s], dx=s) for s in range(1, NX)]
     with jax.named_scope("kv_over_y"):
         kv = [kv] + [send(kv, dy=s) for s in range(1, NY)]
-    with jax.named_scope("x_over_x"):
-        xp = [xp[i] if i == 0 else send(xp[i], dx=i // 2, dc=i % 2) for i in range(8)]
-        (xt,) = call(turn_x_kernel, [sds((1024, 1024))], (at, *xp), moved=1 << 22)
     with jax.named_scope("attention"):
-        outs = call(
-            attention_kernel,
-            [sds((1024, HD))] * 4 + [sds((512, 256))] * 4,
-            (at, doc_lengths[0], *qd, *kv),
-            scratch=[
-                pltpu.VMEM((4, 2, 1024, HD), BF),
-                pltpu.VMEM((2048, HD), BF),
-                pltpu.VMEM((2048, HD), BF),
-                pltpu.VMEM((8, HD, KB), BF),
-                pltpu.VMEM((MAX_KB, KB, 1024), F32),
-                pltpu.VMEM((MAX_KB, KB, 1024), F32),
-                pltpu.VMEM((KB, 1024), BF),
-                pltpu.VMEM((KB, 1024), BF),
-                pltpu.VMEM((HD, 1024), F32),
-                pltpu.VMEM((2048, HD), F32),
-                pltpu.VMEM((2048, HD), F32),
-                pltpu.VMEM((4, 1024, HD), BF),
-            ],
-            flops=15 * 10**9,
-            moved=6 << 20,
-            smem=2,
+        held = [sds((2048, HD), F32)] * 2 + [sds((2048, HD))] * 2 + [sds((8, HD, KB))]
+        scratch = [
+            pltpu.VMEM((2, 2, 1024, HD), BF),
+            pltpu.VMEM((MAX_KB, KB, 1024), F32),
+            pltpu.VMEM((MAX_KB, KB, 1024), F32),
+            pltpu.VMEM((KB, 1024), BF),
+            pltpu.VMEM((KB, 1024), BF),
+            pltpu.VMEM((HD, 1024), F32),
+            pltpu.VMEM((2, 1024, HD), BF),
+        ]
+        dq_a, held = split(
+            2,
+            call(
+                functools.partial(attention_kernel, 0),
+                [sds((1024, HD))] * 2 + held,
+                (at, doc_lengths[0], *qd[:2], *kv),
+                scratch=scratch,
+                flops=8 * 10**9,
+                moved=6 << 20,
+                limit=32,
+                smem=2,
+            ),
         )
-    dq, terms = outs[:4], outs[4:]
+        give = after(xp[1:], [dq_a[0], qd[2]])
+        xp = [xp[0]] + [send(d, dx=s + 1) for s, d in enumerate(give)]
+        dq_b, terms = split(
+            2,
+            call(
+                functools.partial(attention_kernel, 2),
+                [sds((1024, HD))] * 2 + [sds((512, 256))] * 4,
+                (at, doc_lengths[0], *qd[2:], *held),
+                scratch=scratch + [pltpu.VMEM((2048, HD), F32)] * 2,
+                flops=8 * 10**9,
+                moved=6 << 20,
+                limit=32,
+                smem=2,
+                late=give[:1],
+            ),
+        )
+    dq = dq_a + dq_b
     with jax.named_scope("terms_over_y"):
-        dkv = total([terms[0]] + [send(terms[s], dy=s) for s in range(1, NY)])
+        terms = [terms[0]] + [send(d, dy=s + 1) for s, d in enumerate(after(terms[1:], [xp[1]]))]
+        dkv = total(terms)
+    with jax.named_scope("turn_x"):
+        xt, xt_give = call(turn_x_kernel, [sds((1024, 512))] * 2, (at, *xp), moved=1 << 22, late=terms[1:])
+        xt_other = send(xt_give, dc=1)
     with jax.named_scope("dkv_over_x"):
         own = [dkv] + [send(dkv, dx=s) for s in range(1, NX)]
-        other = [send(piece, dc=1) for piece in own]
+        other = [send(piece, dc=1) for piece in own[:2]]
     with jax.named_scope("project"):
-        halves = []
-        for half in range(2):
-            pick = slice(2 * half, 2 * half + 2)
+        parts = []
+        for pick in (slice(0, 1), slice(1, 4)):
+            n = pick.stop - pick.start
             partial = call(
-                functools.partial(project_kernel, 2),
-                [sds((NZ, 32, 512))] * 4,
-                (at, xt, *own[pick], *other[pick]),
+                functools.partial(project_kernel, n),
+                [sds((NZ, 32, 256 * n))] * 4,
+                (at, xt, xt_other, *own[pick], *other[pick]),
                 scratch=[pltpu.VMEM((1024, 256), F32)],
-                flops=10**9,
+                flops=n * 5 * 10**8,
                 moved=1 << 22,
+
             )
             with jax.named_scope("partial_over_y"):
-                summed = total([partial[0]] + [send(partial[s], dy=s) for s in range(1, NY)])
-            with jax.named_scope("partial_over_z"):
-                groups = [[z * NC + c for z in range(NZ)] for c in range(NC)]
-                halves.append(lax.all_to_all(summed, "dp", 0, 0, axis_index_groups=groups, tiled=True))
+                parts += [partial[0]] + [send(partial[s], dy=s) for s in range(1, NY)]
+            if len(other) == 2:
+                other += [send(piece, dc=1) for piece in after(own[2:], parts[1:])]
+    with jax.named_scope("partial_over_z"):
+        dq = [dq[0]] + [send(d, dx=-s - 1) for s, d in enumerate(after(dq[1:], [parts[4]]))]
+        (summed,) = call(add_kernel, [sds((NZ, 32, 1024))], parts, moved=5 << 20, smem=0, late=dq[1:])
+        groups = [[z * NC + c for z in range(NZ)] for c in range(NC)]
+        last = lax.all_to_all(summed, "dp", 0, 0, axis_index_groups=groups, tiled=True)
     with jax.named_scope("grad_q"):
-        dq = [dq[0]] + [send(dq[s], dx=-s) for s in range(1, NX)]
         (grad_q,) = call(join_q_kernel, [sds((BLK, HQ * HD))], (at, *dq), moved=1 << 21)
     with jax.named_scope("finish"):
-        wk, wv = call(finish_kernel, [sds((32, 512), F32)] * 2, (at, *halves), moved=1 << 20)
+        wk, wv = call(finish_kernel, [sds((32, 512), F32)] * 2, (at, last), moved=1 << 20)
     return grad_q, wk, wv
 
 

time: 183 us -> 154 us (0.84)
  Pallas kernels: 42.4 us -> 24.1 us
  waiting for transfers between devices: 73.4 us -> 64.3 us
  starting transfers between devices: 56.7 us -> 60.7 us
  other arithmetic: 3.34 us -> 0.22 us
    pallas_call x9 -> x17, Pallas kernels: 42.4 us -> 24.1 us  [call(): pl.pallas_call(body, out_shape=outs, in_specs=[SM] * smem + [VM] * (len(i...]
    ppermute x35 -> x32, waiting for transfers between devices: 66.4 us -> 49.6 us  [send(): return lax.ppermute(value, AXES, pairs)]
    all_to_all x2 -> x1, waiting for transfers between devices: 7.02 us -> 14.6 us  [on_device(): lax.all_to_all(summed, 'dp', 0, 0, axis_index_groups=groups, tiled=True)]
    ppermute x35 -> x32, starting transfers between devices: 44.5 us -> 48 us  [send(): return lax.ppermute(value, AXES, pairs)]
    convert_element_type x3 -> x1, other arithmetic: 2.78 us -> 0.15 us  [total(): return acc.astype(BF)]
    unnamed x69 -> x12, local copies, waits for them, and re-layouts: 5.72 us -> 4.27 us
    all_to_all x2 -> x1, starting transfers between devices: 12.2 us -> 12.7 us  [on_device(): lax.all_to_all(summed, 'dp', 0, 0, axis_index_groups=groups, tiled=True)]
  transfers between devices with their start and end apart: 37 -> 33, of which waited for: 20 -> 13; matrix products, arithmetic and copies ran while one was open for 2% -> 0% of each run, Pallas kernels for 12% -> 11%
where the time goes in v2:
time: 154 us
  waiting for transfers between devices  64.3 us (42%)
  starting transfers between devices  60.7 us (39%)
  Pallas kernels  24.1 us (16%)
  local copies, waits for them, and re-layouts  4.27 us (3%)
    ppermute x32, waiting for transfers between devices, send(): return lax.ppermute(value, AXES, pairs)  49.6 us
    ppermute x32, starting transfers between devices, send(): return lax.ppermute(value, AXES, pairs)  48 us
    pallas_call x17, Pallas kernels, call(): pl.pallas_call(body, out_shape=outs, in_specs=[SM] * smem + [VM] * (len(i...  24.1 us
    all_to_all x1, waiting for transfers between devices, on_device(): lax.all_to_all(summed, 'dp', 0, 0, axis_index_groups=groups, tiled=True)  14.6 us
    all_to_all x1, starting transfers between devices, on_device(): lax.all_to_all(summed, 'dp', 0, 0, axis_index_groups=groups, tiled=True)  12.7 us
    unnamed x12, local copies, waits for them, and re-layouts  4.27 us
  transfers between devices with their start and end apart: 33, of which 13 were waited for; matrix products, arithmetic and copies ran while one was open for 0% of the time, Pallas kernels for 11%

profile of v2, /device:TPU:1, one launch (start us, length us, event | category | flops | bytes accessed | tf_op | source)
XLA Modules:
  0.0 154.4 jit_solution(10530833223670515862)
XLA Ops:
  0.7 0.9 copy-done.3
  1.7 0.9 copy-done.4
  2.6 0.6 pack_kv.1
  3.2 2.1 %collective-permute-start = (bf16[128,256]{1,0:T(8,128)(2,1)S(1)}, bf16[128,256]{1,0:T(8,128)(2,1)S(1)}, u32[]{:S(2)}, u32[]{:S(2)}) collective-permute-start(bf16[128,256]{1,0:T(8,128)(2,1)S(1)} %get-tuple-element.54.refs_3_), channel_id=1, source_target_pairs={{0,4},{1,5},{2,6},{3,7},{4,8},{5,9},{6,10},{7,11},{8,12},{9,13},{1... | collective-permute-start | bytes 196616 | tf_op jit(solution)/shard_map/kv_over_x/ppermute | solution.py:39
  5.3 2.5 %collective-permute-start.1 = (bf16[128,256]{1,0:T(8,128)(2,1)S(1)}, bf16[128,256]{1,0:T(8,128)(2,1)S(1)}, u32[]{:S(2)}, u32[]{:S(2)}) collective-permute-start(bf16[128,256]{1,0:T(8,128)(2,1)S(1)} %get-tuple-element.59), channel_id=1, source_target_pairs={{0,8},{1,9},{2,10},{3,11},{4,12},{5,13},{6,14},{7,15},{8,0},{9,1},... | collective-permute-start | bytes 196616 | tf_op jit(solution)/shard_map/kv_over_x/ppermute | solution.py:39
  7.7 1.2 collective-permute-start.2
  8.9 1.2 copy-done.1
  10.1 1.2 copy-done.2
  11.3 1.1 pack_q_do.1
  13.0 0.6 kv_over_x.3.refs_2_
  13.5 1.4 collective-permute-start.4
  14.9 2.6 %collective-permute-start.5 = (bf16[512,256]{1,0:T(8,128)(2,1)S(1)}, bf16[512,256]{1,0:T(8,128)(2,1)S(1)}, u32[]{:S(2)}, u32[]{:S(2)}) collective-permute-start(bf16[512,256]{1,0:T(8,128)(2,1)S(1)} %kv_over_x.3.refs_2_), channel_id=1, source_target_pairs={{0,2},{1,3},{2,0},{3,1},{4,6},{5,7},{6,4},{7,5},{8,10},{9,11},{10,... | collective-permute-start | bytes 786440 | tf_op jit(solution)/shard_map/kv_over_y/ppermute | solution.py:39
  17.5 1.1 collective-permute-start.6
  18.6 1.9 %collective-permute-start.7 = (bf16[2,1024,128]{2,1,0:T(8,128)(2,1)S(1)}, bf16[2,1024,128]{2,1,0:T(8,128)(2,1)S(1)}, u32[]{:S(2)}, u32[]{:S(2)}) collective-permute-start(bf16[2,1024,128]{2,1,0:T(8,128)(2,1)S(1)} %get-tuple-element.65), channel_id=1, source_target_pairs={{0,8},{1,9},{2,10},{3,11},{4,12},{5,13},{6,14},{7,15},{8,0},{9,1},... | collective-permute-start | bytes 1572872 | tf_op jit(solution)/shard_map/q_do_over_x/ppermute | solution.py:39
  20.5 1.1 pack_x.1
  21.6 1.7 %collective-permute-start.8 = (bf16[2,1024,128]{2,1,0:T(8,128)(2,1)S(1)}, bf16[2,1024,128]{2,1,0:T(8,128)(2,1)S(1)}, u32[]{:S(2)}, u32[]{:S(2)}) collective-permute-start(bf16[2,1024,128]{2,1,0:T(8,128)(2,1)S(1)} %get-tuple-element.66), channel_id=1, source_target_pairs={{0,12},{1,13},{2,14},{3,15},{4,0},{5,1},{6,2},{7,3},{8,4},{9,5},{1... | collective-permute-start | bytes 1572872 | tf_op jit(solution)/shard_map/q_do_over_x/ppermute | solution.py:39
  23.3 4.4 %collective-permute-done.5.refs_4_ = bf16[512,256]{1,0:T(8,128)(2,1)S(1)} collective-permute-done((bf16[512,256]{1,0:T(8,128)(2,1)S(1)}, bf16[512,256]{1,0:T(8,128)(2,1)S(1)}, u32[]{:S(2)}, u32[]{:S(2)}) %collective-permute-start.5) | collective-permute-done | bytes 262176 | tf_op jit(solution)/shard_map/kv_over_y/ppermute | solution.py:39
  27.7 5.1 %attention.3 = (bf16[1024,128]{1,0:T(8,128)(2,1)S(1)}, bf16[1024,128]{1,0:T(8,128)(2,1)S(1)}, f32[2048,128]{1,0:T(8,128)S(1)}, f32[2048,128]{1,0:T(8,128)S(1)}, ...) custom-call(s32[4]{0:T(128)S(1)} %pad_add_fusion.at.refs_0_, ...), custom_call_target="tpu_custom_call" | custom-call | flops 8000000000 | bytes 6291456 | tf_op jit(solution)/shard_map/attention/pallas_call | solution.py:47
  32.8 2.3 %collective-permute-done.7.refs_4_.refs_2_ = bf16[2,1024,128]{2,1,0:T(8,128)(2,1)S(1)} collective-permute-done((bf16[2,1024,128]{2,1,0:T(8,128)(2,1)S(1)}, bf16[2,1024,128]{2,1,0:T(8,128)(2,1)S(1)}, u32[]{:S(2)}, u32[]{:S(2)}) %collective-permute-start.7) | collective-permute-done | bytes 524320 | tf_op jit(solution)/shard_map/q_do_over_x/ppermute | solution.py:39
  35.3 2.3 %collective-permute-start.10 = (bf16[2,128,1024]{2,1,0:T(8,128)(2,1)S(1)}, bf16[2,128,1024]{2,1,0:T(8,128)(2,1)S(1)}, u32[]{:S(2)}, u32[]{:S(2)}) collective-permute-start(bf16[2,128,1024]{2,1,0:T(8,128)(2,1)S(1)} %get-tuple-element.79), channel_id=1, source_target_pairs={{0,8},{1,9},{2,10},{3,11},{4,12},{5,13},{6,14},{7,15},{8,0},{9,1},... | collective-permute-start | bytes 1572872 | tf_op jit(solution)/shard_map/attention/ppermute | solution.py:39
  37.6 2.0 %collective-permute-start.11 = (bf16[2,128,1024]{2,1,0:T(8,128)(2,1)S(1)}, bf16[2,128,1024]{2,1,0:T(8,128)(2,1)S(1)}, u32[]{:S(2)}, u32[]{:S(2)}) collective-permute-start(bf16[2,128,1024]{2,1,0:T(8,128)(2,1)S(1)} %get-tuple-element.80), channel_id=1, source_target_pairs={{0,12},{1,13},{2,14},{3,15},{4,0},{5,1},{6,2},{7,3},{8,4},{9,5},{1... | collective-permute-start | bytes 1572872 | tf_op jit(solution)/shard_map/attention/ppermute | solution.py:39
  39.6 7.1 %collective-permute-done.8.refs_3_ = bf16[2,1024,128]{2,1,0:T(8,128)(2,1)S(1)} collective-permute-done((bf16[2,1024,128]{2,1,0:T(8,128)(2,1)S(1)}, bf16[2,1024,128]{2,1,0:T(8,128)(2,1)S(1)}, u32[]{:S(2)}, u32[]{:S(2)}) %collective-permute-start.8) | collective-permute-done | bytes 524320 | tf_op jit(solution)/shard_map/q_do_over_x/ppermute | solution.py:39
  46.7 6.1 %attention.5 = (bf16[1024,128]{1,0:T(8,128)(2,1)S(1)}, bf16[1024,128]{1,0:T(8,128)(2,1)S(1)}, bf16[512,256]{1,0:T(8,128)(2,1)S(1)}, bf16[512,256]{1,0:T(8,128)(2...) custom-call(s32[4]{0:T(128)S(1)} %pad_add_fusion.at.refs_0_, s32[8]{0:T(128)S(1)} %bitcast.6, ...), custom_call_target="tpu_custom_call" | custom-call | flops 8000000000 | bytes 6291456 | tf_op jit(solution)/shard_map/attention/pallas_call | solution.py:47
  53.5 2.4 %collective-permute-start.14 = (bf16[512,256]{1,0:T(8,128)(2,1)S(1)}, bf16[512,256]{1,0:T(8,128)(2,1)S(1)}, u32[]{:S(2)}, u32[]{:S(2)}) collective-permute-start(bf16[512,256]{1,0:T(8,128)(2,1)S(1)} %get-tuple-element.86), channel_id=1, source_target_pairs={{0,3},{1,0},{2,1},{3,2},{4,7},{5,4},{6,5},{7,6},{8,11},{9,8},{10,9... | collective-permute-start | bytes 786440 | tf_op jit(solution)/shard_map/terms_over_y/ppermute | solution.py:39
  55.8 10.2 %collective-permute-done.11.refs_4_ = bf16[2,128,1024]{2,1,0:T(8,128)(2,1)S(1)} collective-permute-done((bf16[2,128,1024]{2,1,0:T(8,128)(2,1)S(1)}, bf16[2,128,1024]{2,1,0:T(8,128)(2,1)S(1)}, u32[]{:S(2)}, u32[]{:S(2)}) %collective-permute-start.11) | collective-permute-done | bytes 524320 | tf_op jit(solution)/shard_map/attention/ppermute | solution.py:39
  66.0 1.1 turn_x.1
  67.1 8.9 %collective-permute-start.15 = (bf16[1024,512]{1,0:T(8,128)(2,1)S(1)}, bf16[1024,512]{1,0:T(8,128)(2,1)S(1)}, u32[]{:S(2)}, u32[]{:S(2)}) collective-permute-start(bf16[1024,512]{1,0:T(8,128)(2,1)S(1)} %get-tuple-element.88), channel_id=1, source_target_pairs={{0,16},{1,17},{2,18},{3,19},{4,20},{5,21},{6,22},{7,23},{8,24},{9,... | collective-permute-start | bytes 3145736 | tf_op jit(solution)/shard_map/turn_x/ppermute | solution.py:39
  76.8 2.2 %collective-permute-start.18 = (bf16[512,256]{1,0:T(8,128)(2,1)S(1)}, bf16[512,256]{1,0:T(8,128)(2,1)S(1)}, u32[]{:S(2)}, u32[]{:S(2)}) collective-permute-start(bf16[512,256]{1,0:T(8,128)(2,1)S(1)} %add_convert_fusion.refs_0_), channel_id=1, source_target_pairs={{0,12},{1,13},{2,14},{3,15},{4,0},{5,1},{6,2},{7,3},{8,4},{9,5},{1... | collective-permute-start | bytes 786440 | tf_op jit(solution)/shard_map/dkv_over_x/ppermute | solution.py:39
  79.0 1.3 project.3
  80.3 1.3 collective-permute-start.21
  81.6 1.8 %collective-permute-start.22 = (bf16[8,32,256]{2,1,0:T(8,128)(2,1)S(1)}, bf16[8,32,256]{2,1,0:T(8,128)(2,1)S(1)}, u32[]{:S(2)}, u32[]{:S(2)}) collective-permute-start(bf16[8,32,256]{2,1,0:T(8,128)(2,1)S(1)} %get-tuple-element.91), channel_id=1, source_target_pairs={{0,2},{1,3},{2,0},{3,1},{4,6},{5,7},{6,4},{7,5},{8,10},{9,11},{10,... | collective-permute-start | bytes 393224 | tf_op jit(solution)/shard_map/project/partial_over_y/ppermute | solution.py:39
  83.5 7.1 %collective-permute-done.16.refs_0_ = bf16[512,256]{1,0:T(8,128)(2,1)S(1)} collective-permute-done((bf16[512,256]{1,0:T(8,128)(2,1)S(1)}, bf16[512,256]{1,0:T(8,128)(2,1)S(1)}, u32[]{:S(2)}, u32[]{:S(2)}) %collective-permute-start.16) | collective-permute-done | bytes 262176 | tf_op jit(solution)/shard_map/dkv_over_x/ppermute | solution.py:39
  90.6 1.9 %collective-permute-start.23 = (bf16[8,32,256]{2,1,0:T(8,128)(2,1)S(1)}, bf16[8,32,256]{2,1,0:T(8,128)(2,1)S(1)}, u32[]{:S(2)}, u32[]{:S(2)}) collective-permute-start(bf16[8,32,256]{2,1,0:T(8,128)(2,1)S(1)} %get-tuple-element.92), channel_id=1, source_target_pairs={{0,3},{1,0},{2,1},{3,2},{4,7},{5,4},{6,5},{7,6},{8,11},{9,8},{10,9... | collective-permute-start | bytes 393224 | tf_op jit(solution)/shard_map/project/partial_over_y/ppermute | solution.py:39
  92.5 1.5 collective-permute-start.19
  94.5 2.5 %collective-permute-start.24 = (bf16[512,256]{1,0:T(8,128)(2,1)S(1)}, bf16[512,256]{1,0:T(8,128)(2,1)S(1)}, u32[]{:S(2)}, u32[]{:S(2)}) collective-permute-start(bf16[512,256]{1,0:T(8,128)(2,1)S(1)} %get-tuple-element.93), channel_id=1, source_target_pairs={{0,16},{1,17},{2,18},{3,19},{4,20},{5,21},{6,22},{7,23},{8,24},{9,... | collective-permute-start | bytes 786440 | tf_op jit(solution)/shard_map/project/ppermute | solution.py:39
  97.3 0.8 collective-permute-done.24.refs_4_
  98.5 2.7 %project.5 = (bf16[8,32,768]{2,1,0:T(8,128)(2,1)S(1)}, bf16[8,32,768]{2,1,0:T(8,128)(2,1)S(1)}, bf16[8,32,768]{2,1,0:T(8,128)(2,1)S(1)}, bf16[8,32,768]{2,1,0:T(8,128)(2,1)S(1)}) custom-call(s32[4]{0:T(128)S(1)} %pad_add_fusion.at.refs_0_, bf16[1024,512]{1,0:T(8,128)(2,1)S(1)} %get-tuple-element.87.xt, ...), custom_call_target="tpu_custom_call" | custom-call | flops 1500000000 | bytes 4194304 | tf_op jit(solution)/shard_map/project/pallas_call | solution.py:47
  101.4 1.3 collective-permute-start.29
  102.7 3.1 %collective-permute-start.30 = (bf16[8,32,768]{2,1,0:T(8,128)(2,1)S(1)}, bf16[8,32,768]{2,1,0:T(8,128)(2,1)S(1)}, u32[]{:S(2)}, u32[]{:S(2)}) collective-permute-start(bf16[8,32,768]{2,1,0:T(8,128)(2,1)S(1)} %get-tuple-element.101), channel_id=1, source_target_pairs={{0,2},{1,3},{2,0},{3,1},{4,6},{5,7},{6,4},{7,5},{8,10},{9,11},{10,... | collective-permute-start | bytes 1179656 | tf_op jit(solution)/shard_map/project/partial_over_y/ppermute | solution.py:39
  106.1 2.8 %collective-permute-done.26.refs_1_.refs_8_ = bf16[1024,128]{1,0:T(8,128)(2,1)S(1)} collective-permute-done((bf16[1024,128]{1,0:T(8,128)(2,1)S(1)}, bf16[1024,128]{1,0:T(8,128)(2,1)S(1)}, u32[]{:S(2)}, u32[]{:S(2)}) %collective-permute-start.26) | collective-permute-done | bytes 262176 | tf_op jit(solution)/shard_map/partial_over_z/ppermute | solution.py:39
  108.9 5.3 %collective-permute-done.27.refs_2_.refs_9_ = bf16[1024,128]{1,0:T(8,128)(2,1)S(1)} collective-permute-done((bf16[1024,128]{1,0:T(8,128)(2,1)S(1)}, bf16[1024,128]{1,0:T(8,128)(2,1)S(1)}, u32[]{:S(2)}, u32[]{:S(2)}) %collective-permute-start.27) | collective-permute-done | bytes 262176 | tf_op jit(solution)/shard_map/partial_over_z/ppermute | solution.py:39
  114.2 6.8 %collective-permute-done.28.refs_3_.refs_10_ = bf16[1024,128]{1,0:T(8,128)(2,1)S(1)} collective-permute-done((bf16[1024,128]{1,0:T(8,128)(2,1)S(1)}, bf16[1024,128]{1,0:T(8,128)(2,1)S(1)}, u32[]{:S(2)}, u32[]{:S(2)}) %collective-permute-start.28) | collective-permute-done | bytes 262176 | tf_op jit(solution)/shard_map/partial_over_z/ppermute | solution.py:39
  120.9 2.1 %collective-permute-done.30.refs_6_ = bf16[8,32,768]{2,1,0:T(8,128)(2,1)S(1)} collective-permute-done((bf16[8,32,768]{2,1,0:T(8,128)(2,1)S(1)}, bf16[8,32,768]{2,1,0:T(8,128)(2,1)S(1)}, u32[]{:S(2)}, u32[]{:S(2)}) %collective-permute-start.30) | collective-permute-done | bytes 393248 | tf_op jit(solution)/shard_map/project/partial_over_y/ppermute | solution.py:39
  123.0 1.1 partial_over_z.3
  124.1 12.7 %all-to-all-start = ((bf16[8,32,1024]{2,1,0:T(8,128)(2,1)}), bf16[8,32,1024]{2,1,0:T(8,128)(2,1)S(1)}, u32[]{:S(2)}, u32[]{:S(2)}) async-start(bf16[8,32,1024]{2,1,0:T(8,128)(2,1)} %partial_over_z.3), calls=%async_computation | async-start | bytes 1048576 | tf_op jit(solution)/shard_map/partial_over_z/all_to_all | solution.py:362
  136.7 1.8 %grad_q.1 = bf16[128,4096]{1,0:T(8,128)(2,1)} custom-call(s32[4]{0:T(128)S(1)} %pad_add_fusion.at.refs_0_, bf16[1024,128]{1,0:T(8,128)(2,1)S(1)} %get-tuple-element.63.refs_3_.refs_0_, bf16[1024,128]{1,0:T(8,128)(2,1)S(1)} %collective-permute-done.26.refs_1_.refs_8_, bf16[1024,128]{1,0:T(8,128)(2,1)S(1)} %collective-permute-done.27.refs_2_.refs_9_, ...), custom_call_target="tpu_custom_call" | custom-call | bytes 2097152 | tf_op jit(solution)/shard_map/grad_q/pallas_call | solution.py:47
  138.5 14.6 %all-to-all-done.part = bf16[8,32,1024]{2,1,0:T(8,128)(2,1)S(1)} async-done(((bf16[8,32,1024]{2,1,0:T(8,128)(2,1)}), bf16[8,32,1024]{2,1,0:T(8,128)(2,1)S(1)}, u32[]{:S(2)}, u32[]{:S(2)}) %all-to-all-start) | async-done | bytes 524320 | tf_op jit(solution)/shard_map/partial_over_z/all_to_all | solution.py:362
  153.2 1.3 finish.1
  (49 shorter events, 3.9 us)
Async XLA Ops:
  0.7 0.9 copy-start.3
  1.6 0.9 copy-start.4
  3.2 9.3 %collective-permute-start = (bf16[128,256]{1,0:T(8,128)(2,1)S(1)}, bf16[128,256]{1,0:T(8,128)(2,1)S(1)}, u32[]{:S(2)}, u32[]{:S(2)}) collective-permute-start(bf16[128,256]{1,0:T(8,128)(2,1)S(1)} %get-tuple-element.54.refs_3_), channel_id=1, source_target_pairs={{0,4},{1,5},{2,6},{3,7},{4,8},{5,9},{6,10},{7,11},{8,12},{9,13},{1... | collective-permute-start | bytes 196616 | tf_op jit(solution)/shard_map/kv_over_x/ppermute | solution.py:39
  5.3 7.2 %collective-permute-start.1 = (bf16[128,256]{1,0:T(8,128)(2,1)S(1)}, bf16[128,256]{1,0:T(8,128)(2,1)S(1)}, u32[]{:S(2)}, u32[]{:S(2)}) collective-permute-start(bf16[128,256]{1,0:T(8,128)(2,1)S(1)} %get-tuple-element.59), channel_id=1, source_target_pairs={{0,8},{1,9},{2,10},{3,11},{4,12},{5,13},{6,14},{7,15},{8,0},{9,1},... | collective-permute-start | bytes 196616 | tf_op jit(solution)/shard_map/kv_over_x/ppermute | solution.py:39
  7.7 12.8 %copy-start = (bf16[128,8192]{1,0:T(8,128)(2,1)S(1)}, bf16[128,8192]{1,0:T(8,128)(2,1)}, u32[]{:S(2)}) copy-start(bf16[128,8192]{1,0:T(8,128)(2,1)} %refs_1_.3) | copy-start | bytes 6291460
  7.7 4.7 %collective-permute-start.2 = (bf16[128,256]{1,0:T(8,128)(2,1)S(1)}, bf16[128,256]{1,0:T(8,128)(2,1)S(1)}, u32[]{:S(2)}, u32[]{:S(2)}) collective-permute-start(bf16[128,256]{1,0:T(8,128)(2,1)S(1)} %get-tuple-element.60), channel_id=1, source_target_pairs={{0,12},{1,13},{2,14},{3,15},{4,0},{5,1},{6,2},{7,3},{8,4},{9,5},{1... | collective-permute-start | bytes 196616 | tf_op jit(solution)/shard_map/kv_over_x/ppermute | solution.py:39
  8.9 1.2 copy-start.1
  10.1 1.2 copy-start.2
  12.6 15.1 %copy-start.5 = (s32[1,8]{1,0:T(1,128)S(1)}, s32[1,8]{1,0:T(1,128)}, u32[]{:S(2)}) copy-start(s32[1,8]{1,0:T(1,128)} %param.11) | copy-start | bytes 100
  12.6 15.1 %collective-permute-start.3 = (bf16[2,1024,128]{2,1,0:T(8,128)(2,1)S(1)}, bf16[2,1024,128]{2,1,0:T(8,128)(2,1)S(1)}, u32[]{:S(2)}, u32[]{:S(2)}) collective-permute-start(bf16[2,1024,128]{2,1,0:T(8,128)(2,1)S(1)} %get-tuple-element.61.refs_5_), channel_id=1, source_target_pairs={{0,4},{1,5},{2,6},{3,7},{4,8},{5,9},{6,10},{7,11},{8,12},{9,13},{1... | collective-permute-start | bytes 1572872 | tf_op jit(solution)/shard_map/q_do_over_x/ppermute | solution.py:39
  13.5 8.1 %collective-permute-start.4 = (bf16[512,256]{1,0:T(8,128)(2,1)S(1)}, bf16[512,256]{1,0:T(8,128)(2,1)S(1)}, u32[]{:S(2)}, u32[]{:S(2)}) collective-permute-start(bf16[512,256]{1,0:T(8,128)(2,1)S(1)} %kv_over_x.3.refs_2_), channel_id=1, source_target_pairs={{0,1},{1,2},{2,3},{3,0},{4,5},{5,6},{6,7},{7,4},{8,9},{9,10},{10,1... | collective-permute-start | bytes 786440 | tf_op jit(solution)/shard_map/kv_over_y/ppermute | solution.py:39
  14.9 12.8 %collective-permute-start.5 = (bf16[512,256]{1,0:T(8,128)(2,1)S(1)}, bf16[512,256]{1,0:T(8,128)(2,1)S(1)}, u32[]{:S(2)}, u32[]{:S(2)}) collective-permute-start(bf16[512,256]{1,0:T(8,128)(2,1)S(1)} %kv_over_x.3.refs_2_), channel_id=1, source_target_pairs={{0,2},{1,3},{2,0},{3,1},{4,6},{5,7},{6,4},{7,5},{8,10},{9,11},{10,... | collective-permute-start | bytes 786440 | tf_op jit(solution)/shard_map/kv_over_y/ppermute | solution.py:39
  17.5 10.2 %collective-permute-start.6 = (bf16[512,256]{1,0:T(8,128)(2,1)S(1)}, bf16[512,256]{1,0:T(8,128)(2,1)S(1)}, u32[]{:S(2)}, u32[]{:S(2)}) collective-permute-start(bf16[512,256]{1,0:T(8,128)(2,1)S(1)} %kv_over_x.3.refs_2_), channel_id=1, source_target_pairs={{0,3},{1,0},{2,1},{3,2},{4,7},{5,4},{6,5},{7,6},{8,11},{9,8},{10,9... | collective-permute-start | bytes 786440 | tf_op jit(solution)/shard_map/kv_over_y/ppermute | solution.py:39
  18.6 16.5 %collective-permute-start.7 = (bf16[2,1024,128]{2,1,0:T(8,128)(2,1)S(1)}, bf16[2,1024,128]{2,1,0:T(8,128)(2,1)S(1)}, u32[]{:S(2)}, u32[]{:S(2)}) collective-permute-start(bf16[2,1024,128]{2,1,0:T(8,128)(2,1)S(1)} %get-tuple-element.65), channel_id=1, source_target_pairs={{0,8},{1,9},{2,10},{3,11},{4,12},{5,13},{6,14},{7,15},{8,0},{9,1},... | collective-permute-start | bytes 1572872 | tf_op jit(solution)/shard_map/q_do_over_x/ppermute | solution.py:39
  21.6 25.0 %collective-permute-start.8 = (bf16[2,1024,128]{2,1,0:T(8,128)(2,1)S(1)}, bf16[2,1024,128]{2,1,0:T(8,128)(2,1)S(1)}, u32[]{:S(2)}, u32[]{:S(2)}) collective-permute-start(bf16[2,1024,128]{2,1,0:T(8,128)(2,1)S(1)} %get-tuple-element.66), channel_id=1, source_target_pairs={{0,12},{1,13},{2,14},{3,15},{4,0},{5,1},{6,2},{7,3},{8,4},{9,5},{1... | collective-permute-start | bytes 1572872 | tf_op jit(solution)/shard_map/q_do_over_x/ppermute | solution.py:39
  35.2 17.6 %collective-permute-start.9 = (bf16[2,128,1024]{2,1,0:T(8,128)(2,1)S(1)}, bf16[2,128,1024]{2,1,0:T(8,128)(2,1)S(1)}, u32[]{:S(2)}, u32[]{:S(2)}) collective-permute-start(bf16[2,128,1024]{2,1,0:T(8,128)(2,1)S(1)} %get-tuple-element.75.refs_9_), channel_id=1, source_target_pairs={{0,4},{1,5},{2,6},{3,7},{4,8},{5,9},{6,10},{7,11},{8,12},{9,13},{1... | collective-permute-start | bytes 1572872 | tf_op jit(solution)/shard_map/attention/ppermute | solution.py:39
  35.3 20.5 %collective-permute-start.10 = (bf16[2,128,1024]{2,1,0:T(8,128)(2,1)S(1)}, bf16[2,128,1024]{2,1,0:T(8,128)(2,1)S(1)}, u32[]{:S(2)}, u32[]{:S(2)}) collective-permute-start(bf16[2,128,1024]{2,1,0:T(8,128)(2,1)S(1)} %get-tuple-element.79), channel_id=1, source_target_pairs={{0,8},{1,9},{2,10},{3,11},{4,12},{5,13},{6,14},{7,15},{8,0},{9,1},... | collective-permute-start | bytes 1572872 | tf_op jit(solution)/shard_map/attention/ppermute | solution.py:39
  37.6 28.3 %collective-permute-start.11 = (bf16[2,128,1024]{2,1,0:T(8,128)(2,1)S(1)}, bf16[2,128,1024]{2,1,0:T(8,128)(2,1)S(1)}, u32[]{:S(2)}, u32[]{:S(2)}) collective-permute-start(bf16[2,128,1024]{2,1,0:T(8,128)(2,1)S(1)} %get-tuple-element.80), channel_id=1, source_target_pairs={{0,12},{1,13},{2,14},{3,15},{4,0},{5,1},{6,2},{7,3},{8,4},{9,5},{1... | collective-permute-start | bytes 1572872 | tf_op jit(solution)/shard_map/attention/ppermute | solution.py:39
  52.9 13.1 %collective-permute-start.12 = (bf16[512,256]{1,0:T(8,128)(2,1)S(1)}, bf16[512,256]{1,0:T(8,128)(2,1)S(1)}, u32[]{:S(2)}, u32[]{:S(2)}) collective-permute-start(bf16[512,256]{1,0:T(8,128)(2,1)S(1)} %get-tuple-element.84), channel_id=1, source_target_pairs={{0,1},{1,2},{2,3},{3,0},{4,5},{5,6},{6,7},{7,4},{8,9},{9,10},{10,1... | collective-permute-start | bytes 786440 | tf_op jit(solution)/shard_map/terms_over_y/ppermute | solution.py:39
  53.3 12.7 %collective-permute-start.13 = (bf16[512,256]{1,0:T(8,128)(2,1)S(1)}, bf16[512,256]{1,0:T(8,128)(2,1)S(1)}, u32[]{:S(2)}, u32[]{:S(2)}) collective-permute-start(bf16[512,256]{1,0:T(8,128)(2,1)S(1)} %get-tuple-element.85), channel_id=1, source_target_pairs={{0,2},{1,3},{2,0},{3,1},{4,6},{5,7},{6,4},{7,5},{8,10},{9,11},{10,... | collective-permute-start | bytes 786440 | tf_op jit(solution)/shard_map/terms_over_y/ppermute | solution.py:39
  53.5 12.5 %collective-permute-start.14 = (bf16[512,256]{1,0:T(8,128)(2,1)S(1)}, bf16[512,256]{1,0:T(8,128)(2,1)S(1)}, u32[]{:S(2)}, u32[]{:S(2)}) collective-permute-start(bf16[512,256]{1,0:T(8,128)(2,1)S(1)} %get-tuple-element.86), channel_id=1, source_target_pairs={{0,3},{1,0},{2,1},{3,2},{4,7},{5,4},{6,5},{7,6},{8,11},{9,8},{10,9... | collective-permute-start | bytes 786440 | tf_op jit(solution)/shard_map/terms_over_y/ppermute | solution.py:39
  67.1 11.9 %collective-permute-start.15 = (bf16[1024,512]{1,0:T(8,128)(2,1)S(1)}, bf16[1024,512]{1,0:T(8,128)(2,1)S(1)}, u32[]{:S(2)}, u32[]{:S(2)}) collective-permute-start(bf16[1024,512]{1,0:T(8,128)(2,1)S(1)} %get-tuple-element.88), channel_id=1, source_target_pairs={{0,16},{1,17},{2,18},{3,19},{4,20},{5,21},{6,22},{7,23},{8,24},{9,... | collective-permute-start | bytes 3145736 | tf_op jit(solution)/shard_map/turn_x/ppermute | solution.py:39
  76.2 2.9 %collective-permute-start.20 = (bf16[512,256]{1,0:T(8,128)(2,1)S(1)}, bf16[512,256]{1,0:T(8,128)(2,1)S(1)}, u32[]{:S(2)}, u32[]{:S(2)}) collective-permute-start(bf16[512,256]{1,0:T(8,128)(2,1)S(1)} %add_convert_fusion.refs_0_), channel_id=1, source_target_pairs={{0,16},{1,17},{2,18},{3,19},{4,20},{5,21},{6,22},{7,23},{8,24},{9,... | collective-permute-start | bytes 786440 | tf_op jit(solution)/shard_map/dkv_over_x/ppermute | solution.py:39
  76.3 14.4 %collective-permute-start.16 = (bf16[512,256]{1,0:T(8,128)(2,1)S(1)}, bf16[512,256]{1,0:T(8,128)(2,1)S(1)}, u32[]{:S(2)}, u32[]{:S(2)}) collective-permute-start(bf16[512,256]{1,0:T(8,128)(2,1)S(1)} %add_convert_fusion.refs_0_), channel_id=1, source_target_pairs={{0,4},{1,5},{2,6},{3,7},{4,8},{5,9},{6,10},{7,11},{8,12},{9,13},{1... | collective-permute-start | bytes 786440 | tf_op jit(solution)/shard_map/dkv_over_x/ppermute | solution.py:39
  76.3 16.2 %collective-permute-start.17 = (bf16[512,256]{1,0:T(8,128)(2,1)S(1)}, bf16[512,256]{1,0:T(8,128)(2,1)S(1)}, u32[]{:S(2)}, u32[]{:S(2)}) collective-permute-start(bf16[512,256]{1,0:T(8,128)(2,1)S(1)} %add_convert_fusion.refs_0_), channel_id=1, source_target_pairs={{0,8},{1,9},{2,10},{3,11},{4,12},{5,13},{6,14},{7,15},{8,0},{9,1},... | collective-permute-start | bytes 786440 | tf_op jit(solution)/shard_map/dkv_over_x/ppermute | solution.py:39
  76.8 17.2 %collective-permute-start.18 = (bf16[512,256]{1,0:T(8,128)(2,1)S(1)}, bf16[512,256]{1,0:T(8,128)(2,1)S(1)}, u32[]{:S(2)}, u32[]{:S(2)}) collective-permute-start(bf16[512,256]{1,0:T(8,128)(2,1)S(1)} %add_convert_fusion.refs_0_), channel_id=1, source_target_pairs={{0,12},{1,13},{2,14},{3,15},{4,0},{5,1},{6,2},{7,3},{8,4},{9,5},{1... | collective-permute-start | bytes 786440 | tf_op jit(solution)/shard_map/dkv_over_x/ppermute | solution.py:39
  80.3 13.7 %collective-permute-start.21 = (bf16[8,32,256]{2,1,0:T(8,128)(2,1)S(1)}, bf16[8,32,256]{2,1,0:T(8,128)(2,1)S(1)}, u32[]{:S(2)}, u32[]{:S(2)}) collective-permute-start(bf16[8,32,256]{2,1,0:T(8,128)(2,1)S(1)} %get-tuple-element.90), channel_id=1, source_target_pairs={{0,1},{1,2},{2,3},{3,0},{4,5},{5,6},{6,7},{7,4},{8,9},{9,10},{10,1... | collective-permute-start | bytes 393224 | tf_op jit(solution)/shard_map/project/partial_over_y/ppermute | solution.py:39
  81.6 12.4 %collective-permute-start.22 = (bf16[8,32,256]{2,1,0:T(8,128)(2,1)S(1)}, bf16[8,32,256]{2,1,0:T(8,128)(2,1)S(1)}, u32[]{:S(2)}, u32[]{:S(2)}) collective-permute-start(bf16[8,32,256]{2,1,0:T(8,128)(2,1)S(1)} %get-tuple-element.91), channel_id=1, source_target_pairs={{0,2},{1,3},{2,0},{3,1},{4,6},{5,7},{6,4},{7,5},{8,10},{9,11},{10,... | collective-permute-start | bytes 393224 | tf_op jit(solution)/shard_map/project/partial_over_y/ppermute | solution.py:39
  90.6 3.8 %collective-permute-start.23 = (bf16[8,32,256]{2,1,0:T(8,128)(2,1)S(1)}, bf16[8,32,256]{2,1,0:T(8,128)(2,1)S(1)}, u32[]{:S(2)}, u32[]{:S(2)}) collective-permute-start(bf16[8,32,256]{2,1,0:T(8,128)(2,1)S(1)} %get-tuple-element.92), channel_id=1, source_target_pairs={{0,3},{1,0},{2,1},{3,2},{4,7},{5,4},{6,5},{7,6},{8,11},{9,8},{10,9... | collective-permute-start | bytes 393224 | tf_op jit(solution)/shard_map/project/partial_over_y/ppermute | solution.py:39
  92.5 4.8 %collective-permute-start.19 = (bf16[512,256]{1,0:T(8,128)(2,1)S(1)}, bf16[512,256]{1,0:T(8,128)(2,1)S(1)}, u32[]{:S(2)}, u32[]{:S(2)}) collective-permute-start(bf16[512,256]{1,0:T(8,128)(2,1)S(1)} %collective-permute-done.16.refs_0_), channel_id=1, source_target_pairs={{0,16},{1,17},{2,18},{3,19},{4,20},{5,21},{6,22},{7,23},{8,24},{9,... | collective-permute-start | bytes 786440 | tf_op jit(solution)/shard_map/dkv_over_x/ppermute | solution.py:39
  94.5 3.6 %collective-permute-start.24 = (bf16[512,256]{1,0:T(8,128)(2,1)S(1)}, bf16[512,256]{1,0:T(8,128)(2,1)S(1)}, u32[]{:S(2)}, u32[]{:S(2)}) collective-permute-start(bf16[512,256]{1,0:T(8,128)(2,1)S(1)} %get-tuple-element.93), channel_id=1, source_target_pairs={{0,16},{1,17},{2,18},{3,19},{4,20},{5,21},{6,22},{7,23},{8,24},{9,... | collective-permute-start | bytes 786440 | tf_op jit(solution)/shard_map/project/ppermute | solution.py:39
  97.0 1.5 collective-permute-start.25
  101.3 7.6 %collective-permute-start.26 = (bf16[1024,128]{1,0:T(8,128)(2,1)S(1)}, bf16[1024,128]{1,0:T(8,128)(2,1)S(1)}, u32[]{:S(2)}, u32[]{:S(2)}) collective-permute-start(bf16[1024,128]{1,0:T(8,128)(2,1)S(1)} %get-tuple-element.96), channel_id=1, source_target_pairs={{0,12},{1,13},{2,14},{3,15},{4,0},{5,1},{6,2},{7,3},{8,4},{9,5},{1... | collective-permute-start | bytes 786440 | tf_op jit(solution)/shard_map/partial_over_z/ppermute | solution.py:39
  101.4 19.6 %collective-permute-start.29 = (bf16[8,32,768]{2,1,0:T(8,128)(2,1)S(1)}, bf16[8,32,768]{2,1,0:T(8,128)(2,1)S(1)}, u32[]{:S(2)}, u32[]{:S(2)}) collective-permute-start(bf16[8,32,768]{2,1,0:T(8,128)(2,1)S(1)} %get-tuple-element.100), channel_id=1, source_target_pairs={{0,1},{1,2},{2,3},{3,0},{4,5},{5,6},{6,7},{7,4},{8,9},{9,10},{10,1... | collective-permute-start | bytes 1179656 | tf_op jit(solution)/shard_map/project/partial_over_y/ppermute | solution.py:39
  102.7 20.3 %collective-permute-start.30 = (bf16[8,32,768]{2,1,0:T(8,128)(2,1)S(1)}, bf16[8,32,768]{2,1,0:T(8,128)(2,1)S(1)}, u32[]{:S(2)}, u32[]{:S(2)}) collective-permute-start(bf16[8,32,768]{2,1,0:T(8,128)(2,1)S(1)} %get-tuple-element.101), channel_id=1, source_target_pairs={{0,2},{1,3},{2,0},{3,1},{4,6},{5,7},{6,4},{7,5},{8,10},{9,11},{10,... | collective-permute-start | bytes 1179656 | tf_op jit(solution)/shard_map/project/partial_over_y/ppermute | solution.py:39
  105.7 17.3 %collective-permute-start.31 = (bf16[8,32,768]{2,1,0:T(8,128)(2,1)S(1)}, bf16[8,32,768]{2,1,0:T(8,128)(2,1)S(1)}, u32[]{:S(2)}, u32[]{:S(2)}) collective-permute-start(bf16[8,32,768]{2,1,0:T(8,128)(2,1)S(1)} %get-tuple-element.102), channel_id=1, source_target_pairs={{0,3},{1,0},{2,1},{3,2},{4,7},{5,4},{6,5},{7,6},{8,11},{9,8},{10,9... | collective-permute-start | bytes 1179656 | tf_op jit(solution)/shard_map/project/partial_over_y/ppermute | solution.py:39
  106.1 8.1 %collective-permute-start.27 = (bf16[1024,128]{1,0:T(8,128)(2,1)S(1)}, bf16[1024,128]{1,0:T(8,128)(2,1)S(1)}, u32[]{:S(2)}, u32[]{:S(2)}) collective-permute-start(bf16[1024,128]{1,0:T(8,128)(2,1)S(1)} %get-tuple-element.97), channel_id=1, source_target_pairs={{0,8},{1,9},{2,10},{3,11},{4,12},{5,13},{6,14},{7,15},{8,0},{9,1},... | collective-permute-start | bytes 786440 | tf_op jit(solution)/shard_map/partial_over_z/ppermute | solution.py:39
  108.9 12.1 %collective-permute-start.28 = (bf16[1024,128]{1,0:T(8,128)(2,1)S(1)}, bf16[1024,128]{1,0:T(8,128)(2,1)S(1)}, u32[]{:S(2)}, u32[]{:S(2)}) collective-permute-start(bf16[1024,128]{1,0:T(8,128)(2,1)S(1)} %get-tuple-element.98), channel_id=1, source_target_pairs={{0,4},{1,5},{2,6},{3,7},{4,8},{5,9},{6,10},{7,11},{8,12},{9,13},{1... | collective-permute-start | bytes 786440 | tf_op jit(solution)/shard_map/partial_over_z/ppermute | solution.py:39
  124.1 29.1 %all-to-all-start = ((bf16[8,32,1024]{2,1,0:T(8,128)(2,1)}), bf16[8,32,1024]{2,1,0:T(8,128)(2,1)S(1)}, u32[]{:S(2)}, u32[]{:S(2)}) async-start(bf16[8,32,1024]{2,1,0:T(8,128)(2,1)} %partial_over_z.3), calls=%async_computation | async-start | bytes 1048576 | tf_op jit(solution)/shard_map/partial_over_z/all_to_all | solution.py:362

commit v3 on v2

--- a/solution.py
+++ b/solution.py
@@ -100,16 +100,17 @@
                 outs[d][rows, pl.ds(spot, BLK)] = refs[s][d, :, z * BLK : (z + 1) * BLK].T
 
 
-def attention_kernel(first_piece, at, lens, *refs):
+def attention_kernel(pieces, at, lens, *refs):
     x, y = at[0], at[1]
     group = HQ // HK
     rows_n = group * BLK
     chunks = [slice(i * KB, (i + 1) * KB) for i in range(rows_n // KB)]
     nt = (((1,), (1,)), ((), ()))
-    qd_in, refs = refs[0:2], refs[2:]
-    if first_piece == 0:
-        kv_in, dq_out = refs[0:4], refs[4:6]
-        dk, dv, k_all, v_all, kt_all, qd, s_all, dp_all, pb, dsb, dqt, dq_all = refs[6:]
+    n = len(pieces)
+    qd_in, refs = refs[0:n], refs[n:]
+    if n == 3:
+        kv_in, dq_out = refs[0:4], refs[4:7]
+        dk, dv, k_all, v_all, kt_all, qd, s_all, dp_all, pb, dsb, dqt, dq_all = refs[7:]
         for s in range(NY):
             for t in range(NX):
                 blk = NY * lax.rem(x - t + NX, NX) + lax.rem(y - s + NY, NY)
@@ -122,23 +123,24 @@
         dv[...] = jnp.zeros_like(dv)
     else:
         dk_in, dv_in, k_all, v_all, kt_all = refs[0:5]
-        dq_out, r_out = refs[5:7], refs[7:11]
-        qd, s_all, dp_all, pb, dsb, dqt, dq_all, dk, dv = refs[11:]
+        dq_out, r_out = refs[5:6], refs[6:10]
+        qd, s_all, dp_all, pb, dsb, dqt, dq_all, dk, dv = refs[10:]
         dk[...] = dk_in[...]
         dv[...] = dv_in[...]
-    for s in range(2):
-        qd[s] = qd_in[s][...]
+    for i in range(n):
+        qd[i] = qd_in[i][...]
 
     def fold(value, op):
         return op(value.reshape(KB // 8, 8, KB), axis=0)
 
     def query_block(j, carry):
-        base = (NY * lax.rem(x - j - first_piece + NX, NX) + y) * BLK
+        shift = j + lax.div(j, 2) if n == 3 else pieces[0]
+        base = (NY * lax.rem(x - shift + NX, NX) + y) * BLK
         q_pos = base + (lax.broadcasted_iota(jnp.int32, (1, KB), 1) & (BLK - 1))
         start = jnp.zeros((1, KB), jnp.int32)
         first, run = jnp.int32(0), jnp.int32(0)
-        for n in range(8):
-            run = run + lens[n]
+        for doc in range(8):
+            run = run + lens[doc]
             start = jnp.maximum(start, jnp.where(q_pos >= run, run, 0))
             first = jnp.maximum(first, jnp.where(base >= run, run, 0))
         lo, hi = lax.div(first, KB), lax.div(base, KB) + 1
@@ -194,10 +196,10 @@
             dq_all[j, head, :] = (dqt[:, head].T * SCALE).astype(BF)
         return carry
 
-    lax.fori_loop(0, 2, query_block, 0)
-    for s in range(2):
-        dq_out[s][...] = dq_all[s]
-    if first_piece == 0:
+    lax.fori_loop(0, n, query_block, 0)
+    for i in range(n):
+        dq_out[i][...] = dq_all[i]
+    if n == 3:
         return
     for s in range(NY):
         for t in range(NX):
@@ -264,11 +266,11 @@
     return list(values[:n]), list(values[n:])
 
 
-def total(values):
-    acc = values[0].astype(F32)
-    for value in values[1:]:
-        acc = acc + value.astype(F32)
-    return acc.astype(BF)
+def sum_kernel(*refs):
+    acc = refs[0][...].astype(F32)
+    for ref in refs[1:NY]:
+        acc = acc + ref[...].astype(F32)
+    refs[-1][...] = acc.astype(BF)
 
 
 def on_device(layer_input, queries, key_rows, value_rows, d_out, doc_lengths):
@@ -290,57 +292,60 @@
         kv = [kv] + [send(kv, dy=s) for s in range(1, NY)]
     with jax.named_scope("attention"):
         held = [sds((2048, HD), F32)] * 2 + [sds((2048, HD))] * 2 + [sds((8, HD, KB))]
-        scratch = [
-            pltpu.VMEM((2, 2, 1024, HD), BF),
-            pltpu.VMEM((MAX_KB, KB, 1024), F32),
-            pltpu.VMEM((MAX_KB, KB, 1024), F32),
-            pltpu.VMEM((KB, 1024), BF),
-            pltpu.VMEM((KB, 1024), BF),
-            pltpu.VMEM((HD, 1024), F32),
-            pltpu.VMEM((2, 1024, HD), BF),
-        ]
-        dq_a, held = split(
-            2,
+        def scratch(n):
+            return [
+                pltpu.VMEM((n, 2, 1024, HD), BF),
+                pltpu.VMEM((MAX_KB, KB, 1024), F32),
+                pltpu.VMEM((MAX_KB, KB, 1024), F32),
+                pltpu.VMEM((KB, 1024), BF),
+                pltpu.VMEM((KB, 1024), BF),
+                pltpu.VMEM((HD, 1024), F32),
+                pltpu.VMEM((n, 1024, HD), BF),
+            ]
+
+        (dq0, dq1, dq3), held = split(
+            3,
             call(
-                functools.partial(attention_kernel, 0),
-                [sds((1024, HD))] * 2 + held,
-                (at, doc_lengths[0], *qd[:2], *kv),
-                scratch=scratch,
-                flops=8 * 10**9,
+                functools.partial(attention_kernel, (0, 1, 3)),
+                [sds((1024, HD))] * 3 + held,
+                (at, doc_lengths[0], qd[0], qd[1], qd[3], *kv),
+                scratch=scratch(3),
+                flops=12 * 10**9,
                 moved=6 << 20,
                 limit=32,
                 smem=2,
             ),
         )
-        give = after(xp[1:], [dq_a[0], qd[2]])
-        xp = [xp[0]] + [send(d, dx=s + 1) for s, d in enumerate(give)]
-        dq_b, terms = split(
-            2,
+        (dq2,), terms = split(
+            1,
             call(
-                functools.partial(attention_kernel, 2),
-                [sds((1024, HD))] * 2 + [sds((512, 256))] * 4,
-                (at, doc_lengths[0], *qd[2:], *held),
-                scratch=scratch + [pltpu.VMEM((2048, HD), F32)] * 2,
-                flops=8 * 10**9,
+                functools.partial(attention_kernel, (2,)),
+                [sds((1024, HD))] + [sds((512, 256))] * 4,
+                (at, doc_lengths[0], qd[2], *held),
+                scratch=scratch(1) + [pltpu.VMEM((2048, HD), F32)] * 2,
+                flops=4 * 10**9,
                 moved=6 << 20,
                 limit=32,
                 smem=2,
-                late=give[:1],
             ),
         )
-    dq = dq_a + dq_b
+    dq = [dq0, dq1, dq2, dq3]
     with jax.named_scope("terms_over_y"):
-        terms = [terms[0]] + [send(d, dy=s + 1) for s, d in enumerate(after(terms[1:], [xp[1]]))]
-        dkv = total(terms)
-    with jax.named_scope("turn_x"):
-        xt, xt_give = call(turn_x_kernel, [sds((1024, 512))] * 2, (at, *xp), moved=1 << 22, late=terms[1:])
-        xt_other = send(xt_give, dc=1)
+        give = after(xp[1:], terms[:1])
+        terms = [terms[0]] + [send(terms[s], dy=s) for s in range(1, NY)]
+        xp = [xp[0]] + [send(d, dx=s + 1) for s, d in enumerate(give)]
+        (dkv,) = call(sum_kernel, [sds((512, 256))], terms, moved=5 << 18, smem=0, late=[xp[1]])
     with jax.named_scope("dkv_over_x"):
         own = [dkv] + [send(dkv, dx=s) for s in range(1, NX)]
-        other = [send(piece, dc=1) for piece in own[:2]]
+        other = [send(piece, dc=1) for piece in own]
+    with jax.named_scope("turn_x"):
+        xt, xt_give = call(turn_x_kernel, [sds((1024, 512))] * 2, (at, *xp), moved=1 << 22, late=own[1:])
+        xt_other = send(xt_give, dc=1)
+    with jax.named_scope("grad_q"):
+        dq = [dq[0]] + [send(d, dx=-s - 1) for s, d in enumerate(after(dq[1:], own[1:]))]
     with jax.named_scope("project"):
         parts = []
-        for pick in (slice(0, 1), slice(1, 4)):
+        for pick in (slice(0, 2), slice(2, 4)):
             n = pick.stop - pick.start
             partial = call(
                 functools.partial(project_kernel, n),
@@ -349,15 +354,12 @@
                 scratch=[pltpu.VMEM((1024, 256), F32)],
                 flops=n * 5 * 10**8,
                 moved=1 << 22,
-
+                late=parts[:1] + dq[1:] if parts else [],
             )
             with jax.named_scope("partial_over_y"):
                 parts += [partial[0]] + [send(partial[s], dy=s) for s in range(1, NY)]
-            if len(other) == 2:
-                other += [send(piece, dc=1) for piece in after(own[2:], parts[1:])]
     with jax.named_scope("partial_over_z"):
-        dq = [dq[0]] + [send(d, dx=-s - 1) for s, d in enumerate(after(dq[1:], [parts[4]]))]
-        (summed,) = call(add_kernel, [sds((NZ, 32, 1024))], parts, moved=5 << 20, smem=0, late=dq[1:])
+        (summed,) = call(add_kernel, [sds((NZ, 32, 1024))], parts, moved=5 << 20, smem=0)
         groups = [[z * NC + c for z in range(NZ)] for c in range(NC)]
         last = lax.all_to_all(summed, "dp", 0, 0, axis_index_groups=groups, tiled=True)
     with jax.named_scope("grad_q"):

time: 154 us -> 159 us (1.032); the launches traced: 154 us -> 157 us
  starting transfers between devices: 60.7 us -> 63.6 us
    ppermute x32, starting transfers between devices: 48 us -> 51 us  [send(): return lax.ppermute(value, AXES, pairs)]
    pallas_call x17 -> x16, Pallas kernels: 24.1 us -> 24.2 us  [call(): pl.pallas_call(body, out_shape=outs, in_specs=[SM] * smem + [VM] * (len(i...]
  transfers between devices with their start and end apart: 33 -> 33, of which waited for: 13 -> 16; matrix products, arithmetic and copies ran while one was open for 0% -> 0% of each run, Pallas kernels for 11% -> 11%
where the time goes in v3:
time: 159 us; the launch traced here: 157 us
  waiting for transfers between devices  64 us (40%)
  starting transfers between devices  63.6 us (40%)
  Pallas kernels  24.2 us (15%)
  local copies, waits for them, and re-layouts  4.3 us (3%)
    ppermute x32, starting transfers between devices, send(): return lax.ppermute(value, AXES, pairs)  51 us
    ppermute x32, waiting for transfers between devices, send(): return lax.ppermute(value, AXES, pairs)  50.1 us
    pallas_call x16, Pallas kernels, call(): pl.pallas_call(body, out_shape=outs, in_specs=[SM] * smem + [VM] * (len(i...  24.2 us
    all_to_all x1, waiting for transfers between devices, on_device(): lax.all_to_all(summed, 'dp', 0, 0, axis_index_groups=groups, tiled=True)  13.9 us
    all_to_all x1, starting transfers between devices, on_device(): lax.all_to_all(summed, 'dp', 0, 0, axis_index_groups=groups, tiled=True)  12.6 us
    unnamed x12, local copies, waits for them, and re-layouts  4.3 us
  transfers between devices with their start and end apart: 33, of which 16 were waited for; matrix products, arithmetic and copies ran while one was open for 0% of the time, Pallas kernels for 11%

profile of v3, /device:TPU:1, one launch (start us, length us, event | category | flops | bytes accessed | tf_op | source)
XLA Modules:
  0.0 157.1 jit_solution(13557003511996448936)
XLA Ops:
  0.7 0.9 copy-done.3
  1.7 0.9 copy-done.4
  3.2 3.7 %collective-permute-start.1 = (bf16[128,256]{1,0:T(8,128)(2,1)S(1)}, bf16[128,256]{1,0:T(8,128)(2,1)S(1)}, u32[]{:S(2)}, u32[]{:S(2)}) collective-permute-start(bf16[128,256]{1,0:T(8,128)(2,1)S(1)} %get-tuple-element.54), channel_id=1, source_target_pairs={{0,8},{1,9},{2,10},{3,11},{4,12},{5,13},{6,14},{7,15},{8,0},{9,1},... | collective-permute-start | bytes 196616 | tf_op jit(solution)/shard_map/kv_over_x/ppermute | solution.py:39
  6.8 0.9 collective-permute-start.2
  7.7 0.6 collective-permute-start
  8.3 1.3 copy-done.1
  9.5 1.2 copy-done.2
  10.8 1.1 pack_q_do.1
  12.4 1.8 %collective-permute-start.4 = (bf16[2,1024,128]{2,1,0:T(8,128)(2,1)S(1)}, bf16[2,1024,128]{2,1,0:T(8,128)(2,1)S(1)}, u32[]{:S(2)}, u32[]{:S(2)}) collective-permute-start(bf16[2,1024,128]{2,1,0:T(8,128)(2,1)S(1)} %get-tuple-element.57), channel_id=1, source_target_pairs={{0,12},{1,13},{2,14},{3,15},{4,0},{5,1},{6,2},{7,3},{8,4},{9,5},{1... | collective-permute-start | bytes 1572872 | tf_op jit(solution)/shard_map/q_do_over_x/ppermute | solution.py:39
  14.7 2.8 %collective-permute-start.7 = (bf16[512,256]{1,0:T(8,128)(2,1)S(1)}, bf16[512,256]{1,0:T(8,128)(2,1)S(1)}, u32[]{:S(2)}, u32[]{:S(2)}) collective-permute-start(bf16[512,256]{1,0:T(8,128)(2,1)S(1)} %kv_over_x.3.refs_3_.refs_2_), channel_id=1, source_target_pairs={{0,3},{1,0},{2,1},{3,2},{4,7},{5,4},{6,5},{7,6},{8,11},{9,8},{10,9... | collective-permute-start | bytes 786440 | tf_op jit(solution)/shard_map/kv_over_y/ppermute | solution.py:39
  17.9 0.7 collective-permute-start.5
  18.6 1.1 pack_x.1
  19.7 3.9 %collective-permute-done.7.refs_6_ = bf16[512,256]{1,0:T(8,128)(2,1)S(1)} collective-permute-done((bf16[512,256]{1,0:T(8,128)(2,1)S(1)}, bf16[512,256]{1,0:T(8,128)(2,1)S(1)}, u32[]{:S(2)}, u32[]{:S(2)}) %collective-permute-start.7) | collective-permute-done | bytes 262176 | tf_op jit(solution)/shard_map/kv_over_y/ppermute | solution.py:39
  23.6 1.3 collective-permute-start.8
  24.9 7.4 %collective-permute-done.5.refs_4_ = bf16[512,256]{1,0:T(8,128)(2,1)S(1)} collective-permute-done((bf16[512,256]{1,0:T(8,128)(2,1)S(1)}, bf16[512,256]{1,0:T(8,128)(2,1)S(1)}, u32[]{:S(2)}, u32[]{:S(2)}) %collective-permute-start.5) | collective-permute-done | bytes 262176 | tf_op jit(solution)/shard_map/kv_over_y/ppermute | solution.py:39
  32.3 8.9 %attention.2 = (bf16[1024,128]{1,0:T(8,128)(2,1)S(1)}, bf16[1024,128]{1,0:T(8,128)(2,1)S(1)}, bf16[1024,128]{1,0:T(8,128)(2,1)S(1)}, f32[2048,128]{1,0:T(8,128)S...) custom-call(s32[4]{0:T(128)S(1)} %pad_add_fusion.at.refs_0_, ...), custom_call_target="tpu_custom_call" | custom-call | flops 12000000000 | bytes 6291456 | tf_op jit(solution)/shard_map/attention/pallas_call | solution.py:47
  41.2 2.3 %attention.3 = (bf16[1024,128]{1,0:T(8,128)(2,1)S(1)}, bf16[512,256]{1,0:T(8,128)(2,1)S(1)}, bf16[512,256]{1,0:T(8,128)(2,1)S(1)}, bf16[512,256]{1,0:T(8,128)(2,1)S(1)}, bf16[512,256]{1,0:T(8,128)(2,1)S(1)}) custom-call(s32[4]{0:T(128)S(1)} %pad_add_fusion.at.refs_0_, s32[8]{0:T(128)S(1)} %bitcast.6, ...), custom_call_target="tpu_custom_call" | custom-call | flops 4000000000 | bytes 6291456 | tf_op jit(solution)/shard_map/attention/pallas_call | solution.py:47
  43.9 3.3 %collective-permute-start.10 = (bf16[512,256]{1,0:T(8,128)(2,1)S(1)}, bf16[512,256]{1,0:T(8,128)(2,1)S(1)}, u32[]{:S(2)}, u32[]{:S(2)}) collective-permute-start(bf16[512,256]{1,0:T(8,128)(2,1)S(1)} %get-tuple-element.71), channel_id=1, source_target_pairs={{0,2},{1,3},{2,0},{3,1},{4,6},{5,7},{6,4},{7,5},{8,10},{9,11},{10,... | collective-permute-start | bytes 786440 | tf_op jit(solution)/shard_map/terms_over_y/ppermute | solution.py:39
  47.3 2.1 %collective-permute-start.11 = (bf16[512,256]{1,0:T(8,128)(2,1)S(1)}, bf16[512,256]{1,0:T(8,128)(2,1)S(1)}, u32[]{:S(2)}, u32[]{:S(2)}) collective-permute-start(bf16[512,256]{1,0:T(8,128)(2,1)S(1)} %get-tuple-element.72), channel_id=1, source_target_pairs={{0,3},{1,0},{2,1},{3,2},{4,7},{5,4},{6,5},{7,6},{8,11},{9,8},{10,9... | collective-permute-start | bytes 786440 | tf_op jit(solution)/shard_map/terms_over_y/ppermute | solution.py:39
  49.3 4.2 %collective-permute-start.19 = (bf16[2,128,1024]{2,1,0:T(8,128)(2,1)S(1)}, bf16[2,128,1024]{2,1,0:T(8,128)(2,1)S(1)}, u32[]{:S(2)}, u32[]{:S(2)}) collective-permute-start(bf16[2,128,1024]{2,1,0:T(8,128)(2,1)S(1)} %get-tuple-element.81), channel_id=1, source_target_pairs={{0,8},{1,9},{2,10},{3,11},{4,12},{5,13},{6,14},{7,15},{8,0},{9,1},... | collective-permute-start | bytes 1572872 | tf_op jit(solution)/shard_map/terms_over_y/ppermute | solution.py:39
  54.0 3.5 %collective-permute-start.15 = (bf16[512,256]{1,0:T(8,128)(2,1)S(1)}, bf16[512,256]{1,0:T(8,128)(2,1)S(1)}, u32[]{:S(2)}, u32[]{:S(2)}) collective-permute-start(bf16[512,256]{1,0:T(8,128)(2,1)S(1)} %terms_over_y.3.refs_0_), channel_id=1, source_target_pairs={{0,12},{1,13},{2,14},{3,15},{4,0},{5,1},{6,2},{7,3},{8,4},{9,5},{1... | collective-permute-start | bytes 786440 | tf_op jit(solution)/shard_map/dkv_over_x/ppermute | solution.py:39
  57.5 3.6 %collective-permute-start.14 = (bf16[512,256]{1,0:T(8,128)(2,1)S(1)}, bf16[512,256]{1,0:T(8,128)(2,1)S(1)}, u32[]{:S(2)}, u32[]{:S(2)}) collective-permute-start(bf16[512,256]{1,0:T(8,128)(2,1)S(1)} %terms_over_y.3.refs_0_), channel_id=1, source_target_pairs={{0,8},{1,9},{2,10},{3,11},{4,12},{5,13},{6,14},{7,15},{8,0},{9,1},... | collective-permute-start | bytes 786440 | tf_op jit(solution)/shard_map/dkv_over_x/ppermute | solution.py:39
  61.1 0.6 collective-permute-start.13
  61.7 2.7 %collective-permute-done.19.refs_3_ = bf16[2,128,1024]{2,1,0:T(8,128)(2,1)S(1)} collective-permute-done((bf16[2,128,1024]{2,1,0:T(8,128)(2,1)S(1)}, bf16[2,128,1024]{2,1,0:T(8,128)(2,1)S(1)}, u32[]{:S(2)}, u32[]{:S(2)}) %collective-permute-start.19) | collective-permute-done | bytes 524320 | tf_op jit(solution)/shard_map/terms_over_y/ppermute | solution.py:39
  64.4 1.1 collective-permute-done.20.refs_4_
  65.5 11.5 %collective-permute-done.15.refs_5_.refs_7_.refs_4_ = bf16[512,256]{1,0:T(8,128)(2,1)S(1)} collective-permute-done((bf16[512,256]{1,0:T(8,128)(2,1)S(1)}, bf16[512,256]{1,0:T(8,128)(2,1)S(1)}, u32[]{:S(2)}, u32[]{:S(2)}) %collective-permute-start.15) | collective-permute-done | bytes 262176 | tf_op jit(solution)/shard_map/dkv_over_x/ppermute | solution.py:39
  77.0 1.0 collective-permute-done.13.refs_3_.refs_5_.refs_1_
  78.0 1.1 turn_x.1
  79.1 11.3 %collective-permute-start.21 = (bf16[1024,512]{1,0:T(8,128)(2,1)S(1)}, bf16[1024,512]{1,0:T(8,128)(2,1)S(1)}, u32[]{:S(2)}, u32[]{:S(2)}) collective-permute-start(bf16[1024,512]{1,0:T(8,128)(2,1)S(1)} %get-tuple-element.84), channel_id=1, source_target_pairs={{0,16},{1,17},{2,18},{3,19},{4,20},{5,21},{6,22},{7,23},{8,24},{9,... | collective-permute-start | bytes 3145736 | tf_op jit(solution)/shard_map/turn_x/ppermute | solution.py:39
  91.5 1.6 %collective-permute-done.22.refs_2_ = bf16[512,256]{1,0:T(8,128)(2,1)S(1)} collective-permute-done((bf16[512,256]{1,0:T(8,128)(2,1)S(1)}, bf16[512,256]{1,0:T(8,128)(2,1)S(1)}, u32[]{:S(2)}, u32[]{:S(2)}) %collective-permute-start.22) | collective-permute-done | bytes 262176 | tf_op jit(solution)/shard_map/dkv_over_x/ppermute | solution.py:39
  93.1 1.6 %collective-permute-start.16 = (bf16[1024,128]{1,0:T(8,128)(2,1)S(1)}, bf16[1024,128]{1,0:T(8,128)(2,1)S(1)}, u32[]{:S(2)}, u32[]{:S(2)}) collective-permute-start(bf16[1024,128]{1,0:T(8,128)(2,1)S(1)} %get-tuple-element.77), channel_id=1, source_target_pairs={{0,12},{1,13},{2,14},{3,15},{4,0},{5,1},{6,2},{7,3},{8,4},{9,5},{1... | collective-permute-start | bytes 786440 | tf_op jit(solution)/shard_map/grad_q/ppermute | solution.py:39
  94.9 0.8 collective-permute-start.18
  95.6 2.0 %project.2 = (bf16[8,32,512]{2,1,0:T(8,128)(2,1)S(1)}, bf16[8,32,512]{2,1,0:T(8,128)(2,1)S(1)}, bf16[8,32,512]{2,1,0:T(8,128)(2,1)S(1)}, bf16[8,32,512]{2,1,0:T(8,128)(2,1)S(1)}) custom-call(s32[4]{0:T(128)S(1)} %pad_add_fusion.at.refs_0_, bf16[1024,512]{1,0:T(8,128)(2,1)S(1)} %get-tuple-element.83.xt.refs_1_, ...), custom_call_target="tpu_custom_call" | custom-call | flops 1000000000 | bytes 4194304 | tf_op jit(solution)/shard_map/project/pallas_call | solution.py:47
  98.0 1.9 %collective-permute-start.25 = (bf16[8,32,512]{2,1,0:T(8,128)(2,1)S(1)}, bf16[8,32,512]{2,1,0:T(8,128)(2,1)S(1)}, u32[]{:S(2)}, u32[]{:S(2)}) collective-permute-start(bf16[8,32,512]{2,1,0:T(8,128)(2,1)S(1)} %get-tuple-element.87), channel_id=1, source_target_pairs={{0,2},{1,3},{2,0},{3,1},{4,6},{5,7},{6,4},{7,5},{8,10},{9,11},{10,... | collective-permute-start | bytes 786440 | tf_op jit(solution)/shard_map/project/partial_over_y/ppermute | solution.py:39
  99.9 0.7 collective-permute-done.16.refs_1_.refs_8_
  100.6 1.5 collective-permute-start.26
  102.1 1.3 collective-permute-done.17.refs_2_.refs_9_
  103.5 6.4 %collective-permute-done.18.refs_3_.refs_10_ = bf16[1024,128]{1,0:T(8,128)(2,1)S(1)} collective-permute-done((bf16[1024,128]{1,0:T(8,128)(2,1)S(1)}, bf16[1024,128]{1,0:T(8,128)(2,1)S(1)}, u32[]{:S(2)}, u32[]{:S(2)}) %collective-permute-start.18) | collective-permute-done | bytes 262176 | tf_op jit(solution)/shard_map/grad_q/ppermute | solution.py:39
  109.8 2.0 %project.3 = (bf16[8,32,512]{2,1,0:T(8,128)(2,1)S(1)}, bf16[8,32,512]{2,1,0:T(8,128)(2,1)S(1)}, bf16[8,32,512]{2,1,0:T(8,128)(2,1)S(1)}, bf16[8,32,512]{2,1,0:T(8,128)(2,1)S(1)}) custom-call(s32[4]{0:T(128)S(1)} %pad_add_fusion.at.refs_0_, bf16[1024,512]{1,0:T(8,128)(2,1)S(1)} %get-tuple-element.83.xt.refs_1_, ...), custom_call_target="tpu_custom_call" | custom-call | flops 1000000000 | bytes 4194304 | tf_op jit(solution)/shard_map/project/pallas_call | solution.py:47
  112.0 2.1 %collective-permute-start.30 = (bf16[8,32,512]{2,1,0:T(8,128)(2,1)S(1)}, bf16[8,32,512]{2,1,0:T(8,128)(2,1)S(1)}, u32[]{:S(2)}, u32[]{:S(2)}) collective-permute-start(bf16[8,32,512]{2,1,0:T(8,128)(2,1)S(1)} %get-tuple-element.91), channel_id=1, source_target_pairs={{0,2},{1,3},{2,0},{3,1},{4,6},{5,7},{6,4},{7,5},{8,10},{9,11},{10,... | collective-permute-start | bytes 786440 | tf_op jit(solution)/shard_map/project/partial_over_y/ppermute | solution.py:39
  114.6 6.2 %collective-permute-done.29.refs_5_ = bf16[8,32,512]{2,1,0:T(8,128)(2,1)S(1)} collective-permute-done((bf16[8,32,512]{2,1,0:T(8,128)(2,1)S(1)}, bf16[8,32,512]{2,1,0:T(8,128)(2,1)S(1)}, u32[]{:S(2)}, u32[]{:S(2)}) %collective-permute-start.29) | collective-permute-done | bytes 262176 | tf_op jit(solution)/shard_map/project/partial_over_y/ppermute | solution.py:39
  120.9 4.8 %collective-permute-done.30.refs_6_ = bf16[8,32,512]{2,1,0:T(8,128)(2,1)S(1)} collective-permute-done((bf16[8,32,512]{2,1,0:T(8,128)(2,1)S(1)}, bf16[8,32,512]{2,1,0:T(8,128)(2,1)S(1)}, u32[]{:S(2)}, u32[]{:S(2)}) %collective-permute-start.30) | collective-permute-done | bytes 262176 | tf_op jit(solution)/shard_map/project/partial_over_y/ppermute | solution.py:39
  125.6 0.8 collective-permute-done.31.refs_7_
  126.4 1.1 partial_over_z.1
  127.5 12.6 %all-to-all-start = ((bf16[8,32,1024]{2,1,0:T(8,128)(2,1)}), bf16[8,32,1024]{2,1,0:T(8,128)(2,1)S(1)}, u32[]{:S(2)}, u32[]{:S(2)}) async-start(bf16[8,32,1024]{2,1,0:T(8,128)(2,1)} %partial_over_z.1), calls=%async_computation | async-start | bytes 1048576 | tf_op jit(solution)/shard_map/partial_over_z/all_to_all | solution.py:364
  140.1 1.8 %grad_q.3 = bf16[128,4096]{1,0:T(8,128)(2,1)} custom-call(s32[4]{0:T(128)S(1)} %pad_add_fusion.at.refs_0_, bf16[1024,128]{1,0:T(8,128)(2,1)S(1)} %get-tuple-element.59.refs_0_, bf16[1024,128]{1,0:T(8,128)(2,1)S(1)} %collective-permute-done.16.refs_1_.refs_8_, bf16[1024,128]{1,0:T(8,128)(2,1)S(1)} %collective-permute-done.17.refs_2_.refs_9_, ...), custom_call_target="tpu_custom_call" | custom-call | bytes 2097152 | tf_op jit(solution)/shard_map/grad_q/pallas_call | solution.py:47
  141.9 13.9 %all-to-all-done.part = bf16[8,32,1024]{2,1,0:T(8,128)(2,1)S(1)} async-done(((bf16[8,32,1024]{2,1,0:T(8,128)(2,1)}), bf16[8,32,1024]{2,1,0:T(8,128)(2,1)S(1)}, u32[]{:S(2)}, u32[]{:S(2)}) %all-to-all-start) | async-done | bytes 524320 | tf_op jit(solution)/shard_map/partial_over_z/all_to_all | solution.py:364
  155.8 1.3 finish.1
  (47 shorter events, 5.3 us)
Async XLA Ops:
  0.7 0.9 copy-start.3
  1.6 0.9 copy-start.4
  3.2 8.7 %collective-permute-start.1 = (bf16[128,256]{1,0:T(8,128)(2,1)S(1)}, bf16[128,256]{1,0:T(8,128)(2,1)S(1)}, u32[]{:S(2)}, u32[]{:S(2)}) collective-permute-start(bf16[128,256]{1,0:T(8,128)(2,1)S(1)} %get-tuple-element.54), channel_id=1, source_target_pairs={{0,8},{1,9},{2,10},{3,11},{4,12},{5,13},{6,14},{7,15},{8,0},{9,1},... | collective-permute-start | bytes 196616 | tf_op jit(solution)/shard_map/kv_over_x/ppermute | solution.py:39
  6.8 5.1 %collective-permute-start.2 = (bf16[128,256]{1,0:T(8,128)(2,1)S(1)}, bf16[128,256]{1,0:T(8,128)(2,1)S(1)}, u32[]{:S(2)}, u32[]{:S(2)}) collective-permute-start(bf16[128,256]{1,0:T(8,128)(2,1)S(1)} %get-tuple-element.55), channel_id=1, source_target_pairs={{0,12},{1,13},{2,14},{3,15},{4,0},{5,1},{6,2},{7,3},{8,4},{9,5},{1... | collective-permute-start | bytes 196616 | tf_op jit(solution)/shard_map/kv_over_x/ppermute | solution.py:39
  7.7 10.9 %copy-start = (bf16[128,8192]{1,0:T(8,128)(2,1)S(1)}, bf16[128,8192]{1,0:T(8,128)(2,1)}, u32[]{:S(2)}) copy-start(bf16[128,8192]{1,0:T(8,128)(2,1)} %refs_1_.3) | copy-start | bytes 6291460
  7.7 4.6 %collective-permute-start = (bf16[128,256]{1,0:T(8,128)(2,1)S(1)}, bf16[128,256]{1,0:T(8,128)(2,1)S(1)}, u32[]{:S(2)}, u32[]{:S(2)}) collective-permute-start(bf16[128,256]{1,0:T(8,128)(2,1)S(1)} %get-tuple-element.49.refs_3_), channel_id=1, source_target_pairs={{0,4},{1,5},{2,6},{3,7},{4,8},{5,9},{6,10},{7,11},{8,12},{9,13},{1... | collective-permute-start | bytes 196616 | tf_op jit(solution)/shard_map/kv_over_x/ppermute | solution.py:39
  8.3 1.3 copy-start.1
  9.5 1.2 copy-start.2
  12.4 19.9 %copy-start.5 = (s32[1,8]{1,0:T(1,128)S(1)}, s32[1,8]{1,0:T(1,128)}, u32[]{:S(2)}) copy-start(s32[1,8]{1,0:T(1,128)} %param.11) | copy-start | bytes 100
  12.4 19.9 %collective-permute-start.4 = (bf16[2,1024,128]{2,1,0:T(8,128)(2,1)S(1)}, bf16[2,1024,128]{2,1,0:T(8,128)(2,1)S(1)}, u32[]{:S(2)}, u32[]{:S(2)}) collective-permute-start(bf16[2,1024,128]{2,1,0:T(8,128)(2,1)S(1)} %get-tuple-element.57), channel_id=1, source_target_pairs={{0,12},{1,13},{2,14},{3,15},{4,0},{5,1},{6,2},{7,3},{8,4},{9,5},{1... | collective-permute-start | bytes 1572872 | tf_op jit(solution)/shard_map/q_do_over_x/ppermute | solution.py:39
  14.1 18.2 %collective-permute-start.3 = (bf16[2,1024,128]{2,1,0:T(8,128)(2,1)S(1)}, bf16[2,1024,128]{2,1,0:T(8,128)(2,1)S(1)}, u32[]{:S(2)}, u32[]{:S(2)}) collective-permute-start(bf16[2,1024,128]{2,1,0:T(8,128)(2,1)S(1)} %get-tuple-element.56.refs_5_), channel_id=1, source_target_pairs={{0,4},{1,5},{2,6},{3,7},{4,8},{5,9},{6,10},{7,11},{8,12},{9,13},{1... | collective-permute-start | bytes 1572872 | tf_op jit(solution)/shard_map/q_do_over_x/ppermute | solution.py:39
  14.7 8.8 %collective-permute-start.7 = (bf16[512,256]{1,0:T(8,128)(2,1)S(1)}, bf16[512,256]{1,0:T(8,128)(2,1)S(1)}, u32[]{:S(2)}, u32[]{:S(2)}) collective-permute-start(bf16[512,256]{1,0:T(8,128)(2,1)S(1)} %kv_over_x.3.refs_3_.refs_2_), channel_id=1, source_target_pairs={{0,3},{1,0},{2,1},{3,2},{4,7},{5,4},{6,5},{7,6},{8,11},{9,8},{10,9... | collective-permute-start | bytes 786440 | tf_op jit(solution)/shard_map/kv_over_y/ppermute | solution.py:39
  17.5 7.4 %collective-permute-start.6 = (bf16[512,256]{1,0:T(8,128)(2,1)S(1)}, bf16[512,256]{1,0:T(8,128)(2,1)S(1)}, u32[]{:S(2)}, u32[]{:S(2)}) collective-permute-start(bf16[512,256]{1,0:T(8,128)(2,1)S(1)} %kv_over_x.3.refs_3_.refs_2_), channel_id=1, source_target_pairs={{0,2},{1,3},{2,0},{3,1},{4,6},{5,7},{6,4},{7,5},{8,10},{9,11},{10,... | collective-permute-start | bytes 786440 | tf_op jit(solution)/shard_map/kv_over_y/ppermute | solution.py:39
  17.9 14.4 %collective-permute-start.5 = (bf16[512,256]{1,0:T(8,128)(2,1)S(1)}, bf16[512,256]{1,0:T(8,128)(2,1)S(1)}, u32[]{:S(2)}, u32[]{:S(2)}) collective-permute-start(bf16[512,256]{1,0:T(8,128)(2,1)S(1)} %kv_over_x.3.refs_3_.refs_2_), channel_id=1, source_target_pairs={{0,1},{1,2},{2,3},{3,0},{4,5},{5,6},{6,7},{7,4},{8,9},{9,10},{10,1... | collective-permute-start | bytes 786440 | tf_op jit(solution)/shard_map/kv_over_y/ppermute | solution.py:39
  23.6 17.6 %collective-permute-start.8 = (bf16[2,1024,128]{2,1,0:T(8,128)(2,1)S(1)}, bf16[2,1024,128]{2,1,0:T(8,128)(2,1)S(1)}, u32[]{:S(2)}, u32[]{:S(2)}) collective-permute-start(bf16[2,1024,128]{2,1,0:T(8,128)(2,1)S(1)} %get-tuple-element.61), channel_id=1, source_target_pairs={{0,8},{1,9},{2,10},{3,11},{4,12},{5,13},{6,14},{7,15},{8,0},{9,1},... | collective-permute-start | bytes 1572872 | tf_op jit(solution)/shard_map/q_do_over_x/ppermute | solution.py:39
  43.5 10.0 %collective-permute-start.9 = (bf16[512,256]{1,0:T(8,128)(2,1)S(1)}, bf16[512,256]{1,0:T(8,128)(2,1)S(1)}, u32[]{:S(2)}, u32[]{:S(2)}) collective-permute-start(bf16[512,256]{1,0:T(8,128)(2,1)S(1)} %get-tuple-element.70), channel_id=1, source_target_pairs={{0,1},{1,2},{2,3},{3,0},{4,5},{5,6},{6,7},{7,4},{8,9},{9,10},{10,1... | collective-permute-start | bytes 786440 | tf_op jit(solution)/shard_map/terms_over_y/ppermute | solution.py:39
  43.7 10.2 %collective-permute-start.12 = (bf16[2,128,1024]{2,1,0:T(8,128)(2,1)S(1)}, bf16[2,128,1024]{2,1,0:T(8,128)(2,1)S(1)}, u32[]{:S(2)}, u32[]{:S(2)}) collective-permute-start(bf16[2,128,1024]{2,1,0:T(8,128)(2,1)S(1)} %get-tuple-element.76), channel_id=1, source_target_pairs={{0,4},{1,5},{2,6},{3,7},{4,8},{5,9},{6,10},{7,11},{8,12},{9,13},{1... | collective-permute-start | bytes 1572872 | tf_op jit(solution)/shard_map/terms_over_y/ppermute | solution.py:39
  43.9 9.5 %collective-permute-start.10 = (bf16[512,256]{1,0:T(8,128)(2,1)S(1)}, bf16[512,256]{1,0:T(8,128)(2,1)S(1)}, u32[]{:S(2)}, u32[]{:S(2)}) collective-permute-start(bf16[512,256]{1,0:T(8,128)(2,1)S(1)} %get-tuple-element.71), channel_id=1, source_target_pairs={{0,2},{1,3},{2,0},{3,1},{4,6},{5,7},{6,4},{7,5},{8,10},{9,11},{10,... | collective-permute-start | bytes 786440 | tf_op jit(solution)/shard_map/terms_over_y/ppermute | solution.py:39
  47.3 6.6 %collective-permute-start.11 = (bf16[512,256]{1,0:T(8,128)(2,1)S(1)}, bf16[512,256]{1,0:T(8,128)(2,1)S(1)}, u32[]{:S(2)}, u32[]{:S(2)}) collective-permute-start(bf16[512,256]{1,0:T(8,128)(2,1)S(1)} %get-tuple-element.72), channel_id=1, source_target_pairs={{0,3},{1,0},{2,1},{3,2},{4,7},{5,4},{6,5},{7,6},{8,11},{9,8},{10,9... | collective-permute-start | bytes 786440 | tf_op jit(solution)/shard_map/terms_over_y/ppermute | solution.py:39
  49.3 15.1 %collective-permute-start.19 = (bf16[2,128,1024]{2,1,0:T(8,128)(2,1)S(1)}, bf16[2,128,1024]{2,1,0:T(8,128)(2,1)S(1)}, u32[]{:S(2)}, u32[]{:S(2)}) collective-permute-start(bf16[2,128,1024]{2,1,0:T(8,128)(2,1)S(1)} %get-tuple-element.81), channel_id=1, source_target_pairs={{0,8},{1,9},{2,10},{3,11},{4,12},{5,13},{6,14},{7,15},{8,0},{9,1},... | collective-permute-start | bytes 1572872 | tf_op jit(solution)/shard_map/terms_over_y/ppermute | solution.py:39
  53.5 12.0 %collective-permute-start.20 = (bf16[2,128,1024]{2,1,0:T(8,128)(2,1)S(1)}, bf16[2,128,1024]{2,1,0:T(8,128)(2,1)S(1)}, u32[]{:S(2)}, u32[]{:S(2)}) collective-permute-start(bf16[2,128,1024]{2,1,0:T(8,128)(2,1)S(1)} %get-tuple-element.82), channel_id=1, source_target_pairs={{0,12},{1,13},{2,14},{3,15},{4,0},{5,1},{6,2},{7,3},{8,4},{9,5},{1... | collective-permute-start | bytes 1572872 | tf_op jit(solution)/shard_map/terms_over_y/ppermute | solution.py:39
  54.0 23.0 %collective-permute-start.15 = (bf16[512,256]{1,0:T(8,128)(2,1)S(1)}, bf16[512,256]{1,0:T(8,128)(2,1)S(1)}, u32[]{:S(2)}, u32[]{:S(2)}) collective-permute-start(bf16[512,256]{1,0:T(8,128)(2,1)S(1)} %terms_over_y.3.refs_0_), channel_id=1, source_target_pairs={{0,12},{1,13},{2,14},{3,15},{4,0},{5,1},{6,2},{7,3},{8,4},{9,5},{1... | collective-permute-start | bytes 786440 | tf_op jit(solution)/shard_map/dkv_over_x/ppermute | solution.py:39
  57.5 19.6 %collective-permute-start.14 = (bf16[512,256]{1,0:T(8,128)(2,1)S(1)}, bf16[512,256]{1,0:T(8,128)(2,1)S(1)}, u32[]{:S(2)}, u32[]{:S(2)}) collective-permute-start(bf16[512,256]{1,0:T(8,128)(2,1)S(1)} %terms_over_y.3.refs_0_), channel_id=1, source_target_pairs={{0,8},{1,9},{2,10},{3,11},{4,12},{5,13},{6,14},{7,15},{8,0},{9,1},... | collective-permute-start | bytes 786440 | tf_op jit(solution)/shard_map/dkv_over_x/ppermute | solution.py:39
  61.1 16.9 %collective-permute-start.13 = (bf16[512,256]{1,0:T(8,128)(2,1)S(1)}, bf16[512,256]{1,0:T(8,128)(2,1)S(1)}, u32[]{:S(2)}, u32[]{:S(2)}) collective-permute-start(bf16[512,256]{1,0:T(8,128)(2,1)S(1)} %terms_over_y.3.refs_0_), channel_id=1, source_target_pairs={{0,4},{1,5},{2,6},{3,7},{4,8},{5,9},{6,10},{7,11},{8,12},{9,13},{1... | collective-permute-start | bytes 786440 | tf_op jit(solution)/shard_map/dkv_over_x/ppermute | solution.py:39
  79.1 15.7 %collective-permute-start.21 = (bf16[1024,512]{1,0:T(8,128)(2,1)S(1)}, bf16[1024,512]{1,0:T(8,128)(2,1)S(1)}, u32[]{:S(2)}, u32[]{:S(2)}) collective-permute-start(bf16[1024,512]{1,0:T(8,128)(2,1)S(1)} %get-tuple-element.84), channel_id=1, source_target_pairs={{0,16},{1,17},{2,18},{3,19},{4,20},{5,21},{6,22},{7,23},{8,24},{9,... | collective-permute-start | bytes 3145736 | tf_op jit(solution)/shard_map/turn_x/ppermute | solution.py:39
  90.4 2.7 %collective-permute-start.22 = (bf16[512,256]{1,0:T(8,128)(2,1)S(1)}, bf16[512,256]{1,0:T(8,128)(2,1)S(1)}, u32[]{:S(2)}, u32[]{:S(2)}) collective-permute-start(bf16[512,256]{1,0:T(8,128)(2,1)S(1)} %terms_over_y.3.refs_0_), channel_id=1, source_target_pairs={{0,16},{1,17},{2,18},{3,19},{4,20},{5,21},{6,22},{7,23},{8,24},{9,... | collective-permute-start | bytes 786440 | tf_op jit(solution)/shard_map/dkv_over_x/ppermute | solution.py:39
  90.5 4.2 %collective-permute-start.23 = (bf16[512,256]{1,0:T(8,128)(2,1)S(1)}, bf16[512,256]{1,0:T(8,128)(2,1)S(1)}, u32[]{:S(2)}, u32[]{:S(2)}) collective-permute-start(bf16[512,256]{1,0:T(8,128)(2,1)S(1)} %collective-permute-done.13.refs_3_.refs_5_.refs_1_), channel_id=1, source_target_pairs={{0,16},{1,17},{2,18},{3,19},{4,20},{5,21},{6,22},{7,23},{8,24},{9,... | collective-permute-start | bytes 786440 | tf_op jit(solution)/shard_map/dkv_over_x/ppermute | solution.py:39
  90.9 6.8 %collective-permute-start.28 = (bf16[512,256]{1,0:T(8,128)(2,1)S(1)}, bf16[512,256]{1,0:T(8,128)(2,1)S(1)}, u32[]{:S(2)}, u32[]{:S(2)}) collective-permute-start(bf16[512,256]{1,0:T(8,128)(2,1)S(1)} %collective-permute-done.15.refs_5_.refs_7_.refs_4_), channel_id=1, source_target_pairs={{0,16},{1,17},{2,18},{3,19},{4,20},{5,21},{6,22},{7,23},{8,24},{9,... | collective-permute-start | bytes 786440 | tf_op jit(solution)/shard_map/dkv_over_x/ppermute | solution.py:39
  91.0 7.0 %collective-permute-start.27 = (bf16[512,256]{1,0:T(8,128)(2,1)S(1)}, bf16[512,256]{1,0:T(8,128)(2,1)S(1)}, u32[]{:S(2)}, u32[]{:S(2)}) collective-permute-start(bf16[512,256]{1,0:T(8,128)(2,1)S(1)} %collective-permute-done.14.refs_4_.refs_6_.refs_3_), channel_id=1, source_target_pairs={{0,16},{1,17},{2,18},{3,19},{4,20},{5,21},{6,22},{7,23},{8,24},{9,... | collective-permute-start | bytes 786440 | tf_op jit(solution)/shard_map/dkv_over_x/ppermute | solution.py:39
  93.1 7.5 %collective-permute-start.16 = (bf16[1024,128]{1,0:T(8,128)(2,1)S(1)}, bf16[1024,128]{1,0:T(8,128)(2,1)S(1)}, u32[]{:S(2)}, u32[]{:S(2)}) collective-permute-start(bf16[1024,128]{1,0:T(8,128)(2,1)S(1)} %get-tuple-element.77), channel_id=1, source_target_pairs={{0,12},{1,13},{2,14},{3,15},{4,0},{5,1},{6,2},{7,3},{8,4},{9,5},{1... | collective-permute-start | bytes 786440 | tf_op jit(solution)/shard_map/grad_q/ppermute | solution.py:39
  94.7 8.8 %collective-permute-start.17 = (bf16[1024,128]{1,0:T(8,128)(2,1)S(1)}, bf16[1024,128]{1,0:T(8,128)(2,1)S(1)}, u32[]{:S(2)}, u32[]{:S(2)}) collective-permute-start(bf16[1024,128]{1,0:T(8,128)(2,1)S(1)} %get-tuple-element.78), channel_id=1, source_target_pairs={{0,8},{1,9},{2,10},{3,11},{4,12},{5,13},{6,14},{7,15},{8,0},{9,1},... | collective-permute-start | bytes 786440 | tf_op jit(solution)/shard_map/grad_q/ppermute | solution.py:39
  94.9 15.0 %collective-permute-start.18 = (bf16[1024,128]{1,0:T(8,128)(2,1)S(1)}, bf16[1024,128]{1,0:T(8,128)(2,1)S(1)}, u32[]{:S(2)}, u32[]{:S(2)}) collective-permute-start(bf16[1024,128]{1,0:T(8,128)(2,1)S(1)} %get-tuple-element.79), channel_id=1, source_target_pairs={{0,4},{1,5},{2,6},{3,7},{4,8},{5,9},{6,10},{7,11},{8,12},{9,13},{1... | collective-permute-start | bytes 786440 | tf_op jit(solution)/shard_map/grad_q/ppermute | solution.py:39
  97.7 16.4 %collective-permute-start.24 = (bf16[8,32,512]{2,1,0:T(8,128)(2,1)S(1)}, bf16[8,32,512]{2,1,0:T(8,128)(2,1)S(1)}, u32[]{:S(2)}, u32[]{:S(2)}) collective-permute-start(bf16[8,32,512]{2,1,0:T(8,128)(2,1)S(1)} %get-tuple-element.86), channel_id=1, source_target_pairs={{0,1},{1,2},{2,3},{3,0},{4,5},{5,6},{6,7},{7,4},{8,9},{9,10},{10,1... | collective-permute-start | bytes 786440 | tf_op jit(solution)/shard_map/project/partial_over_y/ppermute | solution.py:39
  98.0 16.6 %collective-permute-start.25 = (bf16[8,32,512]{2,1,0:T(8,128)(2,1)S(1)}, bf16[8,32,512]{2,1,0:T(8,128)(2,1)S(1)}, u32[]{:S(2)}, u32[]{:S(2)}) collective-permute-start(bf16[8,32,512]{2,1,0:T(8,128)(2,1)S(1)} %get-tuple-element.87), channel_id=1, source_target_pairs={{0,2},{1,3},{2,0},{3,1},{4,6},{5,7},{6,4},{7,5},{8,10},{9,11},{10,... | collective-permute-start | bytes 786440 | tf_op jit(solution)/shard_map/project/partial_over_y/ppermute | solution.py:39
  100.6 14.1 %collective-permute-start.26 = (bf16[8,32,512]{2,1,0:T(8,128)(2,1)S(1)}, bf16[8,32,512]{2,1,0:T(8,128)(2,1)S(1)}, u32[]{:S(2)}, u32[]{:S(2)}) collective-permute-start(bf16[8,32,512]{2,1,0:T(8,128)(2,1)S(1)} %get-tuple-element.88), channel_id=1, source_target_pairs={{0,3},{1,0},{2,1},{3,2},{4,7},{5,4},{6,5},{7,6},{8,11},{9,8},{10,9... | collective-permute-start | bytes 786440 | tf_op jit(solution)/shard_map/project/partial_over_y/ppermute | solution.py:39
  111.9 9.0 %collective-permute-start.29 = (bf16[8,32,512]{2,1,0:T(8,128)(2,1)S(1)}, bf16[8,32,512]{2,1,0:T(8,128)(2,1)S(1)}, u32[]{:S(2)}, u32[]{:S(2)}) collective-permute-start(bf16[8,32,512]{2,1,0:T(8,128)(2,1)S(1)} %get-tuple-element.90), channel_id=1, source_target_pairs={{0,1},{1,2},{2,3},{3,0},{4,5},{5,6},{6,7},{7,4},{8,9},{9,10},{10,1... | collective-permute-start | bytes 786440 | tf_op jit(solution)/shard_map/project/partial_over_y/ppermute | solution.py:39
  112.0 13.7 %collective-permute-start.30 = (bf16[8,32,512]{2,1,0:T(8,128)(2,1)S(1)}, bf16[8,32,512]{2,1,0:T(8,128)(2,1)S(1)}, u32[]{:S(2)}, u32[]{:S(2)}) collective-permute-start(bf16[8,32,512]{2,1,0:T(8,128)(2,1)S(1)} %get-tuple-element.91), channel_id=1, source_target_pairs={{0,2},{1,3},{2,0},{3,1},{4,6},{5,7},{6,4},{7,5},{8,10},{9,11},{10,... | collective-permute-start | bytes 786440 | tf_op jit(solution)/shard_map/project/partial_over_y/ppermute | solution.py:39
  114.1 12.3 %collective-permute-start.31 = (bf16[8,32,512]{2,1,0:T(8,128)(2,1)S(1)}, bf16[8,32,512]{2,1,0:T(8,128)(2,1)S(1)}, u32[]{:S(2)}, u32[]{:S(2)}) collective-permute-start(bf16[8,32,512]{2,1,0:T(8,128)(2,1)S(1)} %get-tuple-element.92), channel_id=1, source_target_pairs={{0,3},{1,0},{2,1},{3,2},{4,7},{5,4},{6,5},{7,6},{8,11},{9,8},{10,9... | collective-permute-start | bytes 786440 | tf_op jit(solution)/shard_map/project/partial_over_y/ppermute | solution.py:39
  127.5 28.3 %all-to-all-start = ((bf16[8,32,1024]{2,1,0:T(8,128)(2,1)}), bf16[8,32,1024]{2,1,0:T(8,128)(2,1)S(1)}, u32[]{:S(2)}, u32[]{:S(2)}) async-start(bf16[8,32,1024]{2,1,0:T(8,128)(2,1)} %partial_over_z.1), calls=%async_computation | async-start | bytes 1048576 | tf_op jit(solution)/shard_map/partial_over_z/all_to_all | solution.py:364

commit v4 on v3

--- a/solution.py
+++ b/solution.py
@@ -341,8 +341,6 @@
     with jax.named_scope("turn_x"):
         xt, xt_give = call(turn_x_kernel, [sds((1024, 512))] * 2, (at, *xp), moved=1 << 22, late=own[1:])
         xt_other = send(xt_give, dc=1)
-    with jax.named_scope("grad_q"):
-        dq = [dq[0]] + [send(d, dx=-s - 1) for s, d in enumerate(after(dq[1:], own[1:]))]
     with jax.named_scope("project"):
         parts = []
         for pick in (slice(0, 2), slice(2, 4)):
@@ -354,12 +352,13 @@
                 scratch=[pltpu.VMEM((1024, 256), F32)],
                 flops=n * 5 * 10**8,
                 moved=1 << 22,
-                late=parts[:1] + dq[1:] if parts else [],
+                late=parts[:1],
             )
             with jax.named_scope("partial_over_y"):
                 parts += [partial[0]] + [send(partial[s], dy=s) for s in range(1, NY)]
     with jax.named_scope("partial_over_z"):
-        (summed,) = call(add_kernel, [sds((NZ, 32, 1024))], parts, moved=5 << 20, smem=0)
+        dq = [dq[0]] + [send(d, dx=-s - 1) for s, d in enumerate(after(dq[1:], [parts[1]]))]
+        (summed,) = call(add_kernel, [sds((NZ, 32, 1024))], parts, moved=5 << 20, smem=0, late=dq[1:])
         groups = [[z * NC + c for z in range(NZ)] for c in range(NC)]
         last = lax.all_to_all(summed, "dp", 0, 0, axis_index_groups=groups, tiled=True)
     with jax.named_scope("grad_q"):

time: 159 us -> 159 us (level); the launches traced: 157 us -> 159 us
  waiting for transfers between devices: 64 us -> 60.5 us
  starting transfers between devices: 63.6 us -> 67.1 us
  Pallas kernels: 24.2 us -> 26.5 us
    ppermute x32, starting transfers between devices: 51 us -> 56.2 us  [send(): return lax.ppermute(value, AXES, pairs)]
    ppermute x32, waiting for transfers between devices: 50.1 us -> 46.6 us  [send(): return lax.ppermute(value, AXES, pairs)]
    pallas_call x16, Pallas kernels: 24.2 us -> 26.5 us  [call(): pl.pallas_call(body, out_shape=outs, in_specs=[SM] * smem + [VM] * (len(i...]
    all_to_all x1, starting transfers between devices: 12.6 us -> 10.9 us  [on_device(): lax.all_to_all(summed, 'dp', 0, 0, axis_index_groups=groups, tiled=True)]
  transfers between devices with their start and end apart: 33 -> 33, of which waited for: 16 -> 15; matrix products, arithmetic and copies ran while one was open for 0% -> 0% of each run, Pallas kernels for 11% -> 10%
where the time goes in v4:
time: 159 us
  starting transfers between devices  67.1 us (42%)
  waiting for transfers between devices  60.5 us (38%)
  Pallas kernels  26.5 us (17%)
  local copies, waits for them, and re-layouts  4.3 us (3%)
    ppermute x32, starting transfers between devices, send(): return lax.ppermute(value, AXES, pairs)  56.2 us
    ppermute x32, waiting for transfers between devices, send(): return lax.ppermute(value, AXES, pairs)  46.6 us
    pallas_call x16, Pallas kernels, call(): pl.pallas_call(body, out_shape=outs, in_specs=[SM] * smem + [VM] * (len(i...  26.5 us
    all_to_all x1, waiting for transfers between devices, on_device(): lax.all_to_all(summed, 'dp', 0, 0, axis_index_groups=groups, tiled=True)  13.9 us
    all_to_all x1, starting transfers between devices, on_device(): lax.all_to_all(summed, 'dp', 0, 0, axis_index_groups=groups, tiled=True)  10.9 us
    unnamed x12, local copies, waits for them, and re-layouts  4.3 us
  transfers between devices with their start and end apart: 33, of which 15 were waited for; matrix products, arithmetic and copies ran while one was open for 0% of the time, Pallas kernels for 10%

profile of v4, /device:TPU:1, one launch (start us, length us, event | category | flops | bytes accessed | tf_op | source)
XLA Modules:
  0.0 159.3 jit_solution(2764038157508776628)
XLA Ops:
  0.7 0.9 copy-done.3
  1.7 0.9 copy-done.4
  2.6 0.6 pack_kv.1
  3.2 3.7 %collective-permute-start.1 = (bf16[128,256]{1,0:T(8,128)(2,1)S(1)}, bf16[128,256]{1,0:T(8,128)(2,1)S(1)}, u32[]{:S(2)}, u32[]{:S(2)}) collective-permute-start(bf16[128,256]{1,0:T(8,128)(2,1)S(1)} %get-tuple-element.54), channel_id=1, source_target_pairs={{0,8},{1,9},{2,10},{3,11},{4,12},{5,13},{6,14},{7,15},{8,0},{9,1},... | collective-permute-start | bytes 196616 | tf_op jit(solution)/shard_map/kv_over_x/ppermute | solution.py:39
  6.8 0.9 collective-permute-start.2
  7.7 0.6 collective-permute-start
  8.3 1.3 copy-done.1
  9.5 1.2 copy-done.2
  10.8 1.1 pack_q_do.1
  12.4 1.8 %collective-permute-start.4 = (bf16[2,1024,128]{2,1,0:T(8,128)(2,1)S(1)}, bf16[2,1024,128]{2,1,0:T(8,128)(2,1)S(1)}, u32[]{:S(2)}, u32[]{:S(2)}) collective-permute-start(bf16[2,1024,128]{2,1,0:T(8,128)(2,1)S(1)} %get-tuple-element.57), channel_id=1, source_target_pairs={{0,12},{1,13},{2,14},{3,15},{4,0},{5,1},{6,2},{7,3},{8,4},{9,5},{1... | collective-permute-start | bytes 1572872 | tf_op jit(solution)/shard_map/q_do_over_x/ppermute | solution.py:39
  14.1 0.6 kv_over_x.3.refs_3_.refs_2_
  14.7 2.8 %collective-permute-start.7 = (bf16[512,256]{1,0:T(8,128)(2,1)S(1)}, bf16[512,256]{1,0:T(8,128)(2,1)S(1)}, u32[]{:S(2)}, u32[]{:S(2)}) collective-permute-start(bf16[512,256]{1,0:T(8,128)(2,1)S(1)} %kv_over_x.3.refs_3_.refs_2_), channel_id=1, source_target_pairs={{0,3},{1,0},{2,1},{3,2},{4,7},{5,4},{6,5},{7,6},{8,11},{9,8},{10,9... | collective-permute-start | bytes 786440 | tf_op jit(solution)/shard_map/kv_over_y/ppermute | solution.py:39
  17.9 0.7 collective-permute-start.5
  18.6 1.1 pack_x.1
  19.7 3.9 %collective-permute-done.7.refs_6_ = bf16[512,256]{1,0:T(8,128)(2,1)S(1)} collective-permute-done((bf16[512,256]{1,0:T(8,128)(2,1)S(1)}, bf16[512,256]{1,0:T(8,128)(2,1)S(1)}, u32[]{:S(2)}, u32[]{:S(2)}) %collective-permute-start.7) | collective-permute-done | bytes 262176 | tf_op jit(solution)/shard_map/kv_over_y/ppermute | solution.py:39
  23.6 1.3 collective-permute-start.8
  24.9 7.4 %collective-permute-done.5.refs_4_ = bf16[512,256]{1,0:T(8,128)(2,1)S(1)} collective-permute-done((bf16[512,256]{1,0:T(8,128)(2,1)S(1)}, bf16[512,256]{1,0:T(8,128)(2,1)S(1)}, u32[]{:S(2)}, u32[]{:S(2)}) %collective-permute-start.5) | collective-permute-done | bytes 262176 | tf_op jit(solution)/shard_map/kv_over_y/ppermute | solution.py:39
  32.3 7.7 %attention.2 = (bf16[1024,128]{1,0:T(8,128)(2,1)S(1)}, bf16[1024,128]{1,0:T(8,128)(2,1)S(1)}, bf16[1024,128]{1,0:T(8,128)(2,1)S(1)}, f32[2048,128]{1,0:T(8,128)S...) custom-call(s32[4]{0:T(128)S(1)} %pad_add_fusion.at.refs_0_, ...), custom_call_target="tpu_custom_call" | custom-call | flops 12000000000 | bytes 6291456 | tf_op jit(solution)/shard_map/attention/pallas_call | solution.py:47
  40.0 5.7 %attention.3 = (bf16[1024,128]{1,0:T(8,128)(2,1)S(1)}, bf16[512,256]{1,0:T(8,128)(2,1)S(1)}, bf16[512,256]{1,0:T(8,128)(2,1)S(1)}, bf16[512,256]{1,0:T(8,128)(2,1)S(1)}, bf16[512,256]{1,0:T(8,128)(2,1)S(1)}) custom-call(s32[4]{0:T(128)S(1)} %pad_add_fusion.at.refs_0_, s32[8]{0:T(128)S(1)} %bitcast.6, ...), custom_call_target="tpu_custom_call" | custom-call | flops 4000000000 | bytes 6291456 | tf_op jit(solution)/shard_map/attention/pallas_call | solution.py:47
  46.2 3.3 %collective-permute-start.13 = (bf16[512,256]{1,0:T(8,128)(2,1)S(1)}, bf16[512,256]{1,0:T(8,128)(2,1)S(1)}, u32[]{:S(2)}, u32[]{:S(2)}) collective-permute-start(bf16[512,256]{1,0:T(8,128)(2,1)S(1)} %get-tuple-element.78), channel_id=1, source_target_pairs={{0,2},{1,3},{2,0},{3,1},{4,6},{5,7},{6,4},{7,5},{8,10},{9,11},{10,... | collective-permute-start | bytes 786440 | tf_op jit(solution)/shard_map/terms_over_y/ppermute | solution.py:39
  49.5 2.1 %collective-permute-start.14 = (bf16[512,256]{1,0:T(8,128)(2,1)S(1)}, bf16[512,256]{1,0:T(8,128)(2,1)S(1)}, u32[]{:S(2)}, u32[]{:S(2)}) collective-permute-start(bf16[512,256]{1,0:T(8,128)(2,1)S(1)} %get-tuple-element.79), channel_id=1, source_target_pairs={{0,3},{1,0},{2,1},{3,2},{4,7},{5,4},{6,5},{7,6},{8,11},{9,8},{10,9... | collective-permute-start | bytes 786440 | tf_op jit(solution)/shard_map/terms_over_y/ppermute | solution.py:39
  51.6 4.2 %collective-permute-start.10 = (bf16[2,128,1024]{2,1,0:T(8,128)(2,1)S(1)}, bf16[2,128,1024]{2,1,0:T(8,128)(2,1)S(1)}, u32[]{:S(2)}, u32[]{:S(2)}) collective-permute-start(bf16[2,128,1024]{2,1,0:T(8,128)(2,1)S(1)} %get-tuple-element.75), channel_id=1, source_target_pairs={{0,8},{1,9},{2,10},{3,11},{4,12},{5,13},{6,14},{7,15},{8,0},{9,1},... | collective-permute-start | bytes 1572872 | tf_op jit(solution)/shard_map/terms_over_y/ppermute | solution.py:39
  56.2 3.5 %collective-permute-start.17 = (bf16[512,256]{1,0:T(8,128)(2,1)S(1)}, bf16[512,256]{1,0:T(8,128)(2,1)S(1)}, u32[]{:S(2)}, u32[]{:S(2)}) collective-permute-start(bf16[512,256]{1,0:T(8,128)(2,1)S(1)} %terms_over_y.3.refs_0_), channel_id=1, source_target_pairs={{0,12},{1,13},{2,14},{3,15},{4,0},{5,1},{6,2},{7,3},{8,4},{9,5},{1... | collective-permute-start | bytes 786440 | tf_op jit(solution)/shard_map/dkv_over_x/ppermute | solution.py:39
  59.7 4.1 %collective-permute-start.16 = (bf16[512,256]{1,0:T(8,128)(2,1)S(1)}, bf16[512,256]{1,0:T(8,128)(2,1)S(1)}, u32[]{:S(2)}, u32[]{:S(2)}) collective-permute-start(bf16[512,256]{1,0:T(8,128)(2,1)S(1)} %terms_over_y.3.refs_0_), channel_id=1, source_target_pairs={{0,8},{1,9},{2,10},{3,11},{4,12},{5,13},{6,14},{7,15},{8,0},{9,1},... | collective-permute-start | bytes 786440 | tf_op jit(solution)/shard_map/dkv_over_x/ppermute | solution.py:39
  64.0 2.7 %collective-permute-done.10.refs_3_ = bf16[2,128,1024]{2,1,0:T(8,128)(2,1)S(1)} collective-permute-done((bf16[2,128,1024]{2,1,0:T(8,128)(2,1)S(1)}, bf16[2,128,1024]{2,1,0:T(8,128)(2,1)S(1)}, u32[]{:S(2)}, u32[]{:S(2)}) %collective-permute-start.10) | collective-permute-done | bytes 524320 | tf_op jit(solution)/shard_map/terms_over_y/ppermute | solution.py:39
  66.7 1.1 collective-permute-done.11.refs_4_
  67.7 11.5 %collective-permute-done.17.refs_7_.refs_4_ = bf16[512,256]{1,0:T(8,128)(2,1)S(1)} collective-permute-done((bf16[512,256]{1,0:T(8,128)(2,1)S(1)}, bf16[512,256]{1,0:T(8,128)(2,1)S(1)}, u32[]{:S(2)}, u32[]{:S(2)}) %collective-permute-start.17) | collective-permute-done | bytes 262176 | tf_op jit(solution)/shard_map/dkv_over_x/ppermute | solution.py:39
  79.3 1.0 collective-permute-done.15.refs_5_.refs_1_
  80.3 1.1 turn_x.1
  81.4 9.0 %collective-permute-start.18 = (bf16[1024,512]{1,0:T(8,128)(2,1)S(1)}, bf16[1024,512]{1,0:T(8,128)(2,1)S(1)}, u32[]{:S(2)}, u32[]{:S(2)}) collective-permute-start(bf16[1024,512]{1,0:T(8,128)(2,1)S(1)} %get-tuple-element.81), channel_id=1, source_target_pairs={{0,16},{1,17},{2,18},{3,19},{4,20},{5,21},{6,22},{7,23},{8,24},{9,... | collective-permute-start | bytes 3145736 | tf_op jit(solution)/shard_map/turn_x/ppermute | solution.py:39
  91.4 1.6 %collective-permute-done.19.refs_2_ = bf16[512,256]{1,0:T(8,128)(2,1)S(1)} collective-permute-done((bf16[512,256]{1,0:T(8,128)(2,1)S(1)}, bf16[512,256]{1,0:T(8,128)(2,1)S(1)}, u32[]{:S(2)}, u32[]{:S(2)}) %collective-permute-start.19) | collective-permute-done | bytes 262176 | tf_op jit(solution)/shard_map/dkv_over_x/ppermute | solution.py:39
  93.4 2.0 %project.2 = (bf16[8,32,512]{2,1,0:T(8,128)(2,1)S(1)}, bf16[8,32,512]{2,1,0:T(8,128)(2,1)S(1)}, bf16[8,32,512]{2,1,0:T(8,128)(2,1)S(1)}, bf16[8,32,512]{2,1,0:T(8,128)(2,1)S(1)}) custom-call(s32[4]{0:T(128)S(1)} %pad_add_fusion.at.refs_0_, bf16[1024,512]{1,0:T(8,128)(2,1)S(1)} %get-tuple-element.80.xt.refs_1_, ...), custom_call_target="tpu_custom_call" | custom-call | flops 1000000000 | bytes 4194304 | tf_op jit(solution)/shard_map/project/pallas_call | solution.py:47
  95.5 0.9 collective-permute-start.21
  96.3 3.5 %collective-permute-start.25 = (bf16[8,32,512]{2,1,0:T(8,128)(2,1)S(1)}, bf16[8,32,512]{2,1,0:T(8,128)(2,1)S(1)}, u32[]{:S(2)}, u32[]{:S(2)}) collective-permute-start(bf16[8,32,512]{2,1,0:T(8,128)(2,1)S(1)} %get-tuple-element.87), channel_id=1, source_target_pairs={{0,2},{1,3},{2,0},{3,1},{4,6},{5,7},{6,4},{7,5},{8,10},{9,11},{10,... | collective-permute-start | bytes 786440 | tf_op jit(solution)/shard_map/project/partial_over_y/ppermute | solution.py:39
  99.8 2.1 %project.3 = (bf16[8,32,512]{2,1,0:T(8,128)(2,1)S(1)}, bf16[8,32,512]{2,1,0:T(8,128)(2,1)S(1)}, bf16[8,32,512]{2,1,0:T(8,128)(2,1)S(1)}, bf16[8,32,512]{2,1,0:T(8,128)(2,1)S(1)}) custom-call(s32[4]{0:T(128)S(1)} %pad_add_fusion.at.refs_0_, bf16[1024,512]{1,0:T(8,128)(2,1)S(1)} %get-tuple-element.80.xt.refs_1_, ...), custom_call_target="tpu_custom_call" | custom-call | flops 1000000000 | bytes 4194304 | tf_op jit(solution)/shard_map/project/pallas_call | solution.py:47
  101.9 1.5 collective-permute-start.29
  103.4 1.6 collective-permute-done.21.refs_3_.refs_1_
  105.0 1.1 collective-permute-start.31
  106.2 5.3 %collective-permute-done.25.refs_2_ = bf16[8,32,512]{2,1,0:T(8,128)(2,1)S(1)} collective-permute-done((bf16[8,32,512]{2,1,0:T(8,128)(2,1)S(1)}, bf16[8,32,512]{2,1,0:T(8,128)(2,1)S(1)}, u32[]{:S(2)}, u32[]{:S(2)}) %collective-permute-start.25) | collective-permute-done | bytes 262176 | tf_op jit(solution)/shard_map/project/partial_over_y/ppermute | solution.py:39
  111.5 2.2 %collective-permute-start.22 = (bf16[1024,128]{1,0:T(8,128)(2,1)S(1)}, bf16[1024,128]{1,0:T(8,128)(2,1)S(1)}, u32[]{:S(2)}, u32[]{:S(2)}) collective-permute-start(bf16[1024,128]{1,0:T(8,128)(2,1)S(1)} %get-tuple-element.83), channel_id=1, source_target_pairs={{0,12},{1,13},{2,14},{3,15},{4,0},{5,1},{6,2},{7,3},{8,4},{9,5},{1... | collective-permute-start | bytes 786440 | tf_op jit(solution)/shard_map/partial_over_z/ppermute | solution.py:39
  114.0 2.4 %collective-permute-done.29.refs_5_ = bf16[8,32,512]{2,1,0:T(8,128)(2,1)S(1)} collective-permute-done((bf16[8,32,512]{2,1,0:T(8,128)(2,1)S(1)}, bf16[8,32,512]{2,1,0:T(8,128)(2,1)S(1)}, u32[]{:S(2)}, u32[]{:S(2)}) %collective-permute-start.29) | collective-permute-done | bytes 262176 | tf_op jit(solution)/shard_map/project/partial_over_y/ppermute | solution.py:39
  116.4 7.1 %collective-permute-start.24 = (bf16[1024,128]{1,0:T(8,128)(2,1)S(1)}, bf16[1024,128]{1,0:T(8,128)(2,1)S(1)}, u32[]{:S(2)}, u32[]{:S(2)}) collective-permute-start(bf16[1024,128]{1,0:T(8,128)(2,1)S(1)} %get-tuple-element.85), channel_id=1, source_target_pairs={{0,4},{1,5},{2,6},{3,7},{4,8},{5,9},{6,10},{7,11},{8,12},{9,13},{1... | collective-permute-start | bytes 786440 | tf_op jit(solution)/shard_map/partial_over_z/ppermute | solution.py:39
  123.5 6.9 %collective-permute-done.24.refs_3_.refs_10_ = bf16[1024,128]{1,0:T(8,128)(2,1)S(1)} collective-permute-done((bf16[1024,128]{1,0:T(8,128)(2,1)S(1)}, bf16[1024,128]{1,0:T(8,128)(2,1)S(1)}, u32[]{:S(2)}, u32[]{:S(2)}) %collective-permute-start.24) | collective-permute-done | bytes 262176 | tf_op jit(solution)/shard_map/partial_over_z/ppermute | solution.py:39
  130.4 1.1 partial_over_z.3
  131.5 10.9 %all-to-all-start = ((bf16[8,32,1024]{2,1,0:T(8,128)(2,1)}), bf16[8,32,1024]{2,1,0:T(8,128)(2,1)S(1)}, u32[]{:S(2)}, u32[]{:S(2)}) async-start(bf16[8,32,1024]{2,1,0:T(8,128)(2,1)} %partial_over_z.3), calls=%async_computation | async-start | bytes 1048576 | tf_op jit(solution)/shard_map/partial_over_z/all_to_all | solution.py:363
  142.4 1.8 %grad_q.1 = bf16[128,4096]{1,0:T(8,128)(2,1)} custom-call(s32[4]{0:T(128)S(1)} %pad_add_fusion.at.refs_0_, bf16[1024,128]{1,0:T(8,128)(2,1)S(1)} %get-tuple-element.59.refs_0_, bf16[1024,128]{1,0:T(8,128)(2,1)S(1)} %collective-permute-done.22.refs_1_.refs_8_, bf16[1024,128]{1,0:T(8,128)(2,1)S(1)} %collective-permute-done.23.refs_2_.refs_9_, ...), custom_call_target="tpu_custom_call" | custom-call | bytes 2097152 | tf_op jit(solution)/shard_map/grad_q/pallas_call | solution.py:47
  144.2 13.9 %all-to-all-done.part = bf16[8,32,1024]{2,1,0:T(8,128)(2,1)S(1)} async-done(((bf16[8,32,1024]{2,1,0:T(8,128)(2,1)}), bf16[8,32,1024]{2,1,0:T(8,128)(2,1)S(1)}, u32[]{:S(2)}, u32[]{:S(2)}) %all-to-all-start) | async-done | bytes 524320 | tf_op jit(solution)/shard_map/partial_over_z/all_to_all | solution.py:363
  158.1 1.3 finish.1
  (47 shorter events, 3.7 us)
Async XLA Ops:
  0.7 0.9 copy-start.3
  1.6 0.9 copy-start.4
  3.2 8.7 %collective-permute-start.1 = (bf16[128,256]{1,0:T(8,128)(2,1)S(1)}, bf16[128,256]{1,0:T(8,128)(2,1)S(1)}, u32[]{:S(2)}, u32[]{:S(2)}) collective-permute-start(bf16[128,256]{1,0:T(8,128)(2,1)S(1)} %get-tuple-element.54), channel_id=1, source_target_pairs={{0,8},{1,9},{2,10},{3,11},{4,12},{5,13},{6,14},{7,15},{8,0},{9,1},... | collective-permute-start | bytes 196616 | tf_op jit(solution)/shard_map/kv_over_x/ppermute | solution.py:39
  6.8 5.1 %collective-permute-start.2 = (bf16[128,256]{1,0:T(8,128)(2,1)S(1)}, bf16[128,256]{1,0:T(8,128)(2,1)S(1)}, u32[]{:S(2)}, u32[]{:S(2)}) collective-permute-start(bf16[128,256]{1,0:T(8,128)(2,1)S(1)} %get-tuple-element.55), channel_id=1, source_target_pairs={{0,12},{1,13},{2,14},{3,15},{4,0},{5,1},{6,2},{7,3},{8,4},{9,5},{1... | collective-permute-start | bytes 196616 | tf_op jit(solution)/shard_map/kv_over_x/ppermute | solution.py:39
  7.7 10.9 %copy-start = (bf16[128,8192]{1,0:T(8,128)(2,1)S(1)}, bf16[128,8192]{1,0:T(8,128)(2,1)}, u32[]{:S(2)}) copy-start(bf16[128,8192]{1,0:T(8,128)(2,1)} %refs_1_.3) | copy-start | bytes 6291460
  7.7 4.6 %collective-permute-start = (bf16[128,256]{1,0:T(8,128)(2,1)S(1)}, bf16[128,256]{1,0:T(8,128)(2,1)S(1)}, u32[]{:S(2)}, u32[]{:S(2)}) collective-permute-start(bf16[128,256]{1,0:T(8,128)(2,1)S(1)} %get-tuple-element.49.refs_3_), channel_id=1, source_target_pairs={{0,4},{1,5},{2,6},{3,7},{4,8},{5,9},{6,10},{7,11},{8,12},{9,13},{1... | collective-permute-start | bytes 196616 | tf_op jit(solution)/shard_map/kv_over_x/ppermute | solution.py:39
  8.3 1.3 copy-start.1
  9.5 1.2 copy-start.2
  12.4 19.9 %copy-start.5 = (s32[1,8]{1,0:T(1,128)S(1)}, s32[1,8]{1,0:T(1,128)}, u32[]{:S(2)}) copy-start(s32[1,8]{1,0:T(1,128)} %param.11) | copy-start | bytes 100
  12.4 19.9 %collective-permute-start.4 = (bf16[2,1024,128]{2,1,0:T(8,128)(2,1)S(1)}, bf16[2,1024,128]{2,1,0:T(8,128)(2,1)S(1)}, u32[]{:S(2)}, u32[]{:S(2)}) collective-permute-start(bf16[2,1024,128]{2,1,0:T(8,128)(2,1)S(1)} %get-tuple-element.57), channel_id=1, source_target_pairs={{0,12},{1,13},{2,14},{3,15},{4,0},{5,1},{6,2},{7,3},{8,4},{9,5},{1... | collective-permute-start | bytes 1572872 | tf_op jit(solution)/shard_map/q_do_over_x/ppermute | solution.py:39
  14.1 18.2 %collective-permute-start.3 = (bf16[2,1024,128]{2,1,0:T(8,128)(2,1)S(1)}, bf16[2,1024,128]{2,1,0:T(8,128)(2,1)S(1)}, u32[]{:S(2)}, u32[]{:S(2)}) collective-permute-start(bf16[2,1024,128]{2,1,0:T(8,128)(2,1)S(1)} %get-tuple-element.56.refs_5_), channel_id=1, source_target_pairs={{0,4},{1,5},{2,6},{3,7},{4,8},{5,9},{6,10},{7,11},{8,12},{9,13},{1... | collective-permute-start | bytes 1572872 | tf_op jit(solution)/shard_map/q_do_over_x/ppermute | solution.py:39
  14.7 8.8 %collective-permute-start.7 = (bf16[512,256]{1,0:T(8,128)(2,1)S(1)}, bf16[512,256]{1,0:T(8,128)(2,1)S(1)}, u32[]{:S(2)}, u32[]{:S(2)}) collective-permute-start(bf16[512,256]{1,0:T(8,128)(2,1)S(1)} %kv_over_x.3.refs_3_.refs_2_), channel_id=1, source_target_pairs={{0,3},{1,0},{2,1},{3,2},{4,7},{5,4},{6,5},{7,6},{8,11},{9,8},{10,9... | collective-permute-start | bytes 786440 | tf_op jit(solution)/shard_map/kv_over_y/ppermute | solution.py:39
  17.5 7.4 %collective-permute-start.6 = (bf16[512,256]{1,0:T(8,128)(2,1)S(1)}, bf16[512,256]{1,0:T(8,128)(2,1)S(1)}, u32[]{:S(2)}, u32[]{:S(2)}) collective-permute-start(bf16[512,256]{1,0:T(8,128)(2,1)S(1)} %kv_over_x.3.refs_3_.refs_2_), channel_id=1, source_target_pairs={{0,2},{1,3},{2,0},{3,1},{4,6},{5,7},{6,4},{7,5},{8,10},{9,11},{10,... | collective-permute-start | bytes 786440 | tf_op jit(solution)/shard_map/kv_over_y/ppermute | solution.py:39
  17.9 14.4 %collective-permute-start.5 = (bf16[512,256]{1,0:T(8,128)(2,1)S(1)}, bf16[512,256]{1,0:T(8,128)(2,1)S(1)}, u32[]{:S(2)}, u32[]{:S(2)}) collective-permute-start(bf16[512,256]{1,0:T(8,128)(2,1)S(1)} %kv_over_x.3.refs_3_.refs_2_), channel_id=1, source_target_pairs={{0,1},{1,2},{2,3},{3,0},{4,5},{5,6},{6,7},{7,4},{8,9},{9,10},{10,1... | collective-permute-start | bytes 786440 | tf_op jit(solution)/shard_map/kv_over_y/ppermute | solution.py:39
  23.6 16.5 %collective-permute-start.8 = (bf16[2,1024,128]{2,1,0:T(8,128)(2,1)S(1)}, bf16[2,1024,128]{2,1,0:T(8,128)(2,1)S(1)}, u32[]{:S(2)}, u32[]{:S(2)}) collective-permute-start(bf16[2,1024,128]{2,1,0:T(8,128)(2,1)S(1)} %get-tuple-element.61), channel_id=1, source_target_pairs={{0,8},{1,9},{2,10},{3,11},{4,12},{5,13},{6,14},{7,15},{8,0},{9,1},... | collective-permute-start | bytes 1572872 | tf_op jit(solution)/shard_map/q_do_over_x/ppermute | solution.py:39
  45.7 10.0 %collective-permute-start.12 = (bf16[512,256]{1,0:T(8,128)(2,1)S(1)}, bf16[512,256]{1,0:T(8,128)(2,1)S(1)}, u32[]{:S(2)}, u32[]{:S(2)}) collective-permute-start(bf16[512,256]{1,0:T(8,128)(2,1)S(1)} %get-tuple-element.77), channel_id=1, source_target_pairs={{0,1},{1,2},{2,3},{3,0},{4,5},{5,6},{6,7},{7,4},{8,9},{9,10},{10,1... | collective-permute-start | bytes 786440 | tf_op jit(solution)/shard_map/terms_over_y/ppermute | solution.py:39
  45.9 10.2 %collective-permute-start.9 = (bf16[2,128,1024]{2,1,0:T(8,128)(2,1)S(1)}, bf16[2,128,1024]{2,1,0:T(8,128)(2,1)S(1)}, u32[]{:S(2)}, u32[]{:S(2)}) collective-permute-start(bf16[2,128,1024]{2,1,0:T(8,128)(2,1)S(1)} %get-tuple-element.74), channel_id=1, source_target_pairs={{0,4},{1,5},{2,6},{3,7},{4,8},{5,9},{6,10},{7,11},{8,12},{9,13},{1... | collective-permute-start | bytes 1572872 | tf_op jit(solution)/shard_map/terms_over_y/ppermute | solution.py:39
  46.2 9.5 %collective-permute-start.13 = (bf16[512,256]{1,0:T(8,128)(2,1)S(1)}, bf16[512,256]{1,0:T(8,128)(2,1)S(1)}, u32[]{:S(2)}, u32[]{:S(2)}) collective-permute-start(bf16[512,256]{1,0:T(8,128)(2,1)S(1)} %get-tuple-element.78), channel_id=1, source_target_pairs={{0,2},{1,3},{2,0},{3,1},{4,6},{5,7},{6,4},{7,5},{8,10},{9,11},{10,... | collective-permute-start | bytes 786440 | tf_op jit(solution)/shard_map/terms_over_y/ppermute | solution.py:39
  49.5 6.6 %collective-permute-start.14 = (bf16[512,256]{1,0:T(8,128)(2,1)S(1)}, bf16[512,256]{1,0:T(8,128)(2,1)S(1)}, u32[]{:S(2)}, u32[]{:S(2)}) collective-permute-start(bf16[512,256]{1,0:T(8,128)(2,1)S(1)} %get-tuple-element.79), channel_id=1, source_target_pairs={{0,3},{1,0},{2,1},{3,2},{4,7},{5,4},{6,5},{7,6},{8,11},{9,8},{10,9... | collective-permute-start | bytes 786440 | tf_op jit(solution)/shard_map/terms_over_y/ppermute | solution.py:39
  51.6 15.1 %collective-permute-start.10 = (bf16[2,128,1024]{2,1,0:T(8,128)(2,1)S(1)}, bf16[2,128,1024]{2,1,0:T(8,128)(2,1)S(1)}, u32[]{:S(2)}, u32[]{:S(2)}) collective-permute-start(bf16[2,128,1024]{2,1,0:T(8,128)(2,1)S(1)} %get-tuple-element.75), channel_id=1, source_target_pairs={{0,8},{1,9},{2,10},{3,11},{4,12},{5,13},{6,14},{7,15},{8,0},{9,1},... | collective-permute-start | bytes 1572872 | tf_op jit(solution)/shard_map/terms_over_y/ppermute | solution.py:39
  55.7 12.0 %collective-permute-start.11 = (bf16[2,128,1024]{2,1,0:T(8,128)(2,1)S(1)}, bf16[2,128,1024]{2,1,0:T(8,128)(2,1)S(1)}, u32[]{:S(2)}, u32[]{:S(2)}) collective-permute-start(bf16[2,128,1024]{2,1,0:T(8,128)(2,1)S(1)} %get-tuple-element.76), channel_id=1, source_target_pairs={{0,12},{1,13},{2,14},{3,15},{4,0},{5,1},{6,2},{7,3},{8,4},{9,5},{1... | collective-permute-start | bytes 1572872 | tf_op jit(solution)/shard_map/terms_over_y/ppermute | solution.py:39
  56.2 23.0 %collective-permute-start.17 = (bf16[512,256]{1,0:T(8,128)(2,1)S(1)}, bf16[512,256]{1,0:T(8,128)(2,1)S(1)}, u32[]{:S(2)}, u32[]{:S(2)}) collective-permute-start(bf16[512,256]{1,0:T(8,128)(2,1)S(1)} %terms_over_y.3.refs_0_), channel_id=1, source_target_pairs={{0,12},{1,13},{2,14},{3,15},{4,0},{5,1},{6,2},{7,3},{8,4},{9,5},{1... | collective-permute-start | bytes 786440 | tf_op jit(solution)/shard_map/dkv_over_x/ppermute | solution.py:39
  59.7 19.6 %collective-permute-start.16 = (bf16[512,256]{1,0:T(8,128)(2,1)S(1)}, bf16[512,256]{1,0:T(8,128)(2,1)S(1)}, u32[]{:S(2)}, u32[]{:S(2)}) collective-permute-start(bf16[512,256]{1,0:T(8,128)(2,1)S(1)} %terms_over_y.3.refs_0_), channel_id=1, source_target_pairs={{0,8},{1,9},{2,10},{3,11},{4,12},{5,13},{6,14},{7,15},{8,0},{9,1},... | collective-permute-start | bytes 786440 | tf_op jit(solution)/shard_map/dkv_over_x/ppermute | solution.py:39
  63.9 16.4 %collective-permute-start.15 = (bf16[512,256]{1,0:T(8,128)(2,1)S(1)}, bf16[512,256]{1,0:T(8,128)(2,1)S(1)}, u32[]{:S(2)}, u32[]{:S(2)}) collective-permute-start(bf16[512,256]{1,0:T(8,128)(2,1)S(1)} %terms_over_y.3.refs_0_), channel_id=1, source_target_pairs={{0,4},{1,5},{2,6},{3,7},{4,8},{5,9},{6,10},{7,11},{8,12},{9,13},{1... | collective-permute-start | bytes 786440 | tf_op jit(solution)/shard_map/dkv_over_x/ppermute | solution.py:39
  81.4 12.0 %collective-permute-start.18 = (bf16[1024,512]{1,0:T(8,128)(2,1)S(1)}, bf16[1024,512]{1,0:T(8,128)(2,1)S(1)}, u32[]{:S(2)}, u32[]{:S(2)}) collective-permute-start(bf16[1024,512]{1,0:T(8,128)(2,1)S(1)} %get-tuple-element.81), channel_id=1, source_target_pairs={{0,16},{1,17},{2,18},{3,19},{4,20},{5,21},{6,22},{7,23},{8,24},{9,... | collective-permute-start | bytes 3145736 | tf_op jit(solution)/shard_map/turn_x/ppermute | solution.py:39
  90.4 2.7 %collective-permute-start.19 = (bf16[512,256]{1,0:T(8,128)(2,1)S(1)}, bf16[512,256]{1,0:T(8,128)(2,1)S(1)}, u32[]{:S(2)}, u32[]{:S(2)}) collective-permute-start(bf16[512,256]{1,0:T(8,128)(2,1)S(1)} %terms_over_y.3.refs_0_), channel_id=1, source_target_pairs={{0,16},{1,17},{2,18},{3,19},{4,20},{5,21},{6,22},{7,23},{8,24},{9,... | collective-permute-start | bytes 786440 | tf_op jit(solution)/shard_map/dkv_over_x/ppermute | solution.py:39
  90.5 2.9 %collective-permute-start.20 = (bf16[512,256]{1,0:T(8,128)(2,1)S(1)}, bf16[512,256]{1,0:T(8,128)(2,1)S(1)}, u32[]{:S(2)}, u32[]{:S(2)}) collective-permute-start(bf16[512,256]{1,0:T(8,128)(2,1)S(1)} %collective-permute-done.15.refs_5_.refs_1_), channel_id=1, source_target_pairs={{0,16},{1,17},{2,18},{3,19},{4,20},{5,21},{6,22},{7,23},{8,24},{9,... | collective-permute-start | bytes 786440 | tf_op jit(solution)/shard_map/dkv_over_x/ppermute | solution.py:39
  90.9 9.0 %collective-permute-start.28 = (bf16[512,256]{1,0:T(8,128)(2,1)S(1)}, bf16[512,256]{1,0:T(8,128)(2,1)S(1)}, u32[]{:S(2)}, u32[]{:S(2)}) collective-permute-start(bf16[512,256]{1,0:T(8,128)(2,1)S(1)} %collective-permute-done.17.refs_7_.refs_4_), channel_id=1, source_target_pairs={{0,16},{1,17},{2,18},{3,19},{4,20},{5,21},{6,22},{7,23},{8,24},{9,... | collective-permute-start | bytes 786440 | tf_op jit(solution)/shard_map/dkv_over_x/ppermute | solution.py:39
  91.0 8.9 %collective-permute-start.27 = (bf16[512,256]{1,0:T(8,128)(2,1)S(1)}, bf16[512,256]{1,0:T(8,128)(2,1)S(1)}, u32[]{:S(2)}, u32[]{:S(2)}) collective-permute-start(bf16[512,256]{1,0:T(8,128)(2,1)S(1)} %collective-permute-done.16.refs_6_.refs_3_), channel_id=1, source_target_pairs={{0,16},{1,17},{2,18},{3,19},{4,20},{5,21},{6,22},{7,23},{8,24},{9,... | collective-permute-start | bytes 786440 | tf_op jit(solution)/shard_map/dkv_over_x/ppermute | solution.py:39
  95.5 9.6 %collective-permute-start.21 = (bf16[8,32,512]{2,1,0:T(8,128)(2,1)S(1)}, bf16[8,32,512]{2,1,0:T(8,128)(2,1)S(1)}, u32[]{:S(2)}, u32[]{:S(2)}) collective-permute-start(bf16[8,32,512]{2,1,0:T(8,128)(2,1)S(1)} %get-tuple-element.82), channel_id=1, source_target_pairs={{0,1},{1,2},{2,3},{3,0},{4,5},{5,6},{6,7},{7,4},{8,9},{9,10},{10,1... | collective-permute-start | bytes 786440 | tf_op jit(solution)/shard_map/project/partial_over_y/ppermute | solution.py:39
  96.3 15.2 %collective-permute-start.25 = (bf16[8,32,512]{2,1,0:T(8,128)(2,1)S(1)}, bf16[8,32,512]{2,1,0:T(8,128)(2,1)S(1)}, u32[]{:S(2)}, u32[]{:S(2)}) collective-permute-start(bf16[8,32,512]{2,1,0:T(8,128)(2,1)S(1)} %get-tuple-element.87), channel_id=1, source_target_pairs={{0,2},{1,3},{2,0},{3,1},{4,6},{5,7},{6,4},{7,5},{8,10},{9,11},{10,... | collective-permute-start | bytes 786440 | tf_op jit(solution)/shard_map/project/partial_over_y/ppermute | solution.py:39
  99.8 13.9 %collective-permute-start.26 = (bf16[8,32,512]{2,1,0:T(8,128)(2,1)S(1)}, bf16[8,32,512]{2,1,0:T(8,128)(2,1)S(1)}, u32[]{:S(2)}, u32[]{:S(2)}) collective-permute-start(bf16[8,32,512]{2,1,0:T(8,128)(2,1)S(1)} %get-tuple-element.88), channel_id=1, source_target_pairs={{0,3},{1,0},{2,1},{3,2},{4,7},{5,4},{6,5},{7,6},{8,11},{9,8},{10,9... | collective-permute-start | bytes 786440 | tf_op jit(solution)/shard_map/project/partial_over_y/ppermute | solution.py:39
  101.9 14.5 %collective-permute-start.29 = (bf16[8,32,512]{2,1,0:T(8,128)(2,1)S(1)}, bf16[8,32,512]{2,1,0:T(8,128)(2,1)S(1)}, u32[]{:S(2)}, u32[]{:S(2)}) collective-permute-start(bf16[8,32,512]{2,1,0:T(8,128)(2,1)S(1)} %get-tuple-element.90), channel_id=1, source_target_pairs={{0,1},{1,2},{2,3},{3,0},{4,5},{5,6},{6,7},{7,4},{8,9},{9,10},{10,1... | collective-permute-start | bytes 786440 | tf_op jit(solution)/shard_map/project/partial_over_y/ppermute | solution.py:39
  103.4 20.0 %collective-permute-start.30 = (bf16[8,32,512]{2,1,0:T(8,128)(2,1)S(1)}, bf16[8,32,512]{2,1,0:T(8,128)(2,1)S(1)}, u32[]{:S(2)}, u32[]{:S(2)}) collective-permute-start(bf16[8,32,512]{2,1,0:T(8,128)(2,1)S(1)} %get-tuple-element.91), channel_id=1, source_target_pairs={{0,2},{1,3},{2,0},{3,1},{4,6},{5,7},{6,4},{7,5},{8,10},{9,11},{10,... | collective-permute-start | bytes 786440 | tf_op jit(solution)/shard_map/project/partial_over_y/ppermute | solution.py:39
  105.0 18.5 %collective-permute-start.31 = (bf16[8,32,512]{2,1,0:T(8,128)(2,1)S(1)}, bf16[8,32,512]{2,1,0:T(8,128)(2,1)S(1)}, u32[]{:S(2)}, u32[]{:S(2)}) collective-permute-start(bf16[8,32,512]{2,1,0:T(8,128)(2,1)S(1)} %get-tuple-element.92), channel_id=1, source_target_pairs={{0,3},{1,0},{2,1},{3,2},{4,7},{5,4},{6,5},{7,6},{8,11},{9,8},{10,9... | collective-permute-start | bytes 786440 | tf_op jit(solution)/shard_map/project/partial_over_y/ppermute | solution.py:39
  111.5 11.9 %collective-permute-start.22 = (bf16[1024,128]{1,0:T(8,128)(2,1)S(1)}, bf16[1024,128]{1,0:T(8,128)(2,1)S(1)}, u32[]{:S(2)}, u32[]{:S(2)}) collective-permute-start(bf16[1024,128]{1,0:T(8,128)(2,1)S(1)} %get-tuple-element.83), channel_id=1, source_target_pairs={{0,12},{1,13},{2,14},{3,15},{4,0},{5,1},{6,2},{7,3},{8,4},{9,5},{1... | collective-permute-start | bytes 786440 | tf_op jit(solution)/shard_map/partial_over_z/ppermute | solution.py:39
  113.7 9.7 %collective-permute-start.23 = (bf16[1024,128]{1,0:T(8,128)(2,1)S(1)}, bf16[1024,128]{1,0:T(8,128)(2,1)S(1)}, u32[]{:S(2)}, u32[]{:S(2)}) collective-permute-start(bf16[1024,128]{1,0:T(8,128)(2,1)S(1)} %get-tuple-element.84), channel_id=1, source_target_pairs={{0,8},{1,9},{2,10},{3,11},{4,12},{5,13},{6,14},{7,15},{8,0},{9,1},... | collective-permute-start | bytes 786440 | tf_op jit(solution)/shard_map/partial_over_z/ppermute | solution.py:39
  116.4 14.1 %collective-permute-start.24 = (bf16[1024,128]{1,0:T(8,128)(2,1)S(1)}, bf16[1024,128]{1,0:T(8,128)(2,1)S(1)}, u32[]{:S(2)}, u32[]{:S(2)}) collective-permute-start(bf16[1024,128]{1,0:T(8,128)(2,1)S(1)} %get-tuple-element.85), channel_id=1, source_target_pairs={{0,4},{1,5},{2,6},{3,7},{4,8},{5,9},{6,10},{7,11},{8,12},{9,13},{1... | collective-permute-start | bytes 786440 | tf_op jit(solution)/shard_map/partial_over_z/ppermute | solution.py:39
  131.5 26.6 %all-to-all-start = ((bf16[8,32,1024]{2,1,0:T(8,128)(2,1)}), bf16[8,32,1024]{2,1,0:T(8,128)(2,1)S(1)}, u32[]{:S(2)}, u32[]{:S(2)}) async-start(bf16[8,32,1024]{2,1,0:T(8,128)(2,1)} %partial_over_z.3), calls=%async_computation | async-start | bytes 1048576 | tf_op jit(solution)/shard_map/partial_over_z/all_to_all | solution.py:363

commit v5 on v4

--- a/solution.py
+++ b/solution.py
@@ -337,9 +337,9 @@
         (dkv,) = call(sum_kernel, [sds((512, 256))], terms, moved=5 << 18, smem=0, late=[xp[1]])
     with jax.named_scope("dkv_over_x"):
         own = [dkv] + [send(dkv, dx=s) for s in range(1, NX)]
-        other = [send(piece, dc=1) for piece in own]
+        other = [send(piece, dc=1) for piece in own[:2]]
     with jax.named_scope("turn_x"):
-        xt, xt_give = call(turn_x_kernel, [sds((1024, 512))] * 2, (at, *xp), moved=1 << 22, late=own[1:])
+        xt, xt_give = call(turn_x_kernel, [sds((1024, 512))] * 2, (at, *xp), moved=1 << 22, late=own[1:2])
         xt_other = send(xt_give, dc=1)
     with jax.named_scope("project"):
         parts = []
@@ -356,8 +356,10 @@
             )
             with jax.named_scope("partial_over_y"):
                 parts += [partial[0]] + [send(partial[s], dy=s) for s in range(1, NY)]
+            if len(other) == 2:
+                other += [send(piece, dc=1) for piece in after(own[2:], parts[1:])]
     with jax.named_scope("partial_over_z"):
-        dq = [dq[0]] + [send(d, dx=-s - 1) for s, d in enumerate(after(dq[1:], [parts[1]]))]
+        dq = [dq[0]] + [send(d, dx=-s - 1) for s, d in enumerate(after(dq[1:], [parts[5]]))]
         (summed,) = call(add_kernel, [sds((NZ, 32, 1024))], parts, moved=5 << 20, smem=0, late=dq[1:])
         groups = [[z * NC + c for z in range(NZ)] for c in range(NC)]
         last = lax.all_to_all(summed, "dp", 0, 0, axis_index_groups=groups, tiled=True)

time: 159 us -> 166 us (1.044)
  waiting for transfers between devices: 60.5 us -> 68.6 us
    ppermute x32, waiting for transfers between devices: 46.6 us -> 52.5 us  [send(): return lax.ppermute(value, AXES, pairs)]
    all_to_all x1, starting transfers between devices: 10.9 us -> 8.56 us  [on_device(): lax.all_to_all(summed, 'dp', 0, 0, axis_index_groups=groups, tiled=True)]
    all_to_all x1, waiting for transfers between devices: 13.9 us -> 16.1 us  [on_device(): lax.all_to_all(summed, 'dp', 0, 0, axis_index_groups=groups, tiled=True)]
    pallas_call x16 -> x17, Pallas kernels: 26.5 us -> 26.5 us  [call(): pl.pallas_call(body, out_shape=outs, in_specs=[SM] * smem + [VM] * (len(i...]
  transfers between devices with their start and end apart: 33 -> 33, of which waited for: 15 -> 19; matrix products, arithmetic and copies ran while one was open for 0% -> 0% of each run, Pallas kernels for 10% -> 10%
where the time goes in v5:
time: 166 us
  waiting for transfers between devices  68.6 us (41%)
  starting transfers between devices  65.9 us (40%)
  Pallas kernels  26.5 us (16%)
  local copies, waits for them, and re-layouts  4.3 us (3%)
    ppermute x32, starting transfers between devices, send(): return lax.ppermute(value, AXES, pairs)  57.3 us
    ppermute x32, waiting for transfers between devices, send(): return lax.ppermute(value, AXES, pairs)  52.5 us
    pallas_call x17, Pallas kernels, call(): pl.pallas_call(body, out_shape=outs, in_specs=[SM] * smem + [VM] * (len(i...  26.5 us
    all_to_all x1, waiting for transfers between devices, on_device(): lax.all_to_all(summed, 'dp', 0, 0, axis_index_groups=groups, tiled=True)  16.1 us
    all_to_all x1, starting transfers between devices, on_device(): lax.all_to_all(summed, 'dp', 0, 0, axis_index_groups=groups, tiled=True)  8.56 us
    unnamed x12, local copies, waits for them, and re-layouts  4.3 us
  transfers between devices with their start and end apart: 33, of which 19 were waited for; matrix products, arithmetic and copies ran while one was open for 0% of the time, Pallas kernels for 10%

profile of v5, /device:TPU:1, one launch (start us, length us, event | category | flops | bytes accessed | tf_op | source)
XLA Modules:
  0.0 166.2 jit_solution(143022709136349486)
XLA Ops:
  0.7 0.9 copy-done.3
  1.7 0.9 copy-done.4
  3.2 3.7 %collective-permute-start.1 = (bf16[128,256]{1,0:T(8,128)(2,1)S(1)}, bf16[128,256]{1,0:T(8,128)(2,1)S(1)}, u32[]{:S(2)}, u32[]{:S(2)}) collective-permute-start(bf16[128,256]{1,0:T(8,128)(2,1)S(1)} %get-tuple-element.56), channel_id=1, source_target_pairs={{0,8},{1,9},{2,10},{3,11},{4,12},{5,13},{6,14},{7,15},{8,0},{9,1},... | collective-permute-start | bytes 196616 | tf_op jit(solution)/shard_map/kv_over_x/ppermute | solution.py:39
  6.8 0.9 collective-permute-start.2
  8.3 1.3 copy-done.1
  9.5 1.2 copy-done.2
  10.8 1.1 pack_q_do.1
  12.4 1.8 %collective-permute-start.4 = (bf16[2,1024,128]{2,1,0:T(8,128)(2,1)S(1)}, bf16[2,1024,128]{2,1,0:T(8,128)(2,1)S(1)}, u32[]{:S(2)}, u32[]{:S(2)}) collective-permute-start(bf16[2,1024,128]{2,1,0:T(8,128)(2,1)S(1)} %get-tuple-element.59), channel_id=1, source_target_pairs={{0,12},{1,13},{2,14},{3,15},{4,0},{5,1},{6,2},{7,3},{8,4},{9,5},{1... | collective-permute-start | bytes 1572872 | tf_op jit(solution)/shard_map/q_do_over_x/ppermute | solution.py:39
  14.7 2.8 %collective-permute-start.7 = (bf16[512,256]{1,0:T(8,128)(2,1)S(1)}, bf16[512,256]{1,0:T(8,128)(2,1)S(1)}, u32[]{:S(2)}, u32[]{:S(2)}) collective-permute-start(bf16[512,256]{1,0:T(8,128)(2,1)S(1)} %kv_over_x.3.refs_3_.refs_2_), channel_id=1, source_target_pairs={{0,3},{1,0},{2,1},{3,2},{4,7},{5,4},{6,5},{7,6},{8,11},{9,8},{10,9... | collective-permute-start | bytes 786440 | tf_op jit(solution)/shard_map/kv_over_y/ppermute | solution.py:39
  17.9 0.7 collective-permute-start.5
  18.6 1.1 pack_x.1
  19.7 3.9 %collective-permute-done.7.refs_6_ = bf16[512,256]{1,0:T(8,128)(2,1)S(1)} collective-permute-done((bf16[512,256]{1,0:T(8,128)(2,1)S(1)}, bf16[512,256]{1,0:T(8,128)(2,1)S(1)}, u32[]{:S(2)}, u32[]{:S(2)}) %collective-permute-start.7) | collective-permute-done | bytes 262176 | tf_op jit(solution)/shard_map/kv_over_y/ppermute | solution.py:39
  23.6 1.3 collective-permute-start.8
  24.9 7.4 %collective-permute-done.5.refs_4_ = bf16[512,256]{1,0:T(8,128)(2,1)S(1)} collective-permute-done((bf16[512,256]{1,0:T(8,128)(2,1)S(1)}, bf16[512,256]{1,0:T(8,128)(2,1)S(1)}, u32[]{:S(2)}, u32[]{:S(2)}) %collective-permute-start.5) | collective-permute-done | bytes 262176 | tf_op jit(solution)/shard_map/kv_over_y/ppermute | solution.py:39
  32.3 10.0 %attention.2 = (bf16[1024,128]{1,0:T(8,128)(2,1)S(1)}, bf16[1024,128]{1,0:T(8,128)(2,1)S(1)}, bf16[1024,128]{1,0:T(8,128)(2,1)S(1)}, f32[2048,128]{1,0:T(8,128)S...) custom-call(s32[4]{0:T(128)S(1)} %pad_add_fusion.at.refs_0_, ...), custom_call_target="tpu_custom_call" | custom-call | flops 12000000000 | bytes 6291456 | tf_op jit(solution)/shard_map/attention/pallas_call | solution.py:47
  42.3 3.4 %attention.3 = (bf16[1024,128]{1,0:T(8,128)(2,1)S(1)}, bf16[512,256]{1,0:T(8,128)(2,1)S(1)}, bf16[512,256]{1,0:T(8,128)(2,1)S(1)}, bf16[512,256]{1,0:T(8,128)(2,1)S(1)}, bf16[512,256]{1,0:T(8,128)(2,1)S(1)}) custom-call(s32[4]{0:T(128)S(1)} %pad_add_fusion.at.refs_0_, s32[8]{0:T(128)S(1)} %bitcast.6, ...), custom_call_target="tpu_custom_call" | custom-call | flops 4000000000 | bytes 6291456 | tf_op jit(solution)/shard_map/attention/pallas_call | solution.py:47
  46.2 3.3 %collective-permute-start.13 = (bf16[512,256]{1,0:T(8,128)(2,1)S(1)}, bf16[512,256]{1,0:T(8,128)(2,1)S(1)}, u32[]{:S(2)}, u32[]{:S(2)}) collective-permute-start(bf16[512,256]{1,0:T(8,128)(2,1)S(1)} %get-tuple-element.80), channel_id=1, source_target_pairs={{0,2},{1,3},{2,0},{3,1},{4,6},{5,7},{6,4},{7,5},{8,10},{9,11},{10,... | collective-permute-start | bytes 786440 | tf_op jit(solution)/shard_map/terms_over_y/ppermute | solution.py:39
  49.5 2.1 %collective-permute-start.14 = (bf16[512,256]{1,0:T(8,128)(2,1)S(1)}, bf16[512,256]{1,0:T(8,128)(2,1)S(1)}, u32[]{:S(2)}, u32[]{:S(2)}) collective-permute-start(bf16[512,256]{1,0:T(8,128)(2,1)S(1)} %get-tuple-element.81), channel_id=1, source_target_pairs={{0,3},{1,0},{2,1},{3,2},{4,7},{5,4},{6,5},{7,6},{8,11},{9,8},{10,9... | collective-permute-start | bytes 786440 | tf_op jit(solution)/shard_map/terms_over_y/ppermute | solution.py:39
  51.6 4.2 %collective-permute-start.10 = (bf16[2,128,1024]{2,1,0:T(8,128)(2,1)S(1)}, bf16[2,128,1024]{2,1,0:T(8,128)(2,1)S(1)}, u32[]{:S(2)}, u32[]{:S(2)}) collective-permute-start(bf16[2,128,1024]{2,1,0:T(8,128)(2,1)S(1)} %get-tuple-element.77), channel_id=1, source_target_pairs={{0,8},{1,9},{2,10},{3,11},{4,12},{5,13},{6,14},{7,15},{8,0},{9,1},... | collective-permute-start | bytes 1572872 | tf_op jit(solution)/shard_map/terms_over_y/ppermute | solution.py:39
  56.2 5.6 %collective-permute-start.15 = (bf16[512,256]{1,0:T(8,128)(2,1)S(1)}, bf16[512,256]{1,0:T(8,128)(2,1)S(1)}, u32[]{:S(2)}, u32[]{:S(2)}) collective-permute-start(bf16[512,256]{1,0:T(8,128)(2,1)S(1)} %terms_over_y.3.refs_0_), channel_id=1, source_target_pairs={{0,4},{1,5},{2,6},{3,7},{4,8},{5,9},{6,10},{7,11},{8,12},{9,13},{1... | collective-permute-start | bytes 786440 | tf_op jit(solution)/shard_map/dkv_over_x/ppermute | solution.py:39
  61.9 3.8 %collective-permute-done.10.refs_3_ = bf16[2,128,1024]{2,1,0:T(8,128)(2,1)S(1)} collective-permute-done((bf16[2,128,1024]{2,1,0:T(8,128)(2,1)S(1)}, bf16[2,128,1024]{2,1,0:T(8,128)(2,1)S(1)}, u32[]{:S(2)}, u32[]{:S(2)}) %collective-permute-start.10) | collective-permute-done | bytes 524320 | tf_op jit(solution)/shard_map/terms_over_y/ppermute | solution.py:39
  65.6 2.9 %collective-permute-done.11.refs_4_ = bf16[2,128,1024]{2,1,0:T(8,128)(2,1)S(1)} collective-permute-done((bf16[2,128,1024]{2,1,0:T(8,128)(2,1)S(1)}, bf16[2,128,1024]{2,1,0:T(8,128)(2,1)S(1)}, u32[]{:S(2)}, u32[]{:S(2)}) %collective-permute-start.11) | collective-permute-done | bytes 524320 | tf_op jit(solution)/shard_map/terms_over_y/ppermute | solution.py:39
  68.5 2.7 %collective-permute-done.15.refs_5_.refs_1_ = bf16[512,256]{1,0:T(8,128)(2,1)S(1)} collective-permute-done((bf16[512,256]{1,0:T(8,128)(2,1)S(1)}, bf16[512,256]{1,0:T(8,128)(2,1)S(1)}, u32[]{:S(2)}, u32[]{:S(2)}) %collective-permute-start.15) | collective-permute-done | bytes 262176 | tf_op jit(solution)/shard_map/dkv_over_x/ppermute | solution.py:39
  71.2 1.1 turn_x.1
  72.4 14.2 %collective-permute-start.16 = (bf16[1024,512]{1,0:T(8,128)(2,1)S(1)}, bf16[1024,512]{1,0:T(8,128)(2,1)S(1)}, u32[]{:S(2)}, u32[]{:S(2)}) collective-permute-start(bf16[1024,512]{1,0:T(8,128)(2,1)S(1)} %get-tuple-element.83), channel_id=1, source_target_pairs={{0,16},{1,17},{2,18},{3,19},{4,20},{5,21},{6,22},{7,23},{8,24},{9,... | collective-permute-start | bytes 3145736 | tf_op jit(solution)/shard_map/turn_x/ppermute | solution.py:39
  87.4 1.8 %collective-permute-done.19.refs_2_ = bf16[512,256]{1,0:T(8,128)(2,1)S(1)} collective-permute-done((bf16[512,256]{1,0:T(8,128)(2,1)S(1)}, bf16[512,256]{1,0:T(8,128)(2,1)S(1)}, u32[]{:S(2)}, u32[]{:S(2)}) %collective-permute-start.19) | collective-permute-done | bytes 262176 | tf_op jit(solution)/shard_map/dkv_over_x/ppermute | solution.py:39
  89.6 2.0 %project.3 = (bf16[8,32,512]{2,1,0:T(8,128)(2,1)S(1)}, bf16[8,32,512]{2,1,0:T(8,128)(2,1)S(1)}, bf16[8,32,512]{2,1,0:T(8,128)(2,1)S(1)}, bf16[8,32,512]{2,1,0:T(8,128)(2,1)S(1)}) custom-call(s32[4]{0:T(128)S(1)} %pad_add_fusion.at.refs_0_, bf16[1024,512]{1,0:T(8,128)(2,1)S(1)} %get-tuple-element.82.xt.refs_1_, ...), custom_call_target="tpu_custom_call" | custom-call | flops 1000000000 | bytes 4194304 | tf_op jit(solution)/shard_map/project/pallas_call | solution.py:47
  91.6 3.4 %collective-permute-start.21 = (bf16[8,32,512]{2,1,0:T(8,128)(2,1)S(1)}, bf16[8,32,512]{2,1,0:T(8,128)(2,1)S(1)}, u32[]{:S(2)}, u32[]{:S(2)}) collective-permute-start(bf16[8,32,512]{2,1,0:T(8,128)(2,1)S(1)} %get-tuple-element.84), channel_id=1, source_target_pairs={{0,1},{1,2},{2,3},{3,0},{4,5},{5,6},{6,7},{7,4},{8,9},{9,10},{10,1... | collective-permute-start | bytes 786440 | tf_op jit(solution)/shard_map/project/partial_over_y/ppermute | solution.py:39
  95.0 0.8 collective-permute-start.22
  95.9 1.7 %collective-permute-start.23 = (bf16[8,32,512]{2,1,0:T(8,128)(2,1)S(1)}, bf16[8,32,512]{2,1,0:T(8,128)(2,1)S(1)}, u32[]{:S(2)}, u32[]{:S(2)}) collective-permute-start(bf16[8,32,512]{2,1,0:T(8,128)(2,1)S(1)} %get-tuple-element.86), channel_id=1, source_target_pairs={{0,3},{1,0},{2,1},{3,2},{4,7},{5,4},{6,5},{7,6},{8,11},{9,8},{10,9... | collective-permute-start | bytes 786440 | tf_op jit(solution)/shard_map/project/partial_over_y/ppermute | solution.py:39
  97.6 3.5 %collective-permute-done.21.refs_2_.refs_1_ = bf16[8,32,512]{2,1,0:T(8,128)(2,1)S(1)} collective-permute-done((bf16[8,32,512]{2,1,0:T(8,128)(2,1)S(1)}, bf16[8,32,512]{2,1,0:T(8,128)(2,1)S(1)}, u32[]{:S(2)}, u32[]{:S(2)}) %collective-permute-start.21) | collective-permute-done | bytes 262176 | tf_op jit(solution)/shard_map/project/partial_over_y/ppermute | solution.py:39
  101.0 6.5 %collective-permute-done.22.refs_3_.refs_2_ = bf16[8,32,512]{2,1,0:T(8,128)(2,1)S(1)} collective-permute-done((bf16[8,32,512]{2,1,0:T(8,128)(2,1)S(1)}, bf16[8,32,512]{2,1,0:T(8,128)(2,1)S(1)}, u32[]{:S(2)}, u32[]{:S(2)}) %collective-permute-start.22) | collective-permute-done | bytes 262176 | tf_op jit(solution)/shard_map/project/partial_over_y/ppermute | solution.py:39
  107.6 1.3 collective-permute-start.24
  109.2 0.8 collective-permute-done.24.refs_5_
  110.4 2.1 %project.5 = (bf16[8,32,512]{2,1,0:T(8,128)(2,1)S(1)}, bf16[8,32,512]{2,1,0:T(8,128)(2,1)S(1)}, bf16[8,32,512]{2,1,0:T(8,128)(2,1)S(1)}, bf16[8,32,512]{2,1,0:T(8,128)(2,1)S(1)}) custom-call(s32[4]{0:T(128)S(1)} %pad_add_fusion.at.refs_0_, bf16[1024,512]{1,0:T(8,128)(2,1)S(1)} %get-tuple-element.82.xt.refs_1_, ...), custom_call_target="tpu_custom_call" | custom-call | flops 1000000000 | bytes 4194304 | tf_op jit(solution)/shard_map/project/pallas_call | solution.py:47
  112.5 1.9 %collective-permute-start.26 = (bf16[8,32,512]{2,1,0:T(8,128)(2,1)S(1)}, bf16[8,32,512]{2,1,0:T(8,128)(2,1)S(1)}, u32[]{:S(2)}, u32[]{:S(2)}) collective-permute-start(bf16[8,32,512]{2,1,0:T(8,128)(2,1)S(1)} %get-tuple-element.90), channel_id=1, source_target_pairs={{0,1},{1,2},{2,3},{3,0},{4,5},{5,6},{6,7},{7,4},{8,9},{9,10},{10,1... | collective-permute-start | bytes 786440 | tf_op jit(solution)/shard_map/project/partial_over_y/ppermute | solution.py:39
  114.3 1.3 collective-permute-start.30
  115.6 1.9 %collective-permute-start.31 = (bf16[8,32,512]{2,1,0:T(8,128)(2,1)S(1)}, bf16[8,32,512]{2,1,0:T(8,128)(2,1)S(1)}, u32[]{:S(2)}, u32[]{:S(2)}) collective-permute-start(bf16[8,32,512]{2,1,0:T(8,128)(2,1)S(1)} %get-tuple-element.96), channel_id=1, source_target_pairs={{0,3},{1,0},{2,1},{3,2},{4,7},{5,4},{6,5},{7,6},{8,11},{9,8},{10,9... | collective-permute-start | bytes 786440 | tf_op jit(solution)/shard_map/project/partial_over_y/ppermute | solution.py:39
  117.5 3.7 %collective-permute-done.26.refs_3_.refs_5_ = bf16[8,32,512]{2,1,0:T(8,128)(2,1)S(1)} collective-permute-done((bf16[8,32,512]{2,1,0:T(8,128)(2,1)S(1)}, bf16[8,32,512]{2,1,0:T(8,128)(2,1)S(1)}, u32[]{:S(2)}, u32[]{:S(2)}) %collective-permute-start.26) | collective-permute-done | bytes 262176 | tf_op jit(solution)/shard_map/project/partial_over_y/ppermute | solution.py:39
  121.3 1.4 collective-permute-start.27
  123.4 3.8 %collective-permute-done.30.refs_6_ = bf16[8,32,512]{2,1,0:T(8,128)(2,1)S(1)} collective-permute-done((bf16[8,32,512]{2,1,0:T(8,128)(2,1)S(1)}, bf16[8,32,512]{2,1,0:T(8,128)(2,1)S(1)}, u32[]{:S(2)}, u32[]{:S(2)}) %collective-permute-start.30) | collective-permute-done | bytes 262176 | tf_op jit(solution)/shard_map/project/partial_over_y/ppermute | solution.py:39
  127.6 2.7 %collective-permute-done.28.refs_2_.refs_9_ = bf16[1024,128]{1,0:T(8,128)(2,1)S(1)} collective-permute-done((bf16[1024,128]{1,0:T(8,128)(2,1)S(1)}, bf16[1024,128]{1,0:T(8,128)(2,1)S(1)}, u32[]{:S(2)}, u32[]{:S(2)}) %collective-permute-start.28) | collective-permute-done | bytes 262176 | tf_op jit(solution)/shard_map/partial_over_z/ppermute | solution.py:39
  130.2 7.2 %collective-permute-done.29.refs_3_.refs_10_ = bf16[1024,128]{1,0:T(8,128)(2,1)S(1)} collective-permute-done((bf16[1024,128]{1,0:T(8,128)(2,1)S(1)}, bf16[1024,128]{1,0:T(8,128)(2,1)S(1)}, u32[]{:S(2)}, u32[]{:S(2)}) %collective-permute-start.29) | collective-permute-done | bytes 262176 | tf_op jit(solution)/shard_map/partial_over_z/ppermute | solution.py:39
  137.4 1.1 partial_over_z.3
  138.5 8.6 %all-to-all-start = ((bf16[8,32,1024]{2,1,0:T(8,128)(2,1)}), bf16[8,32,1024]{2,1,0:T(8,128)(2,1)S(1)}, u32[]{:S(2)}, u32[]{:S(2)}) async-start(bf16[8,32,1024]{2,1,0:T(8,128)(2,1)} %partial_over_z.3), calls=%async_computation | async-start | bytes 1048576 | tf_op jit(solution)/shard_map/partial_over_z/all_to_all | solution.py:365
  147.1 1.8 %grad_q.1 = bf16[128,4096]{1,0:T(8,128)(2,1)} custom-call(s32[4]{0:T(128)S(1)} %pad_add_fusion.at.refs_0_, bf16[1024,128]{1,0:T(8,128)(2,1)S(1)} %get-tuple-element.61.refs_0_, bf16[1024,128]{1,0:T(8,128)(2,1)S(1)} %collective-permute-done.27.refs_1_.refs_8_, bf16[1024,128]{1,0:T(8,128)(2,1)S(1)} %collective-permute-done.28.refs_2_.refs_9_, ...), custom_call_target="tpu_custom_call" | custom-call | bytes 2097152 | tf_op jit(solution)/shard_map/grad_q/pallas_call | solution.py:47
  148.8 16.1 %all-to-all-done.part = bf16[8,32,1024]{2,1,0:T(8,128)(2,1)S(1)} async-done(((bf16[8,32,1024]{2,1,0:T(8,128)(2,1)}), bf16[8,32,1024]{2,1,0:T(8,128)(2,1)S(1)}, u32[]{:S(2)}, u32[]{:S(2)}) %all-to-all-start) | async-done | bytes 524320 | tf_op jit(solution)/shard_map/partial_over_z/all_to_all | solution.py:365
  164.9 1.3 finish.1
  (48 shorter events, 6.6 us)
Async XLA Ops:
  0.7 0.9 copy-start.3
  1.6 0.9 copy-start.4
  3.2 8.7 %collective-permute-start.1 = (bf16[128,256]{1,0:T(8,128)(2,1)S(1)}, bf16[128,256]{1,0:T(8,128)(2,1)S(1)}, u32[]{:S(2)}, u32[]{:S(2)}) collective-permute-start(bf16[128,256]{1,0:T(8,128)(2,1)S(1)} %get-tuple-element.56), channel_id=1, source_target_pairs={{0,8},{1,9},{2,10},{3,11},{4,12},{5,13},{6,14},{7,15},{8,0},{9,1},... | collective-permute-start | bytes 196616 | tf_op jit(solution)/shard_map/kv_over_x/ppermute | solution.py:39
  6.8 5.1 %collective-permute-start.2 = (bf16[128,256]{1,0:T(8,128)(2,1)S(1)}, bf16[128,256]{1,0:T(8,128)(2,1)S(1)}, u32[]{:S(2)}, u32[]{:S(2)}) collective-permute-start(bf16[128,256]{1,0:T(8,128)(2,1)S(1)} %get-tuple-element.57), channel_id=1, source_target_pairs={{0,12},{1,13},{2,14},{3,15},{4,0},{5,1},{6,2},{7,3},{8,4},{9,5},{1... | collective-permute-start | bytes 196616 | tf_op jit(solution)/shard_map/kv_over_x/ppermute | solution.py:39
  7.7 10.9 %copy-start = (bf16[128,8192]{1,0:T(8,128)(2,1)S(1)}, bf16[128,8192]{1,0:T(8,128)(2,1)}, u32[]{:S(2)}) copy-start(bf16[128,8192]{1,0:T(8,128)(2,1)} %refs_1_.3) | copy-start | bytes 6291460
  7.7 4.6 %collective-permute-start = (bf16[128,256]{1,0:T(8,128)(2,1)S(1)}, bf16[128,256]{1,0:T(8,128)(2,1)S(1)}, u32[]{:S(2)}, u32[]{:S(2)}) collective-permute-start(bf16[128,256]{1,0:T(8,128)(2,1)S(1)} %get-tuple-element.51.refs_3_), channel_id=1, source_target_pairs={{0,4},{1,5},{2,6},{3,7},{4,8},{5,9},{6,10},{7,11},{8,12},{9,13},{1... | collective-permute-start | bytes 196616 | tf_op jit(solution)/shard_map/kv_over_x/ppermute | solution.py:39
  8.3 1.3 copy-start.1
  9.5 1.2 copy-start.2
  12.4 19.9 %copy-start.5 = (s32[1,8]{1,0:T(1,128)S(1)}, s32[1,8]{1,0:T(1,128)}, u32[]{:S(2)}) copy-start(s32[1,8]{1,0:T(1,128)} %param.11) | copy-start | bytes 100
  12.4 19.9 %collective-permute-start.4 = (bf16[2,1024,128]{2,1,0:T(8,128)(2,1)S(1)}, bf16[2,1024,128]{2,1,0:T(8,128)(2,1)S(1)}, u32[]{:S(2)}, u32[]{:S(2)}) collective-permute-start(bf16[2,1024,128]{2,1,0:T(8,128)(2,1)S(1)} %get-tuple-element.59), channel_id=1, source_target_pairs={{0,12},{1,13},{2,14},{3,15},{4,0},{5,1},{6,2},{7,3},{8,4},{9,5},{1... | collective-permute-start | bytes 1572872 | tf_op jit(solution)/shard_map/q_do_over_x/ppermute | solution.py:39
  14.1 18.2 %collective-permute-start.3 = (bf16[2,1024,128]{2,1,0:T(8,128)(2,1)S(1)}, bf16[2,1024,128]{2,1,0:T(8,128)(2,1)S(1)}, u32[]{:S(2)}, u32[]{:S(2)}) collective-permute-start(bf16[2,1024,128]{2,1,0:T(8,128)(2,1)S(1)} %get-tuple-element.58.refs_5_), channel_id=1, source_target_pairs={{0,4},{1,5},{2,6},{3,7},{4,8},{5,9},{6,10},{7,11},{8,12},{9,13},{1... | collective-permute-start | bytes 1572872 | tf_op jit(solution)/shard_map/q_do_over_x/ppermute | solution.py:39
  14.7 8.8 %collective-permute-start.7 = (bf16[512,256]{1,0:T(8,128)(2,1)S(1)}, bf16[512,256]{1,0:T(8,128)(2,1)S(1)}, u32[]{:S(2)}, u32[]{:S(2)}) collective-permute-start(bf16[512,256]{1,0:T(8,128)(2,1)S(1)} %kv_over_x.3.refs_3_.refs_2_), channel_id=1, source_target_pairs={{0,3},{1,0},{2,1},{3,2},{4,7},{5,4},{6,5},{7,6},{8,11},{9,8},{10,9... | collective-permute-start | bytes 786440 | tf_op jit(solution)/shard_map/kv_over_y/ppermute | solution.py:39
  17.5 7.4 %collective-permute-start.6 = (bf16[512,256]{1,0:T(8,128)(2,1)S(1)}, bf16[512,256]{1,0:T(8,128)(2,1)S(1)}, u32[]{:S(2)}, u32[]{:S(2)}) collective-permute-start(bf16[512,256]{1,0:T(8,128)(2,1)S(1)} %kv_over_x.3.refs_3_.refs_2_), channel_id=1, source_target_pairs={{0,2},{1,3},{2,0},{3,1},{4,6},{5,7},{6,4},{7,5},{8,10},{9,11},{10,... | collective-permute-start | bytes 786440 | tf_op jit(solution)/shard_map/kv_over_y/ppermute | solution.py:39
  17.9 14.4 %collective-permute-start.5 = (bf16[512,256]{1,0:T(8,128)(2,1)S(1)}, bf16[512,256]{1,0:T(8,128)(2,1)S(1)}, u32[]{:S(2)}, u32[]{:S(2)}) collective-permute-start(bf16[512,256]{1,0:T(8,128)(2,1)S(1)} %kv_over_x.3.refs_3_.refs_2_), channel_id=1, source_target_pairs={{0,1},{1,2},{2,3},{3,0},{4,5},{5,6},{6,7},{7,4},{8,9},{9,10},{10,1... | collective-permute-start | bytes 786440 | tf_op jit(solution)/shard_map/kv_over_y/ppermute | solution.py:39
  23.6 18.7 %collective-permute-start.8 = (bf16[2,1024,128]{2,1,0:T(8,128)(2,1)S(1)}, bf16[2,1024,128]{2,1,0:T(8,128)(2,1)S(1)}, u32[]{:S(2)}, u32[]{:S(2)}) collective-permute-start(bf16[2,1024,128]{2,1,0:T(8,128)(2,1)S(1)} %get-tuple-element.63), channel_id=1, source_target_pairs={{0,8},{1,9},{2,10},{3,11},{4,12},{5,13},{6,14},{7,15},{8,0},{9,1},... | collective-permute-start | bytes 1572872 | tf_op jit(solution)/shard_map/q_do_over_x/ppermute | solution.py:39
  45.7 10.0 %collective-permute-start.12 = (bf16[512,256]{1,0:T(8,128)(2,1)S(1)}, bf16[512,256]{1,0:T(8,128)(2,1)S(1)}, u32[]{:S(2)}, u32[]{:S(2)}) collective-permute-start(bf16[512,256]{1,0:T(8,128)(2,1)S(1)} %get-tuple-element.79), channel_id=1, source_target_pairs={{0,1},{1,2},{2,3},{3,0},{4,5},{5,6},{6,7},{7,4},{8,9},{9,10},{10,1... | collective-permute-start | bytes 786440 | tf_op jit(solution)/shard_map/terms_over_y/ppermute | solution.py:39
  45.9 10.2 %collective-permute-start.9 = (bf16[2,128,1024]{2,1,0:T(8,128)(2,1)S(1)}, bf16[2,128,1024]{2,1,0:T(8,128)(2,1)S(1)}, u32[]{:S(2)}, u32[]{:S(2)}) collective-permute-start(bf16[2,128,1024]{2,1,0:T(8,128)(2,1)S(1)} %get-tuple-element.76), channel_id=1, source_target_pairs={{0,4},{1,5},{2,6},{3,7},{4,8},{5,9},{6,10},{7,11},{8,12},{9,13},{1... | collective-permute-start | bytes 1572872 | tf_op jit(solution)/shard_map/terms_over_y/ppermute | solution.py:39
  46.2 9.6 %collective-permute-start.13 = (bf16[512,256]{1,0:T(8,128)(2,1)S(1)}, bf16[512,256]{1,0:T(8,128)(2,1)S(1)}, u32[]{:S(2)}, u32[]{:S(2)}) collective-permute-start(bf16[512,256]{1,0:T(8,128)(2,1)S(1)} %get-tuple-element.80), channel_id=1, source_target_pairs={{0,2},{1,3},{2,0},{3,1},{4,6},{5,7},{6,4},{7,5},{8,10},{9,11},{10,... | collective-permute-start | bytes 786440 | tf_op jit(solution)/shard_map/terms_over_y/ppermute | solution.py:39
  49.5 6.6 %collective-permute-start.14 = (bf16[512,256]{1,0:T(8,128)(2,1)S(1)}, bf16[512,256]{1,0:T(8,128)(2,1)S(1)}, u32[]{:S(2)}, u32[]{:S(2)}) collective-permute-start(bf16[512,256]{1,0:T(8,128)(2,1)S(1)} %get-tuple-element.81), channel_id=1, source_target_pairs={{0,3},{1,0},{2,1},{3,2},{4,7},{5,4},{6,5},{7,6},{8,11},{9,8},{10,9... | collective-permute-start | bytes 786440 | tf_op jit(solution)/shard_map/terms_over_y/ppermute | solution.py:39
  51.6 14.0 %collective-permute-start.10 = (bf16[2,128,1024]{2,1,0:T(8,128)(2,1)S(1)}, bf16[2,128,1024]{2,1,0:T(8,128)(2,1)S(1)}, u32[]{:S(2)}, u32[]{:S(2)}) collective-permute-start(bf16[2,128,1024]{2,1,0:T(8,128)(2,1)S(1)} %get-tuple-element.77), channel_id=1, source_target_pairs={{0,8},{1,9},{2,10},{3,11},{4,12},{5,13},{6,14},{7,15},{8,0},{9,1},... | collective-permute-start | bytes 1572872 | tf_op jit(solution)/shard_map/terms_over_y/ppermute | solution.py:39
  55.8 12.8 %collective-permute-start.11 = (bf16[2,128,1024]{2,1,0:T(8,128)(2,1)S(1)}, bf16[2,128,1024]{2,1,0:T(8,128)(2,1)S(1)}, u32[]{:S(2)}, u32[]{:S(2)}) collective-permute-start(bf16[2,128,1024]{2,1,0:T(8,128)(2,1)S(1)} %get-tuple-element.78), channel_id=1, source_target_pairs={{0,12},{1,13},{2,14},{3,15},{4,0},{5,1},{6,2},{7,3},{8,4},{9,5},{1... | collective-permute-start | bytes 1572872 | tf_op jit(solution)/shard_map/terms_over_y/ppermute | solution.py:39
  56.2 15.0 %collective-permute-start.15 = (bf16[512,256]{1,0:T(8,128)(2,1)S(1)}, bf16[512,256]{1,0:T(8,128)(2,1)S(1)}, u32[]{:S(2)}, u32[]{:S(2)}) collective-permute-start(bf16[512,256]{1,0:T(8,128)(2,1)S(1)} %terms_over_y.3.refs_0_), channel_id=1, source_target_pairs={{0,4},{1,5},{2,6},{3,7},{4,8},{5,9},{6,10},{7,11},{8,12},{9,13},{1... | collective-permute-start | bytes 786440 | tf_op jit(solution)/shard_map/dkv_over_x/ppermute | solution.py:39
  72.4 17.2 %collective-permute-start.16 = (bf16[1024,512]{1,0:T(8,128)(2,1)S(1)}, bf16[1024,512]{1,0:T(8,128)(2,1)S(1)}, u32[]{:S(2)}, u32[]{:S(2)}) collective-permute-start(bf16[1024,512]{1,0:T(8,128)(2,1)S(1)} %get-tuple-element.83), channel_id=1, source_target_pairs={{0,16},{1,17},{2,18},{3,19},{4,20},{5,21},{6,22},{7,23},{8,24},{9,... | collective-permute-start | bytes 3145736 | tf_op jit(solution)/shard_map/turn_x/ppermute | solution.py:39
  86.5 2.7 %collective-permute-start.19 = (bf16[512,256]{1,0:T(8,128)(2,1)S(1)}, bf16[512,256]{1,0:T(8,128)(2,1)S(1)}, u32[]{:S(2)}, u32[]{:S(2)}) collective-permute-start(bf16[512,256]{1,0:T(8,128)(2,1)S(1)} %terms_over_y.3.refs_0_), channel_id=1, source_target_pairs={{0,16},{1,17},{2,18},{3,19},{4,20},{5,21},{6,22},{7,23},{8,24},{9,... | collective-permute-start | bytes 786440 | tf_op jit(solution)/shard_map/dkv_over_x/ppermute | solution.py:39
  86.7 2.9 %collective-permute-start.20 = (bf16[512,256]{1,0:T(8,128)(2,1)S(1)}, bf16[512,256]{1,0:T(8,128)(2,1)S(1)}, u32[]{:S(2)}, u32[]{:S(2)}) collective-permute-start(bf16[512,256]{1,0:T(8,128)(2,1)S(1)} %collective-permute-done.15.refs_5_.refs_1_), channel_id=1, source_target_pairs={{0,16},{1,17},{2,18},{3,19},{4,20},{5,21},{6,22},{7,23},{8,24},{9,... | collective-permute-start | bytes 786440 | tf_op jit(solution)/shard_map/dkv_over_x/ppermute | solution.py:39
  87.1 10.5 %collective-permute-start.18 = (bf16[512,256]{1,0:T(8,128)(2,1)S(1)}, bf16[512,256]{1,0:T(8,128)(2,1)S(1)}, u32[]{:S(2)}, u32[]{:S(2)}) collective-permute-start(bf16[512,256]{1,0:T(8,128)(2,1)S(1)} %terms_over_y.3.refs_0_), channel_id=1, source_target_pairs={{0,12},{1,13},{2,14},{3,15},{4,0},{5,1},{6,2},{7,3},{8,4},{9,5},{1... | collective-permute-start | bytes 786440 | tf_op jit(solution)/shard_map/dkv_over_x/ppermute | solution.py:39
  87.1 10.5 %collective-permute-start.17 = (bf16[512,256]{1,0:T(8,128)(2,1)S(1)}, bf16[512,256]{1,0:T(8,128)(2,1)S(1)}, u32[]{:S(2)}, u32[]{:S(2)}) collective-permute-start(bf16[512,256]{1,0:T(8,128)(2,1)S(1)} %terms_over_y.3.refs_0_), channel_id=1, source_target_pairs={{0,8},{1,9},{2,10},{3,11},{4,12},{5,13},{6,14},{7,15},{8,0},{9,1},... | collective-permute-start | bytes 786440 | tf_op jit(solution)/shard_map/dkv_over_x/ppermute | solution.py:39
  91.6 9.4 %collective-permute-start.21 = (bf16[8,32,512]{2,1,0:T(8,128)(2,1)S(1)}, bf16[8,32,512]{2,1,0:T(8,128)(2,1)S(1)}, u32[]{:S(2)}, u32[]{:S(2)}) collective-permute-start(bf16[8,32,512]{2,1,0:T(8,128)(2,1)S(1)} %get-tuple-element.84), channel_id=1, source_target_pairs={{0,1},{1,2},{2,3},{3,0},{4,5},{5,6},{6,7},{7,4},{8,9},{9,10},{10,1... | collective-permute-start | bytes 786440 | tf_op jit(solution)/shard_map/project/partial_over_y/ppermute | solution.py:39
  95.0 12.5 %collective-permute-start.22 = (bf16[8,32,512]{2,1,0:T(8,128)(2,1)S(1)}, bf16[8,32,512]{2,1,0:T(8,128)(2,1)S(1)}, u32[]{:S(2)}, u32[]{:S(2)}) collective-permute-start(bf16[8,32,512]{2,1,0:T(8,128)(2,1)S(1)} %get-tuple-element.85), channel_id=1, source_target_pairs={{0,2},{1,3},{2,0},{3,1},{4,6},{5,7},{6,4},{7,5},{8,10},{9,11},{10,... | collective-permute-start | bytes 786440 | tf_op jit(solution)/shard_map/project/partial_over_y/ppermute | solution.py:39
  95.9 11.7 %collective-permute-start.23 = (bf16[8,32,512]{2,1,0:T(8,128)(2,1)S(1)}, bf16[8,32,512]{2,1,0:T(8,128)(2,1)S(1)}, u32[]{:S(2)}, u32[]{:S(2)}) collective-permute-start(bf16[8,32,512]{2,1,0:T(8,128)(2,1)S(1)} %get-tuple-element.86), channel_id=1, source_target_pairs={{0,3},{1,0},{2,1},{3,2},{4,7},{5,4},{6,5},{7,6},{8,11},{9,8},{10,9... | collective-permute-start | bytes 786440 | tf_op jit(solution)/shard_map/project/partial_over_y/ppermute | solution.py:39
  107.6 2.5 %collective-permute-start.24 = (bf16[512,256]{1,0:T(8,128)(2,1)S(1)}, bf16[512,256]{1,0:T(8,128)(2,1)S(1)}, u32[]{:S(2)}, u32[]{:S(2)}) collective-permute-start(bf16[512,256]{1,0:T(8,128)(2,1)S(1)} %get-tuple-element.87), channel_id=1, source_target_pairs={{0,16},{1,17},{2,18},{3,19},{4,20},{5,21},{6,22},{7,23},{8,24},{9,... | collective-permute-start | bytes 786440 | tf_op jit(solution)/shard_map/project/ppermute | solution.py:39
  108.9 1.5 collective-permute-start.25
  112.5 8.8 %collective-permute-start.26 = (bf16[8,32,512]{2,1,0:T(8,128)(2,1)S(1)}, bf16[8,32,512]{2,1,0:T(8,128)(2,1)S(1)}, u32[]{:S(2)}, u32[]{:S(2)}) collective-permute-start(bf16[8,32,512]{2,1,0:T(8,128)(2,1)S(1)} %get-tuple-element.90), channel_id=1, source_target_pairs={{0,1},{1,2},{2,3},{3,0},{4,5},{5,6},{6,7},{7,4},{8,9},{9,10},{10,1... | collective-permute-start | bytes 786440 | tf_op jit(solution)/shard_map/project/partial_over_y/ppermute | solution.py:39
  114.3 12.9 %collective-permute-start.30 = (bf16[8,32,512]{2,1,0:T(8,128)(2,1)S(1)}, bf16[8,32,512]{2,1,0:T(8,128)(2,1)S(1)}, u32[]{:S(2)}, u32[]{:S(2)}) collective-permute-start(bf16[8,32,512]{2,1,0:T(8,128)(2,1)S(1)} %get-tuple-element.95), channel_id=1, source_target_pairs={{0,2},{1,3},{2,0},{3,1},{4,6},{5,7},{6,4},{7,5},{8,10},{9,11},{10,... | collective-permute-start | bytes 786440 | tf_op jit(solution)/shard_map/project/partial_over_y/ppermute | solution.py:39
  115.6 11.7 %collective-permute-start.31 = (bf16[8,32,512]{2,1,0:T(8,128)(2,1)S(1)}, bf16[8,32,512]{2,1,0:T(8,128)(2,1)S(1)}, u32[]{:S(2)}, u32[]{:S(2)}) collective-permute-start(bf16[8,32,512]{2,1,0:T(8,128)(2,1)S(1)} %get-tuple-element.96), channel_id=1, source_target_pairs={{0,3},{1,0},{2,1},{3,2},{4,7},{5,4},{6,5},{7,6},{8,11},{9,8},{10,9... | collective-permute-start | bytes 786440 | tf_op jit(solution)/shard_map/project/partial_over_y/ppermute | solution.py:39
  121.3 6.3 %collective-permute-start.27 = (bf16[1024,128]{1,0:T(8,128)(2,1)S(1)}, bf16[1024,128]{1,0:T(8,128)(2,1)S(1)}, u32[]{:S(2)}, u32[]{:S(2)}) collective-permute-start(bf16[1024,128]{1,0:T(8,128)(2,1)S(1)} %get-tuple-element.91), channel_id=1, source_target_pairs={{0,12},{1,13},{2,14},{3,15},{4,0},{5,1},{6,2},{7,3},{8,4},{9,5},{1... | collective-permute-start | bytes 786440 | tf_op jit(solution)/shard_map/partial_over_z/ppermute | solution.py:39
  122.7 7.5 %collective-permute-start.28 = (bf16[1024,128]{1,0:T(8,128)(2,1)S(1)}, bf16[1024,128]{1,0:T(8,128)(2,1)S(1)}, u32[]{:S(2)}, u32[]{:S(2)}) collective-permute-start(bf16[1024,128]{1,0:T(8,128)(2,1)S(1)} %get-tuple-element.92), channel_id=1, source_target_pairs={{0,8},{1,9},{2,10},{3,11},{4,12},{5,13},{6,14},{7,15},{8,0},{9,1},... | collective-permute-start | bytes 786440 | tf_op jit(solution)/shard_map/partial_over_z/ppermute | solution.py:39
  122.7 14.7 %collective-permute-start.29 = (bf16[1024,128]{1,0:T(8,128)(2,1)S(1)}, bf16[1024,128]{1,0:T(8,128)(2,1)S(1)}, u32[]{:S(2)}, u32[]{:S(2)}) collective-permute-start(bf16[1024,128]{1,0:T(8,128)(2,1)S(1)} %get-tuple-element.93), channel_id=1, source_target_pairs={{0,4},{1,5},{2,6},{3,7},{4,8},{5,9},{6,10},{7,11},{8,12},{9,13},{1... | collective-permute-start | bytes 786440 | tf_op jit(solution)/shard_map/partial_over_z/ppermute | solution.py:39
  138.5 26.4 %all-to-all-start = ((bf16[8,32,1024]{2,1,0:T(8,128)(2,1)}), bf16[8,32,1024]{2,1,0:T(8,128)(2,1)S(1)}, u32[]{:S(2)}, u32[]{:S(2)}) async-start(bf16[8,32,1024]{2,1,0:T(8,128)(2,1)} %partial_over_z.3), calls=%async_computation | async-start | bytes 1048576 | tf_op jit(solution)/shard_map/partial_over_z/all_to_all | solution.py:365

commit v6 on v2

--- a/solution.py
+++ b/solution.py
@@ -357,7 +357,7 @@
                 other += [send(piece, dc=1) for piece in after(own[2:], parts[1:])]
     with jax.named_scope("partial_over_z"):
         dq = [dq[0]] + [send(d, dx=-s - 1) for s, d in enumerate(after(dq[1:], [parts[4]]))]
-        (summed,) = call(add_kernel, [sds((NZ, 32, 1024))], parts, moved=5 << 20, smem=0, late=dq[1:])
+        (summed,) = call(add_kernel, [sds((NZ, 32, 1024))], parts, moved=5 << 20, smem=0, late=dq[1:2])
         groups = [[z * NC + c for z in range(NZ)] for c in range(NC)]
         last = lax.all_to_all(summed, "dp", 0, 0, axis_index_groups=groups, tiled=True)
     with jax.named_scope("grad_q"):

time: 154 us -> 153 us (level)
  starting transfers between devices: 60.7 us -> 58.5 us
    ppermute x32, waiting for transfers between devices: 49.6 us -> 64.8 us  [send(): return lax.ppermute(value, AXES, pairs)]
    all_to_all x1, waiting for transfers between devices: 14.6 us -> 0.01 us  [on_device(): lax.all_to_all(summed, 'dp', 0, 0, axis_index_groups=groups, tiled=True)]
    all_to_all x1, starting transfers between devices: 12.7 us -> 7.44 us  [on_device(): lax.all_to_all(summed, 'dp', 0, 0, axis_index_groups=groups, tiled=True)]
    ppermute x32, starting transfers between devices: 48 us -> 51.1 us  [send(): return lax.ppermute(value, AXES, pairs)]
where the time goes in v6:
time: 153 us
  waiting for transfers between devices  64.8 us (42%)
  starting transfers between devices  58.5 us (38%)
  Pallas kernels  24.1 us (16%)
  local copies, waits for them, and re-layouts  4.27 us (3%)
    ppermute x32, waiting for transfers between devices, send(): return lax.ppermute(value, AXES, pairs)  64.8 us
    ppermute x32, starting transfers between devices, send(): return lax.ppermute(value, AXES, pairs)  51.1 us
    pallas_call x17, Pallas kernels, call(): pl.pallas_call(body, out_shape=outs, in_specs=[SM] * smem + [VM] * (len(i...  24.1 us
    all_to_all x1, starting transfers between devices, on_device(): lax.all_to_all(summed, 'dp', 0, 0, axis_index_groups=groups, tiled=True)  7.44 us
    unnamed x12, local copies, waits for them, and re-layouts  4.27 us
  transfers between devices with their start and end apart: 33, of which 13 were waited for; matrix products, arithmetic and copies ran while one was open for 0% of the time, Pallas kernels for 11%

profile of v6, /device:TPU:1, one launch (start us, length us, event | category | flops | bytes accessed | tf_op | source)
XLA Modules:
  0.0 152.8 jit_solution(5962476858410226771)
XLA Ops:
  0.7 0.9 copy-done.3
  1.7 0.9 copy-done.4
  2.6 0.6 pack_kv.1
  3.2 2.1 %collective-permute-start = (bf16[128,256]{1,0:T(8,128)(2,1)S(1)}, bf16[128,256]{1,0:T(8,128)(2,1)S(1)}, u32[]{:S(2)}, u32[]{:S(2)}) collective-permute-start(bf16[128,256]{1,0:T(8,128)(2,1)S(1)} %get-tuple-element.54.refs_3_), channel_id=1, source_target_pairs={{0,4},{1,5},{2,6},{3,7},{4,8},{5,9},{6,10},{7,11},{8,12},{9,13},{1... | collective-permute-start | bytes 196616 | tf_op jit(solution)/shard_map/kv_over_x/ppermute | solution.py:39
  5.3 2.5 %collective-permute-start.1 = (bf16[128,256]{1,0:T(8,128)(2,1)S(1)}, bf16[128,256]{1,0:T(8,128)(2,1)S(1)}, u32[]{:S(2)}, u32[]{:S(2)}) collective-permute-start(bf16[128,256]{1,0:T(8,128)(2,1)S(1)} %get-tuple-element.59), channel_id=1, source_target_pairs={{0,8},{1,9},{2,10},{3,11},{4,12},{5,13},{6,14},{7,15},{8,0},{9,1},... | collective-permute-start | bytes 196616 | tf_op jit(solution)/shard_map/kv_over_x/ppermute | solution.py:39
  7.7 1.2 collective-permute-start.2
  8.9 1.2 copy-done.1
  10.1 1.2 copy-done.2
  11.3 1.1 pack_q_do.1
  13.0 0.6 kv_over_x.3.refs_2_
  13.5 1.4 collective-permute-start.4
  14.9 2.6 %collective-permute-start.5 = (bf16[512,256]{1,0:T(8,128)(2,1)S(1)}, bf16[512,256]{1,0:T(8,128)(2,1)S(1)}, u32[]{:S(2)}, u32[]{:S(2)}) collective-permute-start(bf16[512,256]{1,0:T(8,128)(2,1)S(1)} %kv_over_x.3.refs_2_), channel_id=1, source_target_pairs={{0,2},{1,3},{2,0},{3,1},{4,6},{5,7},{6,4},{7,5},{8,10},{9,11},{10,... | collective-permute-start | bytes 786440 | tf_op jit(solution)/shard_map/kv_over_y/ppermute | solution.py:39
  17.5 1.1 collective-permute-start.6
  18.6 1.9 %collective-permute-start.7 = (bf16[2,1024,128]{2,1,0:T(8,128)(2,1)S(1)}, bf16[2,1024,128]{2,1,0:T(8,128)(2,1)S(1)}, u32[]{:S(2)}, u32[]{:S(2)}) collective-permute-start(bf16[2,1024,128]{2,1,0:T(8,128)(2,1)S(1)} %get-tuple-element.65), channel_id=1, source_target_pairs={{0,8},{1,9},{2,10},{3,11},{4,12},{5,13},{6,14},{7,15},{8,0},{9,1},... | collective-permute-start | bytes 1572872 | tf_op jit(solution)/shard_map/q_do_over_x/ppermute | solution.py:39
  20.5 1.1 pack_x.1
  21.6 1.7 %collective-permute-start.8 = (bf16[2,1024,128]{2,1,0:T(8,128)(2,1)S(1)}, bf16[2,1024,128]{2,1,0:T(8,128)(2,1)S(1)}, u32[]{:S(2)}, u32[]{:S(2)}) collective-permute-start(bf16[2,1024,128]{2,1,0:T(8,128)(2,1)S(1)} %get-tuple-element.66), channel_id=1, source_target_pairs={{0,12},{1,13},{2,14},{3,15},{4,0},{5,1},{6,2},{7,3},{8,4},{9,5},{1... | collective-permute-start | bytes 1572872 | tf_op jit(solution)/shard_map/q_do_over_x/ppermute | solution.py:39
  23.3 4.4 %collective-permute-done.5.refs_4_ = bf16[512,256]{1,0:T(8,128)(2,1)S(1)} collective-permute-done((bf16[512,256]{1,0:T(8,128)(2,1)S(1)}, bf16[512,256]{1,0:T(8,128)(2,1)S(1)}, u32[]{:S(2)}, u32[]{:S(2)}) %collective-permute-start.5) | collective-permute-done | bytes 262176 | tf_op jit(solution)/shard_map/kv_over_y/ppermute | solution.py:39
  27.7 6.2 %attention.3 = (bf16[1024,128]{1,0:T(8,128)(2,1)S(1)}, bf16[1024,128]{1,0:T(8,128)(2,1)S(1)}, f32[2048,128]{1,0:T(8,128)S(1)}, f32[2048,128]{1,0:T(8,128)S(1)}, ...) custom-call(s32[4]{0:T(128)S(1)} %pad_add_fusion.at.refs_0_, ...), custom_call_target="tpu_custom_call" | custom-call | flops 8000000000 | bytes 6291456 | tf_op jit(solution)/shard_map/attention/pallas_call | solution.py:47
  33.9 1.2 collective-permute-done.7.refs_4_.refs_2_
  35.3 2.3 %collective-permute-start.10 = (bf16[2,128,1024]{2,1,0:T(8,128)(2,1)S(1)}, bf16[2,128,1024]{2,1,0:T(8,128)(2,1)S(1)}, u32[]{:S(2)}, u32[]{:S(2)}) collective-permute-start(bf16[2,128,1024]{2,1,0:T(8,128)(2,1)S(1)} %get-tuple-element.79), channel_id=1, source_target_pairs={{0,8},{1,9},{2,10},{3,11},{4,12},{5,13},{6,14},{7,15},{8,0},{9,1},... | collective-permute-start | bytes 1572872 | tf_op jit(solution)/shard_map/attention/ppermute | solution.py:39
  37.6 2.0 %collective-permute-start.11 = (bf16[2,128,1024]{2,1,0:T(8,128)(2,1)S(1)}, bf16[2,128,1024]{2,1,0:T(8,128)(2,1)S(1)}, u32[]{:S(2)}, u32[]{:S(2)}) collective-permute-start(bf16[2,128,1024]{2,1,0:T(8,128)(2,1)S(1)} %get-tuple-element.80), channel_id=1, source_target_pairs={{0,12},{1,13},{2,14},{3,15},{4,0},{5,1},{6,2},{7,3},{8,4},{9,5},{1... | collective-permute-start | bytes 1572872 | tf_op jit(solution)/shard_map/attention/ppermute | solution.py:39
  39.6 7.1 %collective-permute-done.8.refs_3_ = bf16[2,1024,128]{2,1,0:T(8,128)(2,1)S(1)} collective-permute-done((bf16[2,1024,128]{2,1,0:T(8,128)(2,1)S(1)}, bf16[2,1024,128]{2,1,0:T(8,128)(2,1)S(1)}, u32[]{:S(2)}, u32[]{:S(2)}) %collective-permute-start.8) | collective-permute-done | bytes 524320 | tf_op jit(solution)/shard_map/q_do_over_x/ppermute | solution.py:39
  46.7 5.0 %attention.5 = (bf16[1024,128]{1,0:T(8,128)(2,1)S(1)}, bf16[1024,128]{1,0:T(8,128)(2,1)S(1)}, bf16[512,256]{1,0:T(8,128)(2,1)S(1)}, bf16[512,256]{1,0:T(8,128)(2...) custom-call(s32[4]{0:T(128)S(1)} %pad_add_fusion.at.refs_0_, s32[8]{0:T(128)S(1)} %bitcast.6, ...), custom_call_target="tpu_custom_call" | custom-call | flops 8000000000 | bytes 6291456 | tf_op jit(solution)/shard_map/attention/pallas_call | solution.py:47
  51.7 0.5 collective-permute-start.12
  52.2 2.5 %collective-permute-start.14 = (bf16[512,256]{1,0:T(8,128)(2,1)S(1)}, bf16[512,256]{1,0:T(8,128)(2,1)S(1)}, u32[]{:S(2)}, u32[]{:S(2)}) collective-permute-start(bf16[512,256]{1,0:T(8,128)(2,1)S(1)} %get-tuple-element.86), channel_id=1, source_target_pairs={{0,3},{1,0},{2,1},{3,2},{4,7},{5,4},{6,5},{7,6},{8,11},{9,8},{10,9... | collective-permute-start | bytes 786440 | tf_op jit(solution)/shard_map/terms_over_y/ppermute | solution.py:39
  54.7 11.3 %collective-permute-done.11.refs_4_ = bf16[2,128,1024]{2,1,0:T(8,128)(2,1)S(1)} collective-permute-done((bf16[2,128,1024]{2,1,0:T(8,128)(2,1)S(1)}, bf16[2,128,1024]{2,1,0:T(8,128)(2,1)S(1)}, u32[]{:S(2)}, u32[]{:S(2)}) %collective-permute-start.11) | collective-permute-done | bytes 524320 | tf_op jit(solution)/shard_map/attention/ppermute | solution.py:39
  66.0 1.1 turn_x.1
  67.1 12.2 %collective-permute-start.15 = (bf16[1024,512]{1,0:T(8,128)(2,1)S(1)}, bf16[1024,512]{1,0:T(8,128)(2,1)S(1)}, u32[]{:S(2)}, u32[]{:S(2)}) collective-permute-start(bf16[1024,512]{1,0:T(8,128)(2,1)S(1)} %get-tuple-element.88), channel_id=1, source_target_pairs={{0,16},{1,17},{2,18},{3,19},{4,20},{5,21},{6,22},{7,23},{8,24},{9,... | collective-permute-start | bytes 3145736 | tf_op jit(solution)/shard_map/turn_x/ppermute | solution.py:39
  79.7 0.4 collective-permute-start.17
  80.1 2.2 %collective-permute-start.18 = (bf16[512,256]{1,0:T(8,128)(2,1)S(1)}, bf16[512,256]{1,0:T(8,128)(2,1)S(1)}, u32[]{:S(2)}, u32[]{:S(2)}) collective-permute-start(bf16[512,256]{1,0:T(8,128)(2,1)S(1)} %add_convert_fusion.refs_0_), channel_id=1, source_target_pairs={{0,12},{1,13},{2,14},{3,15},{4,0},{5,1},{6,2},{7,3},{8,4},{9,5},{1... | collective-permute-start | bytes 786440 | tf_op jit(solution)/shard_map/dkv_over_x/ppermute | solution.py:39
  82.4 1.3 project.3
  83.8 3.1 %collective-permute-start.22 = (bf16[8,32,256]{2,1,0:T(8,128)(2,1)S(1)}, bf16[8,32,256]{2,1,0:T(8,128)(2,1)S(1)}, u32[]{:S(2)}, u32[]{:S(2)}) collective-permute-start(bf16[8,32,256]{2,1,0:T(8,128)(2,1)S(1)} %get-tuple-element.91), channel_id=1, source_target_pairs={{0,2},{1,3},{2,0},{3,1},{4,6},{5,7},{6,4},{7,5},{8,10},{9,11},{10,... | collective-permute-start | bytes 393224 | tf_op jit(solution)/shard_map/project/partial_over_y/ppermute | solution.py:39
  86.8 7.1 %collective-permute-done.16.refs_0_ = bf16[512,256]{1,0:T(8,128)(2,1)S(1)} collective-permute-done((bf16[512,256]{1,0:T(8,128)(2,1)S(1)}, bf16[512,256]{1,0:T(8,128)(2,1)S(1)}, u32[]{:S(2)}, u32[]{:S(2)}) %collective-permute-start.16) | collective-permute-done | bytes 262176 | tf_op jit(solution)/shard_map/dkv_over_x/ppermute | solution.py:39
  94.0 1.9 %collective-permute-start.23 = (bf16[8,32,256]{2,1,0:T(8,128)(2,1)S(1)}, bf16[8,32,256]{2,1,0:T(8,128)(2,1)S(1)}, u32[]{:S(2)}, u32[]{:S(2)}) collective-permute-start(bf16[8,32,256]{2,1,0:T(8,128)(2,1)S(1)} %get-tuple-element.92), channel_id=1, source_target_pairs={{0,3},{1,0},{2,1},{3,2},{4,7},{5,4},{6,5},{7,6},{8,11},{9,8},{10,9... | collective-permute-start | bytes 393224 | tf_op jit(solution)/shard_map/project/partial_over_y/ppermute | solution.py:39
  95.8 1.5 %collective-permute-start.19 = (bf16[512,256]{1,0:T(8,128)(2,1)S(1)}, bf16[512,256]{1,0:T(8,128)(2,1)S(1)}, u32[]{:S(2)}, u32[]{:S(2)}) collective-permute-start(bf16[512,256]{1,0:T(8,128)(2,1)S(1)} %collective-permute-done.16.refs_0_), channel_id=1, source_target_pairs={{0,16},{1,17},{2,18},{3,19},{4,20},{5,21},{6,22},{7,23},{8,24},{9,... | collective-permute-start | bytes 786440 | tf_op jit(solution)/shard_map/dkv_over_x/ppermute | solution.py:39
  97.8 2.5 %collective-permute-start.24 = (bf16[512,256]{1,0:T(8,128)(2,1)S(1)}, bf16[512,256]{1,0:T(8,128)(2,1)S(1)}, u32[]{:S(2)}, u32[]{:S(2)}) collective-permute-start(bf16[512,256]{1,0:T(8,128)(2,1)S(1)} %get-tuple-element.93), channel_id=1, source_target_pairs={{0,16},{1,17},{2,18},{3,19},{4,20},{5,21},{6,22},{7,23},{8,24},{9,... | collective-permute-start | bytes 786440 | tf_op jit(solution)/shard_map/project/ppermute | solution.py:39
  100.6 0.8 collective-permute-done.24.refs_4_
  101.8 2.7 %project.5 = (bf16[8,32,768]{2,1,0:T(8,128)(2,1)S(1)}, bf16[8,32,768]{2,1,0:T(8,128)(2,1)S(1)}, bf16[8,32,768]{2,1,0:T(8,128)(2,1)S(1)}, bf16[8,32,768]{2,1,0:T(8,128)(2,1)S(1)}) custom-call(s32[4]{0:T(128)S(1)} %pad_add_fusion.at.refs_0_, bf16[1024,512]{1,0:T(8,128)(2,1)S(1)} %get-tuple-element.87.xt, ...), custom_call_target="tpu_custom_call" | custom-call | flops 1500000000 | bytes 4194304 | tf_op jit(solution)/shard_map/project/pallas_call | solution.py:47
  104.6 4.3 %collective-permute-start.30 = (bf16[8,32,768]{2,1,0:T(8,128)(2,1)S(1)}, bf16[8,32,768]{2,1,0:T(8,128)(2,1)S(1)}, u32[]{:S(2)}, u32[]{:S(2)}) collective-permute-start(bf16[8,32,768]{2,1,0:T(8,128)(2,1)S(1)} %get-tuple-element.101), channel_id=1, source_target_pairs={{0,2},{1,3},{2,0},{3,1},{4,6},{5,7},{6,4},{7,5},{8,10},{9,11},{10,... | collective-permute-start | bytes 1179656 | tf_op jit(solution)/shard_map/project/partial_over_y/ppermute | solution.py:39
  109.1 6.9 %collective-permute-done.26.refs_1_.refs_8_ = bf16[1024,128]{1,0:T(8,128)(2,1)S(1)} collective-permute-done((bf16[1024,128]{1,0:T(8,128)(2,1)S(1)}, bf16[1024,128]{1,0:T(8,128)(2,1)S(1)}, u32[]{:S(2)}, u32[]{:S(2)}) %collective-permute-start.26) | collective-permute-done | bytes 262176 | tf_op jit(solution)/shard_map/partial_over_z/ppermute | solution.py:39
  115.9 1.0 collective-permute-done.29.refs_5_
  116.9 9.3 %collective-permute-done.30.refs_6_ = bf16[8,32,768]{2,1,0:T(8,128)(2,1)S(1)} collective-permute-done((bf16[8,32,768]{2,1,0:T(8,128)(2,1)S(1)}, bf16[8,32,768]{2,1,0:T(8,128)(2,1)S(1)}, u32[]{:S(2)}, u32[]{:S(2)}) %collective-permute-start.30) | collective-permute-done | bytes 393248 | tf_op jit(solution)/shard_map/project/partial_over_y/ppermute | solution.py:39
  126.2 1.0 partial_over_z.3
  127.2 7.4 %all-to-all-start = ((bf16[8,32,1024]{2,1,0:T(8,128)(2,1)}), bf16[8,32,1024]{2,1,0:T(8,128)(2,1)S(1)}, u32[]{:S(2)}, u32[]{:S(2)}) async-start(bf16[8,32,1024]{2,1,0:T(8,128)(2,1)} %partial_over_z.3), calls=%async_computation | async-start | bytes 1048576 | tf_op jit(solution)/shard_map/partial_over_z/all_to_all | solution.py:362
  134.8 7.8 %collective-permute-done.27.refs_2_ = bf16[1024,128]{1,0:T(8,128)(2,1)S(1)} collective-permute-done((bf16[1024,128]{1,0:T(8,128)(2,1)S(1)}, bf16[1024,128]{1,0:T(8,128)(2,1)S(1)}, u32[]{:S(2)}, u32[]{:S(2)}) %collective-permute-start.27) | collective-permute-done | bytes 262176 | tf_op jit(solution)/shard_map/partial_over_z/ppermute | solution.py:39
  142.6 7.1 %collective-permute-done.28.refs_3_ = bf16[1024,128]{1,0:T(8,128)(2,1)S(1)} collective-permute-done((bf16[1024,128]{1,0:T(8,128)(2,1)S(1)}, bf16[1024,128]{1,0:T(8,128)(2,1)S(1)}, u32[]{:S(2)}, u32[]{:S(2)}) %collective-permute-start.28) | collective-permute-done | bytes 262176 | tf_op jit(solution)/shard_map/partial_over_z/ppermute | solution.py:39
  149.7 1.8 %grad_q.1 = bf16[128,4096]{1,0:T(8,128)(2,1)} custom-call(s32[4]{0:T(128)S(1)} %pad_add_fusion.at.refs_0_, bf16[1024,128]{1,0:T(8,128)(2,1)S(1)} %get-tuple-element.63.refs_3_.refs_0_, bf16[1024,128]{1,0:T(8,128)(2,1)S(1)} %collective-permute-done.26.refs_1_.refs_8_, bf16[1024,128]{1,0:T(8,128)(2,1)S(1)} %collective-permute-done.27.refs_2_, ...), custom_call_target="tpu_custom_call" | custom-call | bytes 2097152 | tf_op jit(solution)/shard_map/grad_q/pallas_call | solution.py:47
  151.5 1.3 finish.1
  (49 shorter events, 2.8 us)
Async XLA Ops:
  0.7 0.9 copy-start.3
  1.6 0.9 copy-start.4
  3.2 9.3 %collective-permute-start = (bf16[128,256]{1,0:T(8,128)(2,1)S(1)}, bf16[128,256]{1,0:T(8,128)(2,1)S(1)}, u32[]{:S(2)}, u32[]{:S(2)}) collective-permute-start(bf16[128,256]{1,0:T(8,128)(2,1)S(1)} %get-tuple-element.54.refs_3_), channel_id=1, source_target_pairs={{0,4},{1,5},{2,6},{3,7},{4,8},{5,9},{6,10},{7,11},{8,12},{9,13},{1... | collective-permute-start | bytes 196616 | tf_op jit(solution)/shard_map/kv_over_x/ppermute | solution.py:39
  5.3 7.2 %collective-permute-start.1 = (bf16[128,256]{1,0:T(8,128)(2,1)S(1)}, bf16[128,256]{1,0:T(8,128)(2,1)S(1)}, u32[]{:S(2)}, u32[]{:S(2)}) collective-permute-start(bf16[128,256]{1,0:T(8,128)(2,1)S(1)} %get-tuple-element.59), channel_id=1, source_target_pairs={{0,8},{1,9},{2,10},{3,11},{4,12},{5,13},{6,14},{7,15},{8,0},{9,1},... | collective-permute-start | bytes 196616 | tf_op jit(solution)/shard_map/kv_over_x/ppermute | solution.py:39
  7.7 12.8 %copy-start = (bf16[128,8192]{1,0:T(8,128)(2,1)S(1)}, bf16[128,8192]{1,0:T(8,128)(2,1)}, u32[]{:S(2)}) copy-start(bf16[128,8192]{1,0:T(8,128)(2,1)} %refs_1_.3) | copy-start | bytes 6291460
  7.7 4.7 %collective-permute-start.2 = (bf16[128,256]{1,0:T(8,128)(2,1)S(1)}, bf16[128,256]{1,0:T(8,128)(2,1)S(1)}, u32[]{:S(2)}, u32[]{:S(2)}) collective-permute-start(bf16[128,256]{1,0:T(8,128)(2,1)S(1)} %get-tuple-element.60), channel_id=1, source_target_pairs={{0,12},{1,13},{2,14},{3,15},{4,0},{5,1},{6,2},{7,3},{8,4},{9,5},{1... | collective-permute-start | bytes 196616 | tf_op jit(solution)/shard_map/kv_over_x/ppermute | solution.py:39
  8.9 1.2 copy-start.1
  10.1 1.2 copy-start.2
  12.6 15.1 %copy-start.5 = (s32[1,8]{1,0:T(1,128)S(1)}, s32[1,8]{1,0:T(1,128)}, u32[]{:S(2)}) copy-start(s32[1,8]{1,0:T(1,128)} %param.11) | copy-start | bytes 100
  12.6 15.1 %collective-permute-start.3 = (bf16[2,1024,128]{2,1,0:T(8,128)(2,1)S(1)}, bf16[2,1024,128]{2,1,0:T(8,128)(2,1)S(1)}, u32[]{:S(2)}, u32[]{:S(2)}) collective-permute-start(bf16[2,1024,128]{2,1,0:T(8,128)(2,1)S(1)} %get-tuple-element.61.refs_5_), channel_id=1, source_target_pairs={{0,4},{1,5},{2,6},{3,7},{4,8},{5,9},{6,10},{7,11},{8,12},{9,13},{1... | collective-permute-start | bytes 1572872 | tf_op jit(solution)/shard_map/q_do_over_x/ppermute | solution.py:39
  13.5 8.1 %collective-permute-start.4 = (bf16[512,256]{1,0:T(8,128)(2,1)S(1)}, bf16[512,256]{1,0:T(8,128)(2,1)S(1)}, u32[]{:S(2)}, u32[]{:S(2)}) collective-permute-start(bf16[512,256]{1,0:T(8,128)(2,1)S(1)} %kv_over_x.3.refs_2_), channel_id=1, source_target_pairs={{0,1},{1,2},{2,3},{3,0},{4,5},{5,6},{6,7},{7,4},{8,9},{9,10},{10,1... | collective-permute-start | bytes 786440 | tf_op jit(solution)/shard_map/kv_over_y/ppermute | solution.py:39
  14.9 12.8 %collective-permute-start.5 = (bf16[512,256]{1,0:T(8,128)(2,1)S(1)}, bf16[512,256]{1,0:T(8,128)(2,1)S(1)}, u32[]{:S(2)}, u32[]{:S(2)}) collective-permute-start(bf16[512,256]{1,0:T(8,128)(2,1)S(1)} %kv_over_x.3.refs_2_), channel_id=1, source_target_pairs={{0,2},{1,3},{2,0},{3,1},{4,6},{5,7},{6,4},{7,5},{8,10},{9,11},{10,... | collective-permute-start | bytes 786440 | tf_op jit(solution)/shard_map/kv_over_y/ppermute | solution.py:39
  17.5 10.2 %collective-permute-start.6 = (bf16[512,256]{1,0:T(8,128)(2,1)S(1)}, bf16[512,256]{1,0:T(8,128)(2,1)S(1)}, u32[]{:S(2)}, u32[]{:S(2)}) collective-permute-start(bf16[512,256]{1,0:T(8,128)(2,1)S(1)} %kv_over_x.3.refs_2_), channel_id=1, source_target_pairs={{0,3},{1,0},{2,1},{3,2},{4,7},{5,4},{6,5},{7,6},{8,11},{9,8},{10,9... | collective-permute-start | bytes 786440 | tf_op jit(solution)/shard_map/kv_over_y/ppermute | solution.py:39
  18.6 16.5 %collective-permute-start.7 = (bf16[2,1024,128]{2,1,0:T(8,128)(2,1)S(1)}, bf16[2,1024,128]{2,1,0:T(8,128)(2,1)S(1)}, u32[]{:S(2)}, u32[]{:S(2)}) collective-permute-start(bf16[2,1024,128]{2,1,0:T(8,128)(2,1)S(1)} %get-tuple-element.65), channel_id=1, source_target_pairs={{0,8},{1,9},{2,10},{3,11},{4,12},{5,13},{6,14},{7,15},{8,0},{9,1},... | collective-permute-start | bytes 1572872 | tf_op jit(solution)/shard_map/q_do_over_x/ppermute | solution.py:39
  21.6 25.0 %collective-permute-start.8 = (bf16[2,1024,128]{2,1,0:T(8,128)(2,1)S(1)}, bf16[2,1024,128]{2,1,0:T(8,128)(2,1)S(1)}, u32[]{:S(2)}, u32[]{:S(2)}) collective-permute-start(bf16[2,1024,128]{2,1,0:T(8,128)(2,1)S(1)} %get-tuple-element.66), channel_id=1, source_target_pairs={{0,12},{1,13},{2,14},{3,15},{4,0},{5,1},{6,2},{7,3},{8,4},{9,5},{1... | collective-permute-start | bytes 1572872 | tf_op jit(solution)/shard_map/q_do_over_x/ppermute | solution.py:39
  35.2 16.4 %collective-permute-start.9 = (bf16[2,128,1024]{2,1,0:T(8,128)(2,1)S(1)}, bf16[2,128,1024]{2,1,0:T(8,128)(2,1)S(1)}, u32[]{:S(2)}, u32[]{:S(2)}) collective-permute-start(bf16[2,128,1024]{2,1,0:T(8,128)(2,1)S(1)} %get-tuple-element.75.refs_9_), channel_id=1, source_target_pairs={{0,4},{1,5},{2,6},{3,7},{4,8},{5,9},{6,10},{7,11},{8,12},{9,13},{1... | collective-permute-start | bytes 1572872 | tf_op jit(solution)/shard_map/attention/ppermute | solution.py:39
  35.3 19.4 %collective-permute-start.10 = (bf16[2,128,1024]{2,1,0:T(8,128)(2,1)S(1)}, bf16[2,128,1024]{2,1,0:T(8,128)(2,1)S(1)}, u32[]{:S(2)}, u32[]{:S(2)}) collective-permute-start(bf16[2,128,1024]{2,1,0:T(8,128)(2,1)S(1)} %get-tuple-element.79), channel_id=1, source_target_pairs={{0,8},{1,9},{2,10},{3,11},{4,12},{5,13},{6,14},{7,15},{8,0},{9,1},... | collective-permute-start | bytes 1572872 | tf_op jit(solution)/shard_map/attention/ppermute | solution.py:39
  37.6 28.3 %collective-permute-start.11 = (bf16[2,128,1024]{2,1,0:T(8,128)(2,1)S(1)}, bf16[2,128,1024]{2,1,0:T(8,128)(2,1)S(1)}, u32[]{:S(2)}, u32[]{:S(2)}) collective-permute-start(bf16[2,128,1024]{2,1,0:T(8,128)(2,1)S(1)} %get-tuple-element.80), channel_id=1, source_target_pairs={{0,12},{1,13},{2,14},{3,15},{4,0},{5,1},{6,2},{7,3},{8,4},{9,5},{1... | collective-permute-start | bytes 1572872 | tf_op jit(solution)/shard_map/attention/ppermute | solution.py:39
  51.7 14.3 %collective-permute-start.12 = (bf16[512,256]{1,0:T(8,128)(2,1)S(1)}, bf16[512,256]{1,0:T(8,128)(2,1)S(1)}, u32[]{:S(2)}, u32[]{:S(2)}) collective-permute-start(bf16[512,256]{1,0:T(8,128)(2,1)S(1)} %get-tuple-element.84), channel_id=1, source_target_pairs={{0,1},{1,2},{2,3},{3,0},{4,5},{5,6},{6,7},{7,4},{8,9},{9,10},{10,1... | collective-permute-start | bytes 786440 | tf_op jit(solution)/shard_map/terms_over_y/ppermute | solution.py:39
  52.2 13.8 %collective-permute-start.13 = (bf16[512,256]{1,0:T(8,128)(2,1)S(1)}, bf16[512,256]{1,0:T(8,128)(2,1)S(1)}, u32[]{:S(2)}, u32[]{:S(2)}) collective-permute-start(bf16[512,256]{1,0:T(8,128)(2,1)S(1)} %get-tuple-element.85), channel_id=1, source_target_pairs={{0,2},{1,3},{2,0},{3,1},{4,6},{5,7},{6,4},{7,5},{8,10},{9,11},{10,... | collective-permute-start | bytes 786440 | tf_op jit(solution)/shard_map/terms_over_y/ppermute | solution.py:39
  52.2 13.8 %collective-permute-start.14 = (bf16[512,256]{1,0:T(8,128)(2,1)S(1)}, bf16[512,256]{1,0:T(8,128)(2,1)S(1)}, u32[]{:S(2)}, u32[]{:S(2)}) collective-permute-start(bf16[512,256]{1,0:T(8,128)(2,1)S(1)} %get-tuple-element.86), channel_id=1, source_target_pairs={{0,3},{1,0},{2,1},{3,2},{4,7},{5,4},{6,5},{7,6},{8,11},{9,8},{10,9... | collective-permute-start | bytes 786440 | tf_op jit(solution)/shard_map/terms_over_y/ppermute | solution.py:39
  67.1 15.2 %collective-permute-start.15 = (bf16[1024,512]{1,0:T(8,128)(2,1)S(1)}, bf16[1024,512]{1,0:T(8,128)(2,1)S(1)}, u32[]{:S(2)}, u32[]{:S(2)}) collective-permute-start(bf16[1024,512]{1,0:T(8,128)(2,1)S(1)} %get-tuple-element.88), channel_id=1, source_target_pairs={{0,16},{1,17},{2,18},{3,19},{4,20},{5,21},{6,22},{7,23},{8,24},{9,... | collective-permute-start | bytes 3145736 | tf_op jit(solution)/shard_map/turn_x/ppermute | solution.py:39
  79.5 2.9 %collective-permute-start.20 = (bf16[512,256]{1,0:T(8,128)(2,1)S(1)}, bf16[512,256]{1,0:T(8,128)(2,1)S(1)}, u32[]{:S(2)}, u32[]{:S(2)}) collective-permute-start(bf16[512,256]{1,0:T(8,128)(2,1)S(1)} %add_convert_fusion.refs_0_), channel_id=1, source_target_pairs={{0,16},{1,17},{2,18},{3,19},{4,20},{5,21},{6,22},{7,23},{8,24},{9,... | collective-permute-start | bytes 786440 | tf_op jit(solution)/shard_map/dkv_over_x/ppermute | solution.py:39
  79.6 14.4 %collective-permute-start.16 = (bf16[512,256]{1,0:T(8,128)(2,1)S(1)}, bf16[512,256]{1,0:T(8,128)(2,1)S(1)}, u32[]{:S(2)}, u32[]{:S(2)}) collective-permute-start(bf16[512,256]{1,0:T(8,128)(2,1)S(1)} %add_convert_fusion.refs_0_), channel_id=1, source_target_pairs={{0,4},{1,5},{2,6},{3,7},{4,8},{5,9},{6,10},{7,11},{8,12},{9,13},{1... | collective-permute-start | bytes 786440 | tf_op jit(solution)/shard_map/dkv_over_x/ppermute | solution.py:39
  79.7 16.2 %collective-permute-start.17 = (bf16[512,256]{1,0:T(8,128)(2,1)S(1)}, bf16[512,256]{1,0:T(8,128)(2,1)S(1)}, u32[]{:S(2)}, u32[]{:S(2)}) collective-permute-start(bf16[512,256]{1,0:T(8,128)(2,1)S(1)} %add_convert_fusion.refs_0_), channel_id=1, source_target_pairs={{0,8},{1,9},{2,10},{3,11},{4,12},{5,13},{6,14},{7,15},{8,0},{9,1},... | collective-permute-start | bytes 786440 | tf_op jit(solution)/shard_map/dkv_over_x/ppermute | solution.py:39
  80.1 17.3 %collective-permute-start.18 = (bf16[512,256]{1,0:T(8,128)(2,1)S(1)}, bf16[512,256]{1,0:T(8,128)(2,1)S(1)}, u32[]{:S(2)}, u32[]{:S(2)}) collective-permute-start(bf16[512,256]{1,0:T(8,128)(2,1)S(1)} %add_convert_fusion.refs_0_), channel_id=1, source_target_pairs={{0,12},{1,13},{2,14},{3,15},{4,0},{5,1},{6,2},{7,3},{8,4},{9,5},{1... | collective-permute-start | bytes 786440 | tf_op jit(solution)/shard_map/dkv_over_x/ppermute | solution.py:39
  83.7 13.7 %collective-permute-start.21 = (bf16[8,32,256]{2,1,0:T(8,128)(2,1)S(1)}, bf16[8,32,256]{2,1,0:T(8,128)(2,1)S(1)}, u32[]{:S(2)}, u32[]{:S(2)}) collective-permute-start(bf16[8,32,256]{2,1,0:T(8,128)(2,1)S(1)} %get-tuple-element.90), channel_id=1, source_target_pairs={{0,1},{1,2},{2,3},{3,0},{4,5},{5,6},{6,7},{7,4},{8,9},{9,10},{10,1... | collective-permute-start | bytes 393224 | tf_op jit(solution)/shard_map/project/partial_over_y/ppermute | solution.py:39
  83.8 13.6 %collective-permute-start.22 = (bf16[8,32,256]{2,1,0:T(8,128)(2,1)S(1)}, bf16[8,32,256]{2,1,0:T(8,128)(2,1)S(1)}, u32[]{:S(2)}, u32[]{:S(2)}) collective-permute-start(bf16[8,32,256]{2,1,0:T(8,128)(2,1)S(1)} %get-tuple-element.91), channel_id=1, source_target_pairs={{0,2},{1,3},{2,0},{3,1},{4,6},{5,7},{6,4},{7,5},{8,10},{9,11},{10,... | collective-permute-start | bytes 393224 | tf_op jit(solution)/shard_map/project/partial_over_y/ppermute | solution.py:39
  94.0 3.8 %collective-permute-start.23 = (bf16[8,32,256]{2,1,0:T(8,128)(2,1)S(1)}, bf16[8,32,256]{2,1,0:T(8,128)(2,1)S(1)}, u32[]{:S(2)}, u32[]{:S(2)}) collective-permute-start(bf16[8,32,256]{2,1,0:T(8,128)(2,1)S(1)} %get-tuple-element.92), channel_id=1, source_target_pairs={{0,3},{1,0},{2,1},{3,2},{4,7},{5,4},{6,5},{7,6},{8,11},{9,8},{10,9... | collective-permute-start | bytes 393224 | tf_op jit(solution)/shard_map/project/partial_over_y/ppermute | solution.py:39
  95.8 4.8 %collective-permute-start.19 = (bf16[512,256]{1,0:T(8,128)(2,1)S(1)}, bf16[512,256]{1,0:T(8,128)(2,1)S(1)}, u32[]{:S(2)}, u32[]{:S(2)}) collective-permute-start(bf16[512,256]{1,0:T(8,128)(2,1)S(1)} %collective-permute-done.16.refs_0_), channel_id=1, source_target_pairs={{0,16},{1,17},{2,18},{3,19},{4,20},{5,21},{6,22},{7,23},{8,24},{9,... | collective-permute-start | bytes 786440 | tf_op jit(solution)/shard_map/dkv_over_x/ppermute | solution.py:39
  97.8 3.6 %collective-permute-start.24 = (bf16[512,256]{1,0:T(8,128)(2,1)S(1)}, bf16[512,256]{1,0:T(8,128)(2,1)S(1)}, u32[]{:S(2)}, u32[]{:S(2)}) collective-permute-start(bf16[512,256]{1,0:T(8,128)(2,1)S(1)} %get-tuple-element.93), channel_id=1, source_target_pairs={{0,16},{1,17},{2,18},{3,19},{4,20},{5,21},{6,22},{7,23},{8,24},{9,... | collective-permute-start | bytes 786440 | tf_op jit(solution)/shard_map/project/ppermute | solution.py:39
  100.3 1.5 %collective-permute-start.25 = (bf16[512,256]{1,0:T(8,128)(2,1)S(1)}, bf16[512,256]{1,0:T(8,128)(2,1)S(1)}, u32[]{:S(2)}, u32[]{:S(2)}) collective-permute-start(bf16[512,256]{1,0:T(8,128)(2,1)S(1)} %get-tuple-element.94), channel_id=1, source_target_pairs={{0,16},{1,17},{2,18},{3,19},{4,20},{5,21},{6,22},{7,23},{8,24},{9,... | collective-permute-start | bytes 786440 | tf_op jit(solution)/shard_map/project/ppermute | solution.py:39
  104.5 12.4 %collective-permute-start.29 = (bf16[8,32,768]{2,1,0:T(8,128)(2,1)S(1)}, bf16[8,32,768]{2,1,0:T(8,128)(2,1)S(1)}, u32[]{:S(2)}, u32[]{:S(2)}) collective-permute-start(bf16[8,32,768]{2,1,0:T(8,128)(2,1)S(1)} %get-tuple-element.100), channel_id=1, source_target_pairs={{0,1},{1,2},{2,3},{3,0},{4,5},{5,6},{6,7},{7,4},{8,9},{9,10},{10,1... | collective-permute-start | bytes 1179656 | tf_op jit(solution)/shard_map/project/partial_over_y/ppermute | solution.py:39
  104.6 21.6 %collective-permute-start.30 = (bf16[8,32,768]{2,1,0:T(8,128)(2,1)S(1)}, bf16[8,32,768]{2,1,0:T(8,128)(2,1)S(1)}, u32[]{:S(2)}, u32[]{:S(2)}) collective-permute-start(bf16[8,32,768]{2,1,0:T(8,128)(2,1)S(1)} %get-tuple-element.101), channel_id=1, source_target_pairs={{0,2},{1,3},{2,0},{3,1},{4,6},{5,7},{6,4},{7,5},{8,10},{9,11},{10,... | collective-permute-start | bytes 1179656 | tf_op jit(solution)/shard_map/project/partial_over_y/ppermute | solution.py:39
  108.9 17.3 %collective-permute-start.31 = (bf16[8,32,768]{2,1,0:T(8,128)(2,1)S(1)}, bf16[8,32,768]{2,1,0:T(8,128)(2,1)S(1)}, u32[]{:S(2)}, u32[]{:S(2)}) collective-permute-start(bf16[8,32,768]{2,1,0:T(8,128)(2,1)S(1)} %get-tuple-element.102), channel_id=1, source_target_pairs={{0,3},{1,0},{2,1},{3,2},{4,7},{5,4},{6,5},{7,6},{8,11},{9,8},{10,9... | collective-permute-start | bytes 1179656 | tf_op jit(solution)/shard_map/project/partial_over_y/ppermute | solution.py:39
  109.0 7.0 %collective-permute-start.26 = (bf16[1024,128]{1,0:T(8,128)(2,1)S(1)}, bf16[1024,128]{1,0:T(8,128)(2,1)S(1)}, u32[]{:S(2)}, u32[]{:S(2)}) collective-permute-start(bf16[1024,128]{1,0:T(8,128)(2,1)S(1)} %get-tuple-element.96), channel_id=1, source_target_pairs={{0,12},{1,13},{2,14},{3,15},{4,0},{5,1},{6,2},{7,3},{8,4},{9,5},{1... | collective-permute-start | bytes 786440 | tf_op jit(solution)/shard_map/partial_over_z/ppermute | solution.py:39
  127.2 24.3 %all-to-all-start = ((bf16[8,32,1024]{2,1,0:T(8,128)(2,1)}), bf16[8,32,1024]{2,1,0:T(8,128)(2,1)S(1)}, u32[]{:S(2)}, u32[]{:S(2)}) async-start(bf16[8,32,1024]{2,1,0:T(8,128)(2,1)} %partial_over_z.3), calls=%async_computation | async-start | bytes 1048576 | tf_op jit(solution)/shard_map/partial_over_z/all_to_all | solution.py:362
  134.7 7.9 %collective-permute-start.27 = (bf16[1024,128]{1,0:T(8,128)(2,1)S(1)}, bf16[1024,128]{1,0:T(8,128)(2,1)S(1)}, u32[]{:S(2)}, u32[]{:S(2)}) collective-permute-start(bf16[1024,128]{1,0:T(8,128)(2,1)S(1)} %get-tuple-element.97), channel_id=1, source_target_pairs={{0,8},{1,9},{2,10},{3,11},{4,12},{5,13},{6,14},{7,15},{8,0},{9,1},... | collective-permute-start | bytes 786440 | tf_op jit(solution)/shard_map/partial_over_z/ppermute | solution.py:39
  134.8 14.9 %collective-permute-start.28 = (bf16[1024,128]{1,0:T(8,128)(2,1)S(1)}, bf16[1024,128]{1,0:T(8,128)(2,1)S(1)}, u32[]{:S(2)}, u32[]{:S(2)}) collective-permute-start(bf16[1024,128]{1,0:T(8,128)(2,1)S(1)} %get-tuple-element.98), channel_id=1, source_target_pairs={{0,4},{1,5},{2,6},{3,7},{4,8},{5,9},{6,10},{7,11},{8,12},{9,13},{1... | collective-permute-start | bytes 786440 | tf_op jit(solution)/shard_map/partial_over_z/ppermute | solution.py:39
